TPU v7x, 128 devices: a whole 4x4x4 slice. The times are simulated.
128 devices in a mesh: sec: 2 (over x_hi), seq: 32 (over z, y, core), dp: 2 (over x_lo).
Axes of the slice: x: 4 (x_hi: 2, x_lo: 2; x = x_hi * 2 + x_lo), y: 4, z: 4, core: 2. Of those that a mesh axis runs over, the one named last changes fastest.
Arguments:
- q_heads: bfloat16 [2, 32768, 1024], P('dp', ('sec', 'seq')), may hold values from -6 to 6
- out_grad: bfloat16 [2, 32768, 1024], P('dp', ('sec', 'seq')), may hold values from -6 to 6
- memory: bfloat16 [2, 1024, 2048], P('dp', ('sec', 'seq')), may hold values from -6 to 6
- key_weight: bfloat16 [2048, 1024], replicated, may hold values from -0.125 to 0.125
- value_weight: bfloat16 [2048, 1024], replicated, may hold values from -0.125 to 0.125
- target_modality: int32 [2, 256], P('dp', ('sec', 'seq')), may hold values from 0 to 20
- memory_modality: int32 [2, 8], P('dp'), may hold values from 0 to 20
- allow_pairs: int32 [21, 21], replicated, may hold values 0 or 1
Outputs:
- q_grad: bfloat16 [2, 32768, 1024], P('dp', ('sec', 'seq'))
- memory_grad: bfloat16 [2, 1024, 2048], P('dp', ('sec', 'seq'))
- key_weight_grad: float32 [2048, 1024], P(('sec', 'seq', 'dp'))
- value_weight_grad: float32 [2048, 1024], P(('sec', 'seq', 'dp'))
All inputs are finite; a program needn't handle non-finite values.
Results may differ from a plain program's by a relative error of at most 0.01.
Values may be sent and summed in bfloat16 or wider, within the bound.
No kernel may reach another device: no remote copies, remote signals or barrier semaphores. Data moves between devices by JAX's collectives and lax.ppermute only.
A program may use at most 128 MiB of HBM per device.

v0:
```python
import math

import jax
import jax.numpy as jnp
from jax import lax
from jax.sharding import PartitionSpec as P

HD = 64
BLOCK = 128


def head_grads(query, grad, keys, values, allowed, scale):
    scores = jnp.dot(query, keys.T, preferred_element_type=jnp.float32) * scale
    scores = jnp.where(allowed, scores, -1e30)
    top = jnp.max(scores, axis=1, keepdims=True)
    expd = jnp.where(allowed, jnp.exp(scores - top), 0.0)
    probs = expd / jnp.sum(expd, axis=1, keepdims=True)
    probs_b = probs.astype(jnp.bfloat16)
    attended = jnp.dot(probs_b, values, preferred_element_type=jnp.float32)
    delta = jnp.sum(grad.astype(jnp.float32) * attended, axis=1, keepdims=True)
    dprob = jnp.dot(grad, values.T, preferred_element_type=jnp.float32)
    score_grad = (probs * (dprob - delta)).astype(jnp.bfloat16)
    qgrad = jnp.dot(score_grad, keys, preferred_element_type=jnp.float32) * scale
    kgrad = jnp.dot(score_grad.T, query, preferred_element_type=jnp.float32) * scale
    vgrad = jnp.dot(probs_b.T, grad, preferred_element_type=jnp.float32)
    return (qgrad, kgrad, vgrad)


def body(
    q_heads,
    out_grad,
    memory,
    key_weight,
    value_weight,
    target_modality,
    memory_modality,
    allow_pairs,
):
    scale = 1.0 / math.sqrt(HD)
    width = key_weight.shape[1]
    heads = width // HD
    states = memory[0]
    keys_local = jnp.dot(states, key_weight, preferred_element_type=jnp.float32).astype(
        jnp.bfloat16
    )
    values_local = jnp.dot(states, value_weight, preferred_element_type=jnp.float32).astype(
        jnp.bfloat16
    )
    panels = lax.all_gather(
        jnp.concatenate([keys_local, values_local], axis=1), ("sec", "seq"), axis=0, tiled=True
    )
    keys = panels[:, :width]
    values = panels[:, width:]
    kinds = allow_pairs.shape[0]
    labels = jnp.arange(kinds, dtype=jnp.int32)
    q_onehot = (target_modality[0][:, None] == labels[None, :]).astype(jnp.float32)
    k_onehot = (memory_modality[0][:, None] == labels[None, :]).astype(jnp.float32)
    block_rows = jnp.dot(q_onehot, allow_pairs.astype(jnp.float32))
    block_mask = jnp.dot(block_rows, k_onehot.T) > 0.5
    first_block = jnp.arange(block_mask.shape[1], dtype=jnp.int32) == 0
    block_mask = block_mask | first_block[None, :]
    allowed = jnp.repeat(jnp.repeat(block_mask, BLOCK, axis=0), BLOCK, axis=1)
    queries = q_heads[0]
    grads = out_grad[0]

    def one_head(head):
        start = head * HD
        query = lax.dynamic_slice_in_dim(queries, start, HD, 1)
        grad = lax.dynamic_slice_in_dim(grads, start, HD, 1)
        kslice = lax.dynamic_slice_in_dim(keys, start, HD, 1)
        vslice = lax.dynamic_slice_in_dim(values, start, HD, 1)
        return head_grads(query, grad, kslice, vslice, allowed, scale)

    qgrad, kgrad, vgrad = lax.map(one_head, jnp.arange(heads, dtype=jnp.int32))
    q_rows = queries.shape[0]
    m_rows = keys.shape[0]
    qgrad = jnp.transpose(qgrad, (1, 0, 2)).reshape(q_rows, width).astype(jnp.bfloat16)
    kgrad = jnp.transpose(kgrad, (1, 0, 2)).reshape(m_rows, width)
    vgrad = jnp.transpose(vgrad, (1, 0, 2)).reshape(m_rows, width)
    summed = lax.psum_scatter(
        jnp.concatenate([kgrad, vgrad], axis=1), ("sec", "seq"), scatter_dimension=0, tiled=True
    )
    key_grad = summed[:, :width].astype(jnp.bfloat16)
    value_grad = summed[:, width:].astype(jnp.bfloat16)
    mgrad = jnp.dot(key_grad, key_weight.T, preferred_element_type=jnp.float32) + jnp.dot(
        value_grad, value_weight.T, preferred_element_type=jnp.float32
    )
    wk_part = jnp.dot(states.T, key_grad, preferred_element_type=jnp.float32)
    wv_part = jnp.dot(states.T, value_grad, preferred_element_type=jnp.float32)
    wk_total, wv_total = (
        lax.psum_scatter(wk_part, ("sec", "seq", "dp"), scatter_dimension=0, tiled=True),
        lax.psum_scatter(wv_part, ("sec", "seq", "dp"), scatter_dimension=0, tiled=True),
    )
    return (qgrad[None], mgrad.astype(jnp.bfloat16)[None], wk_total, wv_total)


def solution(mesh):
    in_specs = (
        P("dp", ("sec", "seq"), None),
        P("dp", ("sec", "seq"), None),
        P("dp", ("sec", "seq"), None),
        P(),
        P(),
        P("dp", ("sec", "seq")),
        P("dp", None),
        P(),
    )
    out_specs = (
        P("dp", ("sec", "seq"), None),
        P("dp", ("sec", "seq"), None),
        P(("sec", "seq", "dp"), None),
        P(("sec", "seq", "dp"), None),
    )
    return jax.shard_map(body, mesh=mesh, in_specs=in_specs, out_specs=out_specs, check_vma=False)
```

profile of v0, /device:TPU:1, one launch (start us, length us, event | category | flops | bytes accessed | tf_op | source)
XLA Modules:
  0.0 1963.1 jit_solution(18143767952537163938)
XLA Ops:
  8.0 3.0 convolution_convert_fusion.1
  13.8 74.7 %all-gather.2.cloned.1.call-done = bf16[1024,2048]{1,0:T(8,128)(2,1)} async-done(((bf16[16,2048]{1,0:T(8,128)(2,1)}), bf16[1024,2048]{1,0:T(8,128)(2,1)}) %all-gather.2.cloned.1.call-update) | async-done | bytes 4194320 | tf_op jit(solution)/shard_map/all_gather | solution.py:49
  88.5 4.0 fusion.53
  92.5 199.1 %while.15 = (s32[]{:T(128)}, bf16[16,512,64]{1,2,0:T(8,128)(2,1)}, f32[16,1024,64]{1,2,0:T(8,128)}, f32[16,1024,64]{1,2,0:T(8,128)}, s32[16]{0:T(128)S(1)}, /*in...) while((s32[]{:T(128)}, bf16[16,512,64]{1,2,0:T(8,128)(2,1)}, ...), condition=%wide.region_4.5_spmd.clone, body=%wide.region_0.4_spmd.clone.sunk | while | flops 412285440 | bytes 22107360 | solution.py:74
  99.9 2.1 fusion.91
  103.0 2.0 fusion.92
  112.3 2.1 fusion.91
  124.8 2.1 fusion.91
  137.3 2.1 fusion.91
  140.4 2.0 fusion.92
  149.8 2.1 fusion.91
  162.2 2.1 fusion.91
  174.6 2.1 fusion.91
  187.0 2.1 fusion.91
  199.4 2.1 fusion.91
  211.9 2.1 fusion.91
  224.3 2.1 fusion.91
  236.8 2.1 fusion.91
  249.2 2.1 fusion.91
  261.7 2.1 fusion.91
  274.1 2.1 fusion.91
  286.5 2.1 fusion.91
  291.7 8.4 pad_maximum_fusion
  300.0 9.1 copy.24
  309.2 336.7 %reduce-scatter.10.cloned.1.call-done = f32[16,2048]{1,0:T(8,128)} async-done(((f32[1024,2048]{1,0:T(8,128)}), f32[16,2048]{1,0:T(8,128)}) %reduce-scatter.10.cloned.1.call-update) | async-done | bytes 131088
  647.1 4.4 convolution_bitcast_fusion.1
  651.5 9.3 copy.28
  661.1 4.4 convolution_bitcast_fusion.2
  665.5 9.3 copy.26
  677.3 3.5 fusion.42
  682.8 626.2 %reduce-scatter.14.cloned.1.call-done = f32[16,1024]{1,0:T(8,128)} async-done(((f32[2048,1024]{1,0:T(8,128)}), f32[16,1024]{1,0:T(8,128)}) %reduce-scatter.14.cloned.1.call-update) | async-done | bytes 65552
  1309.0 647.6 %reduce-scatter.12.cloned.1.call-done = f32[16,1024]{1,0:T(8,128)} async-done(((f32[2048,1024]{1,0:T(8,128)}), f32[16,1024]{1,0:T(8,128)}) %reduce-scatter.12.cloned.1.call-update) | async-done | bytes 65552
  (179 shorter events, 159.7 us)
Async XLA Ops:
  7.2 0.8 copy-start
  7.2 81.3 %all-gather.2.cloned.1.call-start = ((), (), s32[]{:S(2)}) async-start(), calls=%async_computation.3 | async-start | bytes 4259840 | tf_op jit(solution)/shard_map/all_gather | solution.py:49
  8.0 3.4 copy-start.1
  11.5 1.4 copy-start.3
  12.1 1.3 copy-start.5
  12.1 1.3 copy-start.6
  12.1 1.3 copy-start.7
  12.8 633.1 %reduce-scatter.10.cloned.1.call-start = ((), (), s32[]{:S(2)}) async-start(), calls=%async_computation.4 | async-start | bytes 8519680
  309.1 999.8 %reduce-scatter.14.cloned.1.call-start = ((), (), s32[]{:S(2)}) async-start(), calls=%async_computation.6 | async-start | bytes 8454144
  660.8 1295.7 %reduce-scatter.12.cloned.1.call-start = ((), (), s32[]{:S(2)}) async-start(), calls=%async_computation.5 | async-start | bytes 8454144
  674.8 1.2 copy-start.4
  677.3 3.5 copy-start.2
Sparse Core Ops, SparseCore 0:
  12.9 75.5 all-gather.1
  309.3 336.6 reduce-scatter.9
  661.0 647.9 reduce-scatter.13
  1311.9 644.6 reduce-scatter.11
where the time goes:
time: 1970 us; the launch traced here: 1960 us
  waiting for transfers between devices  1690 us (86%)
  matrix products  147 us (7%)
  local copies, waits for them, and re-layouts  72.2 us (4%)
  other arithmetic  33.9 us (2%)
    unnamed x7, waiting for transfers between devices  1610 us
    all_gather x1, waiting for transfers between devices, body(): lax.all_gather(jnp.concatenate([keys_local, values_local], axis=1), ('sec...  74.7 us
  transfers between devices with their start and end apart: 4, of which 4 were waited for; matrix products, arithmetic and copies ran while one was open for 1% of the time, Pallas kernels for 0%

commit v1 on v0

v1 whole, which is shorter than its diff:
```python
import functools

import jax
import jax.numpy as jnp
from jax import lax
from jax.experimental import pallas as pl
from jax.experimental.pallas import tpu as pltpu
from jax.sharding import Mesh, PartitionSpec as P

HD = 64
BLOCK = 128
LANES = 128
SCALE = 0.125
CHUNK = 256
NT = (((1,), (1,)), ((), ()))
NN = (((1,), (0,)), ((), ()))
TN = (((0,), (0,)), ((), ()))
HEAD_AXES = ("sec", "y", "core")
SAMPLE_AXES = ("sec", "z", "y", "core")
ALL_AXES = ("sec", "z", "y", "core", "dp")
bf16 = jnp.bfloat16
f32 = jnp.float32


def dot(a, b, dims):
    return lax.dot_general(a, b, dims, preferred_element_type=f32)


def low_half():
    return lax.broadcasted_iota(jnp.int32, (1, LANES), 1) < HD


def swap_halves(a, b):
    lo = low_half()
    return jnp.where(lo, a, pltpu.roll(b, HD, 1)), jnp.where(lo, pltpu.roll(a, HD, 1), b)


def params(**kw):
    return pltpu.CompilerParams(vmem_limit_bytes=48 << 20, **kw)


def pack_kernel(q_ref, g_ref, mask_ref, out_ref):
    for k, ref in enumerate((q_ref, g_ref)):
        for t in range(2):
            a = ref[0, t * 256 : t * 256 + 128, :].astype(f32)
            b = ref[0, t * 256 + 128 : t * 256 + 256, :].astype(f32)
            even, odd = swap_halves(a, b)
            rows = slice(k * 256 + t * 128, k * 256 + t * 128 + 128)
            out_ref[0, rows, :] = even.astype(bf16)
            out_ref[1, rows, :] = odd.astype(bf16)
    out_ref[0, 512:528, :] = mask_ref[...]
    out_ref[1, 512:528, :] = mask_ref[...]


def pack_targets(q, g, mask):
    pairs = q.shape[2] // LANES
    return pl.pallas_call(
        pack_kernel,
        grid=(pairs,),
        in_specs=[
            pl.BlockSpec((1, 512, LANES), lambda p: (0, 0, p)),
            pl.BlockSpec((1, 512, LANES), lambda p: (0, 0, p)),
            pl.BlockSpec((16, LANES), lambda p: (0, 0)),
        ],
        out_specs=pl.BlockSpec((2, 528, LANES), lambda p: (p, 0, 0)),
        out_shape=jax.ShapeDtypeStruct((2 * pairs, 528, LANES), bf16),
        compiler_params=params(),
        cost_estimate=pl.CostEstimate(flops=0, bytes_accessed=5 << 20, transcendentals=0),
        name="pack_targets",
    )(q, g, mask)


def unpack_kernel(in_ref, out_ref):
    for t in range(2):
        even = in_ref[0, t * 128 : t * 128 + 128, :].astype(f32)
        odd = in_ref[1, t * 128 : t * 128 + 128, :].astype(f32)
        a, b = swap_halves(even, odd)
        out_ref[0, t * 256 : t * 256 + 128, :] = a.astype(bf16)
        out_ref[0, t * 256 + 128 : t * 256 + 256, :] = b.astype(bf16)


def unpack_targets(x):
    pairs = x.shape[0] // 2
    return pl.pallas_call(
        unpack_kernel,
        grid=(pairs,),
        in_specs=[pl.BlockSpec((2, 256, LANES), lambda p: (p, 0, 0))],
        out_specs=pl.BlockSpec((1, 512, LANES), lambda p: (0, 0, p)),
        out_shape=jax.ShapeDtypeStruct((1, 512, pairs * LANES), bf16),
        compiler_params=params(),
        cost_estimate=pl.CostEstimate(flops=0, bytes_accessed=2 << 20, transcendentals=0),
        name="unpack_targets",
    )(x)


def project_kernel(mem_ref, wk_ref, wv_ref, out_ref):
    mem = mem_ref[0]
    k = dot(mem, wk_ref[...], NN)
    v = dot(mem, wv_ref[...], NN)
    even, odd = swap_halves(k, v)
    for z in range(4):
        out_ref[0, z, 0] = even.astype(bf16)
        out_ref[0, z, 1] = odd.astype(bf16)


def project(mem, wk, wv):
    d = wk.shape[0]
    return pl.pallas_call(
        project_kernel,
        grid=(8,),
        in_specs=[
            pl.BlockSpec((1, 16, d), lambda p: (0, 0, 0)),
            pl.BlockSpec((d, LANES), lambda p: (0, p)),
            pl.BlockSpec((d, LANES), lambda p: (0, p)),
        ],
        out_specs=pl.BlockSpec((1, 4, 2, 16, LANES), lambda p: (p // 4, 0, p % 4, 0, 0)),
        out_shape=jax.ShapeDtypeStruct((2, 4, 8, 16, LANES), bf16),
        compiler_params=params(),
        cost_estimate=pl.CostEstimate(flops=0, bytes_accessed=9 << 20, transcendentals=0),
        name="project",
    )(mem, wk, wv)


def attend_kernel(mask_ref, kv_ref, r_ref, qg_ref, kvg_ref, k2_ref, v2_ref, kt_ref, ka_ref, va_ref):
    step = pl.program_id(0)
    last = pl.num_programs(0) - 1
    lo = low_half()
    left = lax.broadcasted_iota(jnp.int32, (1, 2 * LANES), 1) < LANES
    n = kv_ref.shape[0]
    per = CHUNK // BLOCK
    chunks = n // CHUNK

    @pl.when(step == 0)
    def _():
        kv = kv_ref[...].astype(f32)
        swapped = pltpu.roll(kv, HD, 1)
        k2 = jnp.where(lo, kv, swapped)
        k2_ref[...] = k2.astype(bf16)
        v2_ref[...] = jnp.where(lo, swapped, kv).astype(bf16)
        kt_ref[...] = jnp.transpose(k2)[:HD].astype(bf16)
        ka_ref[...] = jnp.zeros_like(ka_ref)
        va_ref[...] = jnp.zeros_like(va_ref)

    for t in range(2):
        q = r_ref[0, t * 128 : t * 128 + 128, :] * jnp.asarray(SCALE, bf16)
        g = r_ref[0, 256 + t * 128 : 256 + t * 128 + 128, :]
        zero = jnp.zeros_like(q)
        q2 = jnp.concatenate([jnp.where(lo, q, zero), jnp.where(lo, zero, q)], 0)
        g2 = jnp.concatenate([jnp.where(lo, g, zero), jnp.where(lo, zero, g)], 0)
        rows = [slice(c * CHUNK, c * CHUNK + CHUNK) for c in range(chunks)]
        scores = [dot(k2_ref[r, :], q2, NT) for r in rows]
        block = step * 4 + 2 * t
        hidden = []
        top = None
        for j in range(n // BLOCK):
            part = scores[j // per][(j % per) * BLOCK : (j % per + 1) * BLOCK]
            hide = jnp.where(
                left,
                jnp.where(mask_ref[block, j] > 0, 0.0, 1e30),
                jnp.where(mask_ref[block + 1, j] > 0, 0.0, 1e30),
            )
            hidden.append(hide)
            part_top = jnp.max(part, axis=0, keepdims=True) - hide
            top = part_top if top is None else jnp.maximum(top, part_top)
        expd = []
        total = None
        for c in range(chunks):
            parts = [
                jnp.exp(scores[c][i * BLOCK : (i + 1) * BLOCK] - (top + hidden[c * per + i]))
                for i in range(per)
            ]
            e = jnp.concatenate(parts, 0)
            expd.append(e)
            s = jnp.sum(e, axis=0, keepdims=True)
            total = s if total is None else total + s
        inverse = 1.0 / total
        dprobs = []
        delta = None
        for c in range(chunks):
            dp = dot(v2_ref[rows[c], :], g2, NT)
            dprobs.append(dp)
            s = jnp.sum(expd[c] * dp, axis=0, keepdims=True)
            delta = s if delta is None else delta + s
        delta = delta * inverse
        qgt = None
        for c in range(chunks):
            p = expd[c] * inverse
            ds = (p * (dprobs[c] - delta)).astype(bf16)
            va_ref[rows[c], :] += dot(p.astype(bf16), g2, NN)
            ka_ref[rows[c], :] += dot(ds, q2, NN)
            x = dot(kt_ref[:, rows[c]], ds, NN)
            qgt = x if qgt is None else qgt + x
        qgt = qgt * SCALE
        both = jnp.concatenate([qgt[:, :LANES], qgt[:, LANES:]], 0)
        qg_ref[0, t * 128 : t * 128 + 128, :] = jnp.transpose(both).astype(bf16)

    @pl.when(step == last)
    def _():
        ka = ka_ref[...]
        va = va_ref[...]
        ka = ka + pltpu.roll(ka, HD, 1)
        va = va + pltpu.roll(va, HD, 1)
        kvg_ref[...] = jnp.where(lo, ka, va).astype(bf16)


def attend(mask, kv, r):
    n = kv.shape[0]
    sources = r.shape[0]
    return pl.pallas_call(
        attend_kernel,
        grid_spec=pltpu.PrefetchScalarGridSpec(
            num_scalar_prefetch=1,
            grid=(sources,),
            in_specs=[
                pl.BlockSpec((n, LANES), lambda i, m: (0, 0)),
                pl.BlockSpec((1,) + r.shape[1:], lambda i, m: (i, 0, 0)),
            ],
            out_specs=[
                pl.BlockSpec((1, 256, LANES), lambda i, m: (i, 0, 0)),
                pl.BlockSpec((n, LANES), lambda i, m: (0, 0)),
            ],
            scratch_shapes=[
                pltpu.VMEM((n, LANES), bf16),
                pltpu.VMEM((n, LANES), bf16),
                pltpu.VMEM((HD, n), bf16),
                pltpu.VMEM((n, LANES), f32),
                pltpu.VMEM((n, LANES), f32),
            ],
        ),
        out_shape=[
            jax.ShapeDtypeStruct((sources, 256, LANES), bf16),
            jax.ShapeDtypeStruct((n, LANES), bf16),
        ],
        compiler_params=params(dimension_semantics=("arbitrary",)),
        cost_estimate=pl.CostEstimate(
            flops=45_000_000_000, bytes_accessed=4 << 20, transcendentals=0
        ),
        name="attend",
    )(mask, kv, r)


def memory_kernel(g_ref, wk_ref, wv_ref, out_ref, acc_ref):
    p = pl.program_id(0)
    kg, vg = swap_halves(g_ref[0].astype(f32), g_ref[1].astype(f32))
    part = dot(kg.astype(bf16), wk_ref[...], NT) + dot(vg.astype(bf16), wv_ref[...], NT)

    @pl.when(p == 0)
    def _():
        acc_ref[...] = part

    @pl.when(p > 0)
    def _():
        acc_ref[...] += part

    @pl.when(p == pl.num_programs(0) - 1)
    def _():
        out_ref[0] = acc_ref[...].astype(bf16)


def memory_grad(g, wk, wv):
    d = wk.shape[0]
    return pl.pallas_call(
        memory_kernel,
        grid=(8,),
        in_specs=[
            pl.BlockSpec((2, 16, LANES), lambda p: (p, 0, 0)),
            pl.BlockSpec((d, LANES), lambda p: (0, p)),
            pl.BlockSpec((d, LANES), lambda p: (0, p)),
        ],
        out_specs=pl.BlockSpec((1, 16, d), lambda p: (0, 0, 0)),
        out_shape=jax.ShapeDtypeStruct((1, 16, d), bf16),
        scratch_shapes=[pltpu.VMEM((16, d), f32)],
        compiler_params=params(dimension_semantics=("arbitrary",)),
        cost_estimate=pl.CostEstimate(flops=0, bytes_accessed=9 << 20, transcendentals=0),
        name="memory_grad",
    )(g, wk, wv)


def weight_kernel(in_ref, wk_ref, wv_ref):
    for p in range(8):
        even = in_ref[4 * p] + in_ref[4 * p + 1]
        odd = in_ref[4 * p + 2] + in_ref[4 * p + 3]
        k, v = swap_halves(even, odd)
        wk_ref[:, p * LANES : (p + 1) * LANES] = k
        wv_ref[:, p * LANES : (p + 1) * LANES] = v


def weight_grads(x):
    shape = jax.ShapeDtypeStruct((16, 8 * LANES), f32)
    return pl.pallas_call(
        weight_kernel, out_shape=[shape, shape], compiler_params=params(), name="weight_grads"
    )(x)


def exchange(x, axes):
    return lax.all_to_all(x, axes, 0, 0, tiled=True)


def body(q, g, mem, wk, wv, target_modality, memory_modality, allow_pairs):
    kinds = allow_pairs.shape[0]
    labels = jnp.arange(kinds, dtype=jnp.int32)
    q_onehot = (target_modality[0][:, None] == labels[None, :]).astype(f32)
    k_onehot = (memory_modality[0][:, None] == labels[None, :]).astype(f32)
    block_rows = jnp.dot(q_onehot, allow_pairs.astype(f32))
    block_mask = jnp.dot(block_rows, k_onehot.T) > 0.5
    first_block = jnp.arange(block_mask.shape[1], dtype=jnp.int32) == 0
    block_mask = (block_mask | first_block[None, :]).astype(bf16)
    blocks = block_mask.shape[1]
    mask_rows = jnp.pad(block_mask, ((0, 16 - block_mask.shape[0]), (0, LANES - blocks)))

    kv_blocks = project(mem, wk, wv).reshape(64, 16, LANES)
    kv = exchange(kv_blocks, SAMPLE_AXES).reshape(1024, LANES)
    targets = exchange(pack_targets(q, g, mask_rows), HEAD_AXES)
    mask = targets[:, 512:516, :blocks].reshape(64, blocks).astype(jnp.int32)

    columns = mem[0].reshape(16, 2, 4, 256).transpose(2, 0, 1, 3).reshape(1, 4, 1, 16, 512)
    columns, targets = lax.optimization_barrier((columns, targets))
    columns = jnp.broadcast_to(columns, (2, 4, 8, 16, 512)).reshape(64, 16, 512)
    columns = exchange(columns, SAMPLE_AXES).reshape(1024, 512)

    q_grad, part = attend(mask, kv, targets)
    q_grad = unpack_targets(exchange(q_grad, HEAD_AXES))

    around = [lax.ppermute(part, "z", [(i, (i + k) % 4) for i in range(4)]) for k in (1, 3, 2)]
    total = part.astype(f32)
    for x in around:
        total = total + x.astype(f32)
    total = total.astype(bf16)

    here = lax.axis_index("z")
    tokens = total.reshape(2, 4, 8, 16, LANES)
    tokens = lax.dynamic_index_in_dim(tokens, here, 1, keepdims=False).reshape(16, 16, LANES)
    m_grad = memory_grad(exchange(tokens, HEAD_AXES), wk, wv)

    w_part = dot(columns, total, TN).reshape(32, 16, LANES)
    wk_grad, wv_grad = weight_grads(exchange(w_part, ("sec", "y", "core", "dp")))
    return q_grad, m_grad, wk_grad, wv_grad


def solution(mesh):
    fine = Mesh(mesh.devices.reshape(2, 4, 4, 2, 2), ALL_AXES)
    rows = P("dp", SAMPLE_AXES, None)
    in_specs = (rows, rows, rows, P(), P(), P("dp", SAMPLE_AXES), P("dp", None), P())
    out_specs = (rows, rows, P(ALL_AXES, None), P(ALL_AXES, None))
    return jax.shard_map(body, mesh=fine, in_specs=in_specs, out_specs=out_specs, check_vma=False)
```

time: 1970 us -> 198 us (0.10)
  waiting for transfers between devices: 1690 us -> 56.6 us
  matrix products: 147 us -> 2.14 us
  local copies, waits for them, and re-layouts: 72.2 us -> 7.61 us
  Pallas kernels: 0 us -> 61.3 us
  blocking collectives: 0 us -> 36.4 us
  other arithmetic: 33.9 us -> 0.16 us
  starting transfers between devices: 0.34 us -> 31.6 us
    unnamed x7 -> x0, waiting for transfers between devices: 1610 us -> none
    dot_general x102 -> x1, matrix products: 146 us -> 1.13 us  [dot(): return lax.dot_general(a, b, dims, preferred_element_type=f32)]
    all_gather x1 -> x0, waiting for transfers between devices: 74.7 us -> none  [body(): lax.all_gather(jnp.concatenate([keys_local, values_local], axis=1), ('sec...]
    pallas_call x0 -> x6, Pallas kernels: none -> 61.3 us  [the longest x1 38.3 us: attend(): pl.pallas_call(attend_kernel, grid_spec=pltpu.PrefetchScalarGridSpec(num_...]
    all_to_all x0 -> x4, waiting for transfers between devices: none -> 46.2 us  [exchange(): return lax.all_to_all(x, axes, 0, 0, tiled=True)]
    all_to_all x0 -> x2, blocking collectives: none -> 36.4 us  [exchange(): return lax.all_to_all(x, axes, 0, 0, tiled=True)]
    all_to_all x0 -> x4, starting transfers between devices: none -> 28.9 us  [exchange(): return lax.all_to_all(x, axes, 0, 0, tiled=True)]
    unnamed x22 -> x10, local copies, waits for them, and re-layouts: 33.2 us -> 6.81 us
  transfers between devices with their start and end apart: 4 -> 7, of which waited for: 4 -> 5; matrix products, arithmetic and copies ran while one was open for 1% -> 1% of each run, Pallas kernels for 0% -> 9%
where the time goes in v1:
time: 198 us; the launch traced here: 197 us
  Pallas kernels  61.3 us (31%)
  waiting for transfers between devices  56.6 us (29%)
  blocking collectives  36.4 us (18%)
  starting transfers between devices  31.6 us (16%)
  local copies, waits for them, and re-layouts  7.61 us (4%)
  matrix products  2.14 us (1%)
    all_to_all x4, waiting for transfers between devices, exchange(): return lax.all_to_all(x, axes, 0, 0, tiled=True)  46.2 us
    pallas_call x1, Pallas kernels, attend(): pl.pallas_call(attend_kernel, grid_spec=pltpu.PrefetchScalarGridSpec(num_...  38.3 us
    all_to_all x2, blocking collectives, exchange(): return lax.all_to_all(x, axes, 0, 0, tiled=True)  36.4 us
    all_to_all x4, starting transfers between devices, exchange(): return lax.all_to_all(x, axes, 0, 0, tiled=True)  28.9 us
    ppermute x3, waiting for transfers between devices, body(): lax.ppermute(part, 'z', [(i, (i + k) % 4) for i in range(4)])  10.4 us
    pallas_call x1, Pallas kernels, memory_grad(): pl.pallas_call(memory_kernel, grid=(8,), in_specs=[pl.BlockSpec((2, 16, L...  7.83 us
    pallas_call x1, Pallas kernels, project(): pl.pallas_call(project_kernel, grid=(8,), in_specs=[pl.BlockSpec((1, 16,...  7.38 us
    unnamed x10, local copies, waits for them, and re-layouts  6.81 us
  transfers between devices with their start and end apart: 7, of which 5 were waited for; matrix products, arithmetic and copies ran while one was open for 1% of the time, Pallas kernels for 9%

profile of v1, /device:TPU:1, one launch (start us, length us, event | category | flops | bytes accessed | tf_op | source)
XLA Modules:
  0.0 196.6 jit_solution(5555428181155002425)
XLA Ops:
  0.6 1.0 fusion.6
  1.7 1.2 copy-done.2
  2.9 1.2 copy-done.3
  4.1 3.9 %pack_targets.1 = bf16[16,528,128]{2,1,0:T(8,128)(2,1)} custom-call(bf16[1,512,1024]{2,1,0:T(8,128)(2,1)S(1)} %copy-done.2, bf16[1,512,1024]{2,1,0:T(8,128)(2,1)S(1)} %copy-done.3, bf16[16,128]{1,0:T(8,128)(2,1)S(1)} %pad_convert_fusion.mask_ref), custom_call_target="tpu_custom_call" | custom-call | bytes 5242880 | tf_op jit(solution)/shard_map/pack_targets/pallas_call | solution.py:57
  8.0 8.4 %all-to-all-start = ((bf16[16,528,128]{2,1,0:T(8,128)(2,1)}), bf16[16,528,128]{2,1,0:T(8,128)(2,1)S(1)}, u32[]{:S(2)}, u32[]{:S(2)}) async-start(bf16[16,528,128]{2,1,0:T(8,128)(2,1)} %pack_targets.1), calls=%async_computation | async-start | bytes 4325376 | tf_op jit(solution)/shard_map/all_to_all | solution.py:296
  16.5 0.0 copy-start
  16.5 2.2 %copy-done = bf16[2048,1024]{1,0:T(8,128)(2,1)S(1)} copy-done((bf16[2048,1024]{1,0:T(8,128)(2,1)S(1)}, bf16[2048,1024]{1,0:T(8,128)(2,1)}, u32[]{:S(2)}) %copy-start) | copy-done | bytes 4194328
  18.7 7.4 %project.1 = bf16[2,4,8,16,128]{4,3,2,1,0:T(8,128)(2,1)} custom-call(bf16[1,16,2048]{2,1,0:T(8,128)(2,1)S(1)} %copy-done.4, bf16[2048,1024]{1,0:T(8,128)(2,1)S(1)} %copy-done, bf16[2048,1024]{1,0:T(8,128)(2,1)} %wv_ref.3), custom_call_target="tpu_custom_call" | custom-call | bytes 9437184 | tf_op jit(solution)/shard_map/project/pallas_call | solution.py:108
  26.0 19.6 %all-to-all-done.r_ref = bf16[16,528,128]{2,1,0:T(8,128)(2,1)S(1)} async-done(((bf16[16,528,128]{2,1,0:T(8,128)(2,1)}), bf16[16,528,128]{2,1,0:T(8,128)(2,1)S(1)}, u32[]{:S(2)}, u32[]{:S(2)}) %all-to-all-start) | async-done | bytes 2162720 | tf_op jit(solution)/shard_map/all_to_all | solution.py:296
  45.6 11.5 %all-to-all-start.1 = ((bf16[64,16,128]{2,1,0:T(8,128)(2,1)}), bf16[64,16,128]{2,1,0:T(8,128)(2,1)S(1)}, u32[]{:S(2)}, u32[]{:S(2)}) async-start(bf16[64,16,128]{2,1,0:T(8,128)(2,1)} %bitcast.3), calls=%async_computation.1 | async-start | bytes 524288 | tf_op jit(solution)/shard_map/all_to_all | solution.py:296
  57.2 0.1 copy.18
  57.3 11.1 %all-to-all-done.1 = bf16[64,16,128]{2,1,0:T(8,128)(2,1)S(1)} async-done(((bf16[64,16,128]{2,1,0:T(8,128)(2,1)}), bf16[64,16,128]{2,1,0:T(8,128)(2,1)S(1)}, u32[]{:S(2)}, u32[]{:S(2)}) %all-to-all-start.1) | async-done | bytes 262176 | tf_op jit(solution)/shard_map/all_to_all | solution.py:296
  68.4 38.3 %attend.1 = (bf16[16,256,128]{2,1,0:T(8,128)(2,1)}, bf16[1024,128]{1,0:T(8,128)(2,1)S(1)}) custom-call(s32[64,8]{1,0:T(8,128)S(1)} %convert.3.mask_ref, bf16[1024,128]{1,0:T(8,128)(2,1)S(1)} %bitcast.23, bf16[16,528,128]{2,1,0:T(8,128)(2,1)S(1)} %all-to-all-done.r_ref), custom_call_target="tpu_custom_call" | custom-call | flops 44999999488 | bytes 4194304 | tf_op jit(solution)/shard_map/attend/pallas_call | solution.py:209
  106.7 0.0 collective-permute-start
  106.7 2.7 %collective-permute-start.1 = (bf16[1024,128]{1,0:T(8,128)(2,1)S(1)}, bf16[1024,128]{1,0:T(8,128)(2,1)S(1)}, u32[]{:S(2)}, u32[]{:S(2)}) collective-permute-start(bf16[1024,128]{1,0:T(8,128)(2,1)S(1)} %get-tuple-element.12), channel_id=1, source_target_pairs={{0,48},{16,0},{32,16},{48,32},{1,49},{17,1},{33,17},{49,33},{2,50}... | collective-permute-start | bytes 786440 | tf_op jit(solution)/shard_map/ppermute | solution.py:324
  109.4 7.3 %collective-permute-done = bf16[1024,128]{1,0:T(8,128)(2,1)S(1)} collective-permute-done((bf16[1024,128]{1,0:T(8,128)(2,1)S(1)}, bf16[1024,128]{1,0:T(8,128)(2,1)S(1)}, u32[]{:S(2)}, u32[]{:S(2)}) %collective-permute-start) | collective-permute-done | bytes 262176 | tf_op jit(solution)/shard_map/ppermute | solution.py:324
  116.7 3.1 %collective-permute-done.2 = bf16[1024,128]{1,0:T(8,128)(2,1)S(1)} collective-permute-done((bf16[1024,128]{1,0:T(8,128)(2,1)S(1)}, bf16[1024,128]{1,0:T(8,128)(2,1)S(1)}, u32[]{:S(2)}, u32[]{:S(2)}) %collective-permute-start.2) | collective-permute-done | bytes 262176 | tf_op jit(solution)/shard_map/ppermute | solution.py:324
  119.7 0.1 add_convert_fusion
  119.9 12.3 %all_to_all.30.g_ref = bf16[16,16,128]{2,1,0:T(8,128)(2,1)S(1)} all-to-all(bf16[16,16,128]{2,1,0:T(8,128)(2,1)S(1)} %bitcast.30), channel_id=1, replica_groups=mesh['sec'=2,'z'=4,'y'=4,'core'=2,'dp'=2] {'sec','y','core'}, dimensions={0} | all-to-all | bytes 131072 | tf_op jit(solution)/shard_map/all_to_all | solution.py:296
  132.2 0.1 broadcast_in_dim.5
  132.3 24.1 %all_to_all.31 = bf16[64,16,512]{2,1,0:T(8,128)(2,1)S(1)} all-to-all(bf16[64,16,512]{2,1,0:T(8,128)(2,1)S(1)} %bitcast.26), channel_id=1, replica_groups=mesh['sec'=2,'z'=4,'y'=4,'core'=2,'dp'=2] {'sec','z','y','core'}, dimensions={0} | all-to-all | bytes 2097152 | tf_op jit(solution)/shard_map/all_to_all | solution.py:296
  156.5 4.5 %all-to-all-start.2 = ((bf16[16,256,128]{2,1,0:T(8,128)(2,1)}), bf16[16,256,128]{2,1,0:T(8,128)(2,1)S(1)}, u32[]{:S(2)}, u32[]{:S(2)}) async-start(bf16[16,256,128]{2,1,0:T(8,128)(2,1)} %get-tuple-element.11), calls=%async_computation.2 | async-start | bytes 2097152 | tf_op jit(solution)/shard_map/all_to_all | solution.py:296
  161.0 0.5 copy.15
  161.5 1.1 fusion.9
  162.7 15.5 %all-to-all-done.2.in_ref = bf16[16,256,128]{2,1,0:T(8,128)(2,1)S(1)} async-done(((bf16[16,256,128]{2,1,0:T(8,128)(2,1)}), bf16[16,256,128]{2,1,0:T(8,128)(2,1)S(1)}, u32[]{:S(2)}, u32[]{:S(2)}) %all-to-all-start.2) | async-done | bytes 1048608 | tf_op jit(solution)/shard_map/all_to_all | solution.py:296
  178.2 4.4 %all-to-all-start.5 = ((f32[32,16,128]{2,1,0:T(8,128)}), f32[32,16,128]{2,1,0:T(8,128)S(1)}, u32[]{:S(2)}, u32[]{:S(2)}) async-start(f32[32,16,128]{2,1,0:T(8,128)} %fusion.9), calls=%async_computation.5 | async-start | bytes 524288 | tf_op jit(solution)/shard_map/all_to_all | solution.py:296
  182.7 0.0 copy-start.1
  182.7 2.2 %copy-done.1 = bf16[2048,1024]{1,0:T(8,128)(2,1)S(1)} copy-done((bf16[2048,1024]{1,0:T(8,128)(2,1)S(1)}, bf16[2048,1024]{1,0:T(8,128)(2,1)}, u32[]{:S(2)}) %copy-start.1) | copy-done | bytes 4194328
  184.8 7.8 %memory_grad.1 = bf16[1,16,2048]{2,1,0:T(8,128)(2,1)} custom-call(bf16[16,16,128]{2,1,0:T(8,128)(2,1)S(1)} %all_to_all.30.g_ref, bf16[2048,1024]{1,0:T(8,128)(2,1)S(1)} %copy-done.1, bf16[2048,1024]{1,0:T(8,128)(2,1)} %wv_ref.3), custom_call_target="tpu_custom_call" | custom-call | bytes 9437184 | tf_op jit(solution)/shard_map/memory_grad/pallas_call | solution.py:262
  192.7 3.2 %unpack_targets.1 = bf16[1,512,1024]{2,1,0:T(8,128)(2,1)} custom-call(bf16[16,256,128]{2,1,0:T(8,128)(2,1)S(1)} %all-to-all-done.2.in_ref), custom_call_target="tpu_custom_call" | custom-call | bytes 2097152 | tf_op jit(solution)/shard_map/unpack_targets/pallas_call | solution.py:84
  195.8 0.0 all-to-all-done.5.in_ref
  195.8 0.8 weight_grads.1
  (13 shorter events, 0.1 us)
Async XLA Ops:
  1.7 1.2 copy-start.2
  2.9 1.2 copy-start.3
  4.1 12.3 %copy-start.4 = (bf16[1,16,2048]{2,1,0:T(8,128)(2,1)S(1)}, bf16[1,16,2048]{2,1,0:T(8,128)(2,1)}, u32[]{:S(2)}) copy-start(bf16[1,16,2048]{2,1,0:T(8,128)(2,1)} %mem_ref.1) | copy-start | bytes 196612
  8.0 37.6 %all-to-all-start = ((bf16[16,528,128]{2,1,0:T(8,128)(2,1)}), bf16[16,528,128]{2,1,0:T(8,128)(2,1)S(1)}, u32[]{:S(2)}, u32[]{:S(2)}) async-start(bf16[16,528,128]{2,1,0:T(8,128)(2,1)} %pack_targets.1), calls=%async_computation | async-start | bytes 4325376 | tf_op jit(solution)/shard_map/all_to_all | solution.py:296
  16.5 2.2 %copy-start = (bf16[2048,1024]{1,0:T(8,128)(2,1)S(1)}, bf16[2048,1024]{1,0:T(8,128)(2,1)}, u32[]{:S(2)}) copy-start(bf16[2048,1024]{1,0:T(8,128)(2,1)} %wk_ref.3) | copy-start | bytes 12582916
  45.6 22.8 %all-to-all-start.1 = ((bf16[64,16,128]{2,1,0:T(8,128)(2,1)}), bf16[64,16,128]{2,1,0:T(8,128)(2,1)S(1)}, u32[]{:S(2)}, u32[]{:S(2)}) async-start(bf16[64,16,128]{2,1,0:T(8,128)(2,1)} %bitcast.3), calls=%async_computation.1 | async-start | bytes 524288 | tf_op jit(solution)/shard_map/all_to_all | solution.py:296
  106.7 10.0 %collective-permute-start = (bf16[1024,128]{1,0:T(8,128)(2,1)S(1)}, bf16[1024,128]{1,0:T(8,128)(2,1)S(1)}, u32[]{:S(2)}, u32[]{:S(2)}) collective-permute-start(bf16[1024,128]{1,0:T(8,128)(2,1)S(1)} %get-tuple-element.12), channel_id=1, source_target_pairs={{0,16},{16,32},{32,48},{48,0},{1,17},{17,33},{33,49},{49,1},{2,18}... | collective-permute-start | bytes 786440 | tf_op jit(solution)/shard_map/ppermute | solution.py:324
  106.7 10.0 %collective-permute-start.1 = (bf16[1024,128]{1,0:T(8,128)(2,1)S(1)}, bf16[1024,128]{1,0:T(8,128)(2,1)S(1)}, u32[]{:S(2)}, u32[]{:S(2)}) collective-permute-start(bf16[1024,128]{1,0:T(8,128)(2,1)S(1)} %get-tuple-element.12), channel_id=1, source_target_pairs={{0,48},{16,0},{32,16},{48,32},{1,49},{17,1},{33,17},{49,33},{2,50}... | collective-permute-start | bytes 786440 | tf_op jit(solution)/shard_map/ppermute | solution.py:324
  109.3 10.4 %collective-permute-start.2 = (bf16[1024,128]{1,0:T(8,128)(2,1)S(1)}, bf16[1024,128]{1,0:T(8,128)(2,1)S(1)}, u32[]{:S(2)}, u32[]{:S(2)}) collective-permute-start(bf16[1024,128]{1,0:T(8,128)(2,1)S(1)} %get-tuple-element.12), channel_id=1, source_target_pairs={{0,32},{16,48},{32,0},{48,16},{1,33},{17,49},{33,1},{49,17},{2,34}... | collective-permute-start | bytes 786440 | tf_op jit(solution)/shard_map/ppermute | solution.py:324
  156.5 21.8 %all-to-all-start.2 = ((bf16[16,256,128]{2,1,0:T(8,128)(2,1)}), bf16[16,256,128]{2,1,0:T(8,128)(2,1)S(1)}, u32[]{:S(2)}, u32[]{:S(2)}) async-start(bf16[16,256,128]{2,1,0:T(8,128)(2,1)} %get-tuple-element.11), calls=%async_computation.2 | async-start | bytes 2097152 | tf_op jit(solution)/shard_map/all_to_all | solution.py:296
  178.2 17.6 %all-to-all-start.5 = ((f32[32,16,128]{2,1,0:T(8,128)}), f32[32,16,128]{2,1,0:T(8,128)S(1)}, u32[]{:S(2)}, u32[]{:S(2)}) async-start(f32[32,16,128]{2,1,0:T(8,128)} %fusion.9), calls=%async_computation.5 | async-start | bytes 524288 | tf_op jit(solution)/shard_map/all_to_all | solution.py:296
  182.7 2.2 %copy-start.1 = (bf16[2048,1024]{1,0:T(8,128)(2,1)S(1)}, bf16[2048,1024]{1,0:T(8,128)(2,1)}, u32[]{:S(2)}) copy-start(bf16[2048,1024]{1,0:T(8,128)(2,1)} %wk_ref.3) | copy-start | bytes 12582916

commit v2 on v1

v2 whole, which is shorter than its diff:
```python
import functools

import jax
import jax.numpy as jnp
from jax import lax
from jax.experimental import pallas as pl
from jax.experimental.pallas import tpu as pltpu
from jax.sharding import Mesh, PartitionSpec as P

HD = 64
BLOCK = 128
LANES = 128
SCALE = 0.125
CHUNK = 256
NT = (((1,), (1,)), ((), ()))
NN = (((1,), (0,)), ((), ()))
TN = (((0,), (0,)), ((), ()))
HEAD_AXES = ("sec", "y", "core")
SAMPLE_AXES = ("sec", "z", "y", "core")
ALL_AXES = ("sec", "z", "y", "core", "dp")
bf16 = jnp.bfloat16
f32 = jnp.float32


def dot(a, b, dims):
    return lax.dot_general(a, b, dims, preferred_element_type=f32)


def low_half():
    return lax.broadcasted_iota(jnp.int32, (1, LANES), 1) < HD


def swap_halves(a, b):
    lo = low_half()
    return jnp.where(lo, a, pltpu.roll(b, HD, 1)), jnp.where(lo, pltpu.roll(a, HD, 1), b)


def params(mib=48, **kw):
    return pltpu.CompilerParams(vmem_limit_bytes=mib << 20, **kw)


ROWS = 608


def pack_kernel(q_ref, g_ref, hide_ref, out_ref):
    for i in range(2):
        cols = slice(i * LANES, (i + 1) * LANES)
        for k, ref in enumerate((q_ref, g_ref)):
            for t in range(2):
                a = ref[0, t * 256 : t * 256 + 128, cols].astype(f32)
                b = ref[0, t * 256 + 128 : t * 256 + 256, cols].astype(f32)
                even, odd = swap_halves(a, b)
                rows = slice(k * 256 + t * 128, k * 256 + t * 128 + 128)
                out_ref[2 * i, rows, :] = even.astype(bf16)
                out_ref[2 * i + 1, rows, :] = odd.astype(bf16)
    for i in range(4):
        out_ref[i, 512:576, :] = jnp.zeros((64, LANES), bf16)
        out_ref[i, 576:608, :] = hide_ref[...]


def pack_targets(q, g, hide):
    return pl.pallas_call(
        pack_kernel,
        grid=(4,),
        in_specs=[
            pl.BlockSpec((1, 512, 256), lambda p: (0, 0, p)),
            pl.BlockSpec((1, 512, 256), lambda p: (0, 0, p)),
            pl.BlockSpec((32, LANES), lambda p: (0, 0)),
        ],
        out_specs=pl.BlockSpec((4, ROWS, LANES), lambda p: (p, 0, 0)),
        out_shape=jax.ShapeDtypeStruct((16, ROWS, LANES), bf16),
        compiler_params=params(),
        cost_estimate=pl.CostEstimate(flops=0, bytes_accessed=9 << 20, transcendentals=0),
        name="pack_targets",
    )(q, g, hide)


def project_kernel(z_ref, m0_ref, m1_ref, m2_ref, m3_ref, wk_ref, wv_ref, _, out_ref):
    mem = jnp.concatenate([m0_ref[0], m1_ref[0], m2_ref[0], m3_ref[0]], 0)
    k = dot(mem, wk_ref[...], NN)
    v = dot(mem, wv_ref[...], NN)
    for i in range(2):
        cols = slice(i * LANES, (i + 1) * LANES)
        even, odd = swap_halves(k[:, cols], v[:, cols])
        for j in range(4):
            at = pl.multiple_of(lax.rem(z_ref[0] + 4 - j, 4) * 16, 16)
            out_ref[2 * i, pl.ds(at, 16), :] = even[j * 16 : j * 16 + 16].astype(bf16)
            out_ref[2 * i + 1, pl.ds(at, 16), :] = odd[j * 16 : j * 16 + 16].astype(bf16)


def project(z, mems, wk, wv, payload):
    d = wk.shape[0]
    mem_spec = pl.BlockSpec((1, 16, d), lambda p, z: (0, 0, 0))
    w_spec = pl.BlockSpec((d, 256), lambda p, z: (0, p))
    return pl.pallas_call(
        project_kernel,
        grid_spec=pltpu.PrefetchScalarGridSpec(
            num_scalar_prefetch=1,
            grid=(4,),
            in_specs=[mem_spec] * 4 + [w_spec] * 2 + [pl.BlockSpec(memory_space=pl.ANY)],
            out_specs=pl.BlockSpec((4, 64, LANES), lambda p, z: (p, 8, 0)),
        ),
        out_shape=jax.ShapeDtypeStruct(payload.shape, bf16),
        input_output_aliases={7: 0},
        compiler_params=params(),
        cost_estimate=pl.CostEstimate(flops=0, bytes_accessed=12 << 20, transcendentals=0),
        name="project",
    )(z, *mems, wk, wv, payload)


def unpack_kernel(in_ref, out_ref):
    for i in range(2):
        for t in range(2):
            even = in_ref[2 * i, t * 128 : t * 128 + 128, :].astype(f32)
            odd = in_ref[2 * i + 1, t * 128 : t * 128 + 128, :].astype(f32)
            a, b = swap_halves(even, odd)
            cols = slice(i * LANES, (i + 1) * LANES)
            out_ref[0, t * 256 : t * 256 + 128, cols] = a.astype(bf16)
            out_ref[0, t * 256 + 128 : t * 256 + 256, cols] = b.astype(bf16)


def unpack_targets(x):
    return pl.pallas_call(
        unpack_kernel,
        grid=(4,),
        in_specs=[pl.BlockSpec((4, 256, LANES), lambda p: (p, 0, 0))],
        out_specs=pl.BlockSpec((1, 512, 256), lambda p: (0, 0, p)),
        out_shape=jax.ShapeDtypeStruct((1, 512, 1024), bf16),
        compiler_params=params(),
        cost_estimate=pl.CostEstimate(flops=0, bytes_accessed=6 << 20, transcendentals=0),
        name="unpack_targets",
    )(x)


def attend_kernel(kv_ref, r_ref, qg_ref, kvg_ref, k2_ref, v2_ref, kt_ref, ka_ref, va_ref):
    step = pl.program_id(0)
    last = pl.num_programs(0) - 1
    lo = low_half()
    n = k2_ref.shape[0]
    per = CHUNK // BLOCK
    chunks = n // CHUNK

    @pl.when(step == 0)
    def _():
        order = [(c, z) for c in (0, 8) for z in range(4)]
        kv = jnp.concatenate(
            [kv_ref[c + i, z * 16 : z * 16 + 16, :] for c, z in order for i in range(8)], 0
        ).astype(f32)
        swapped = pltpu.roll(kv, HD, 1)
        k2 = jnp.where(lo, kv, swapped)
        k2_ref[...] = k2.astype(bf16)
        v2_ref[...] = jnp.where(lo, swapped, kv).astype(bf16)
        kt_ref[...] = jnp.transpose(k2)[:HD].astype(bf16)
        ka_ref[...] = jnp.zeros_like(ka_ref)
        va_ref[...] = jnp.zeros_like(va_ref)

    for t in range(2):
        q = r_ref[0, t * 128 : t * 128 + 128, :] * jnp.asarray(SCALE, bf16)
        g = r_ref[0, 256 + t * 128 : 256 + t * 128 + 128, :]
        zero = jnp.zeros_like(q)
        q2 = jnp.concatenate([jnp.where(lo, q, zero), jnp.where(lo, zero, q)], 0)
        g2 = jnp.concatenate([jnp.where(lo, g, zero), jnp.where(lo, zero, g)], 0)
        rows = [slice(c * CHUNK, c * CHUNK + CHUNK) for c in range(chunks)]
        scores = [dot(k2_ref[r, :], q2, NT) for r in rows]
        away = r_ref[0, 576 + t * 16 : 576 + t * 16 + 16, :].astype(f32)
        hidden = []
        top = None
        for j in range(n // BLOCK):
            part = scores[j // per][(j % per) * BLOCK : (j % per + 1) * BLOCK]
            hide = jnp.concatenate([away[j : j + 1], away[8 + j : 9 + j]], 1)
            hidden.append(hide)
            part_top = jnp.max(part, axis=0, keepdims=True) - hide
            top = part_top if top is None else jnp.maximum(top, part_top)
        expd = []
        total = None
        for c in range(chunks):
            parts = [
                jnp.exp(scores[c][i * BLOCK : (i + 1) * BLOCK] - (top + hidden[c * per + i]))
                for i in range(per)
            ]
            e = jnp.concatenate(parts, 0)
            expd.append(e)
            s = jnp.sum(e, axis=0, keepdims=True)
            total = s if total is None else total + s
        inverse = 1.0 / total
        dprobs = []
        delta = None
        for c in range(chunks):
            dp = dot(v2_ref[rows[c], :], g2, NT)
            dprobs.append(dp)
            s = jnp.sum(expd[c] * dp, axis=0, keepdims=True)
            delta = s if delta is None else delta + s
        delta = delta * inverse
        qgt = None
        for c in range(chunks):
            p = expd[c] * inverse
            ds = (p * (dprobs[c] - delta)).astype(bf16)
            va_ref[rows[c], :] += dot(p.astype(bf16), g2, NN)
            ka_ref[rows[c], :] += dot(ds, q2, NN)
            x = dot(kt_ref[:, rows[c]], ds, NN)
            qgt = x if qgt is None else qgt + x
        qgt = qgt * SCALE
        both = jnp.concatenate([qgt[:, :LANES], qgt[:, LANES:]], 0)
        qg_ref[0, t * 128 : t * 128 + 128, :] = jnp.transpose(both).astype(bf16)

    @pl.when(step == last)
    def _():
        ka = ka_ref[...]
        va = va_ref[...]
        ka = ka + pltpu.roll(ka, HD, 1)
        va = va + pltpu.roll(va, HD, 1)
        kvg_ref[...] = jnp.where(lo, ka, va).astype(bf16)


def attend(r):
    sources = r.shape[0]
    n = 64 * sources
    return pl.pallas_call(
        attend_kernel,
        grid=(sources,),
        in_specs=[
            pl.BlockSpec((sources, 64, LANES), lambda i: (0, 8, 0)),
            pl.BlockSpec((1, ROWS, LANES), lambda i: (i, 0, 0)),
        ],
        out_specs=[
            pl.BlockSpec((1, 256, LANES), lambda i: (i, 0, 0)),
            pl.BlockSpec((n, LANES), lambda i: (0, 0)),
        ],
        scratch_shapes=[
            pltpu.VMEM((n, LANES), bf16),
            pltpu.VMEM((n, LANES), bf16),
            pltpu.VMEM((HD, n), bf16),
            pltpu.VMEM((n, LANES), f32),
            pltpu.VMEM((n, LANES), f32),
        ],
        out_shape=[
            jax.ShapeDtypeStruct((sources, 256, LANES), bf16),
            jax.ShapeDtypeStruct((n, LANES), bf16),
        ],
        compiler_params=params(dimension_semantics=("arbitrary",)),
        cost_estimate=pl.CostEstimate(
            flops=45_000_000_000, bytes_accessed=4 << 20, transcendentals=0
        ),
        name="attend",
    )(r, r)


def weight_kernel(z_ref, p0_ref, p1_ref, p2_ref, p3_ref, mem_ref, out_ref, total_ref):
    step = pl.program_id(0)

    @pl.when(step == 0)
    def _():
        total = p0_ref[...].astype(f32) + p1_ref[...].astype(f32)
        total = total + (p2_ref[...].astype(f32) + p3_ref[...].astype(f32))
        total_ref[...] = total.astype(bf16)

    grad = dot(mem_ref[...], total_ref[...], TN).astype(bf16)
    at = pl.multiple_of(step * 512 + z_ref[0] * 128, 128)
    tokens = total_ref[pl.ds(at, 128), :]
    for i in range(16):
        out_ref[i, 0:16, :] = grad[i * 16 : i * 16 + 16]
        out_ref[i, 16:32, :] = tokens[(i // 2) * 16 : (i // 2) * 16 + 16]


def weight_blocks(z, parts, mem):
    n = mem.shape[0]
    part_spec = pl.BlockSpec((n, LANES), lambda s, z: (0, 0))
    return pl.pallas_call(
        weight_kernel,
        grid_spec=pltpu.PrefetchScalarGridSpec(
            num_scalar_prefetch=1,
            grid=(2,),
            in_specs=[part_spec] * 4 + [pl.BlockSpec((n, 256), lambda s, z: (0, s * 4 + z[0]))],
            out_specs=pl.BlockSpec((16, 32, LANES), lambda s, z: (s, 0, 0)),
            scratch_shapes=[pltpu.VMEM((n, LANES), bf16)],
        ),
        out_shape=jax.ShapeDtypeStruct((32, 32, LANES), bf16),
        compiler_params=params(60, dimension_semantics=("arbitrary",)),
        cost_estimate=pl.CostEstimate(flops=0, bytes_accessed=6 << 20, transcendentals=0),
        name="weight_blocks",
    )(z, *parts, mem)


def finish_kernel(dp_ref, in_ref, wk_ref, wv_ref, mg_ref, wkg_ref, wvg_ref, acc_ref):
    p = pl.program_id(0)
    grads = []
    for i in range(2):
        cols = slice(i * LANES, (i + 1) * LANES)
        rows = [in_ref[4 * i + j, 0:16, :].astype(f32) for j in range(4)]
        wkg_ref[:, cols], wvg_ref[:, cols] = swap_halves(rows[0] + rows[1], rows[2] + rows[3])
        even = in_ref[pl.ds(4 * i + dp_ref[0], 1), 16:32, :][0].astype(f32)
        odd = in_ref[pl.ds(4 * i + 2 + dp_ref[0], 1), 16:32, :][0].astype(f32)
        grads.append(swap_halves(even, odd))
    kg = jnp.concatenate([grads[0][0], grads[1][0]], 1).astype(bf16)
    vg = jnp.concatenate([grads[0][1], grads[1][1]], 1).astype(bf16)
    part = dot(kg, wk_ref[...], NT) + dot(vg, wv_ref[...], NT)

    @pl.when(p == 0)
    def _():
        acc_ref[...] = part

    @pl.when(p > 0)
    def _():
        acc_ref[...] += part

    @pl.when(p == pl.num_programs(0) - 1)
    def _():
        mg_ref[0] = acc_ref[...].astype(bf16)


def finish(dp, x, wk, wv):
    d = wk.shape[0]
    w_spec = pl.BlockSpec((d, 256), lambda p, dp: (0, p))
    out_spec = pl.BlockSpec((16, 256), lambda p, dp: (0, p))
    shape = jax.ShapeDtypeStruct((16, wk.shape[1]), f32)
    return pl.pallas_call(
        finish_kernel,
        grid_spec=pltpu.PrefetchScalarGridSpec(
            num_scalar_prefetch=1,
            grid=(4,),
            in_specs=[pl.BlockSpec((8, 32, LANES), lambda p, dp: (p, 0, 0)), w_spec, w_spec],
            out_specs=[pl.BlockSpec((1, 16, d), lambda p, dp: (0, 0, 0)), out_spec, out_spec],
            scratch_shapes=[pltpu.VMEM((16, d), f32)],
        ),
        out_shape=[jax.ShapeDtypeStruct((1, 16, d), bf16), shape, shape],
        compiler_params=params(dimension_semantics=("arbitrary",)),
        cost_estimate=pl.CostEstimate(flops=0, bytes_accessed=12 << 20, transcendentals=0),
        name="finish",
    )(dp, x, wk, wv)


def exchange(x, axes):
    return lax.all_to_all(x, axes, 0, 0, tiled=True)


def shifted(x, axis, k):
    n = lax.axis_size(axis)
    return lax.ppermute(x, axis, [(i, (i + k) % n) for i in range(n)])


def body(q, g, mem, wk, wv, target_modality, memory_modality, allow_pairs):
    z = lax.axis_index("z").reshape(1)
    dp = lax.axis_index("dp").reshape(1)
    mems = [mem] + [shifted(mem, "z", k) for k in (1, 2, 3)]

    labels = jnp.arange(allow_pairs.shape[0], dtype=jnp.int32)
    q_onehot = (target_modality[0][:, None] == labels[None, :]).astype(f32)
    k_onehot = (memory_modality[0][:, None] == labels[None, :]).astype(f32)
    allowed = jnp.dot(jnp.dot(q_onehot, allow_pairs.astype(f32)), k_onehot.T) > 0.5
    allowed = allowed | (jnp.arange(allowed.shape[1], dtype=jnp.int32) == 0)[None, :]
    hide = jnp.where(allowed, 0.0, 1e30).astype(bf16).reshape(32, 1)
    hide = jnp.broadcast_to(hide, (32, LANES))

    payload = project(z, mems, wk, wv, pack_targets(q, g, hide))
    targets = exchange(payload, HEAD_AXES)
    memory = lax.all_gather(mem[0], SAMPLE_AXES, axis=0, tiled=True)

    q_grad, part = attend(targets)
    q_grad = exchange(q_grad, HEAD_AXES)
    parts = [part] + [shifted(part, "z", k) for k in (1, 3, 2)]
    blocks = weight_blocks(z, parts, memory)
    blocks, q_grad = lax.optimization_barrier((blocks, q_grad))
    blocks = exchange(blocks, ("sec", "y", "core", "dp"))
    m_grad, wk_grad, wv_grad = finish(dp, blocks, wk, wv)
    return unpack_targets(q_grad), m_grad, wk_grad, wv_grad


def solution(mesh):
    fine = Mesh(mesh.devices.reshape(2, 4, 4, 2, 2), ALL_AXES)
    rows = P("dp", SAMPLE_AXES, None)
    in_specs = (rows, rows, rows, P(), P(), P("dp", SAMPLE_AXES), P("dp", None), P())
    out_specs = (rows, rows, P(ALL_AXES, None), P(ALL_AXES, None))
    return jax.shard_map(body, mesh=fine, in_specs=in_specs, out_specs=out_specs, check_vma=False)
```

time: 198 us -> 159 us (0.80)
  waiting for transfers between devices: 56.6 us -> 19.2 us
  between operations: 0.76 us -> 14.1 us
  starting transfers between devices: 31.6 us -> 22.1 us
  Pallas kernels: 61.3 us -> 54.2 us
  blocking collectives: 36.4 us -> 42.5 us
    all_to_all x4 -> x2, waiting for transfers between devices: 46.2 us -> 6.75 us  [exchange(): return lax.all_to_all(x, axes, 0, 0, tiled=True)]
    all_to_all x4 -> x2, starting transfers between devices: 28.9 us -> 12.8 us  [exchange(): return lax.all_to_all(x, axes, 0, 0, tiled=True)]
    pallas_call x6, Pallas kernels: 61.3 us -> 54.2 us  [the longest x1 37.3 us: attend(): pl.pallas_call(attend_kernel, grid=(sources,), in_specs=[pl.BlockSpec((so...]
    ppermute x3 -> x6, starting transfers between devices: 2.68 us -> 9.25 us  [shifted(): return lax.ppermute(x, axis, [(i, (i + k) % n) for i in range(n)])]
    all_to_all x2 -> x1, blocking collectives: 36.4 us -> 42.5 us  [exchange(): return lax.all_to_all(x, axes, 0, 0, tiled=True)]
    ppermute x3 -> x6, waiting for transfers between devices: 10.4 us -> 11.8 us  [shifted(): return lax.ppermute(x, axis, [(i, (i + k) % n) for i in range(n)])]
    unnamed x10 -> x16, local copies, waits for them, and re-layouts: 6.81 us -> 5.49 us
  transfers between devices with their start and end apart: 7 -> 9, of which waited for: 5 -> 2; matrix products, arithmetic and copies ran while one was open for 1% -> 1% of each run, Pallas kernels for 9% -> 31%
where the time goes in v2:
time: 159 us
  Pallas kernels  54.2 us (34%)
  blocking collectives  42.5 us (27%)
  starting transfers between devices  22.1 us (14%)
  waiting for transfers between devices  19.2 us (12%)
  between operations  14.1 us (9%)
  local copies, waits for them, and re-layouts  5.65 us (4%)
    all_to_all x1, blocking collectives, exchange(): return lax.all_to_all(x, axes, 0, 0, tiled=True)  42.5 us
    pallas_call x1, Pallas kernels, attend(): pl.pallas_call(attend_kernel, grid=(sources,), in_specs=[pl.BlockSpec((so...  37.3 us
    all_to_all x2, starting transfers between devices, exchange(): return lax.all_to_all(x, axes, 0, 0, tiled=True)  12.8 us
    ppermute x6, waiting for transfers between devices, shifted(): return lax.ppermute(x, axis, [(i, (i + k) % n) for i in range(n)])  11.8 us
    ppermute x6, starting transfers between devices, shifted(): return lax.ppermute(x, axis, [(i, (i + k) % n) for i in range(n)])  9.25 us
    all_to_all x2, waiting for transfers between devices, exchange(): return lax.all_to_all(x, axes, 0, 0, tiled=True)  6.75 us
    pallas_call x1, Pallas kernels, finish(): pl.pallas_call(finish_kernel, grid_spec=pltpu.PrefetchScalarGridSpec(num_...  5.64 us
    unnamed x16, local copies, waits for them, and re-layouts  5.49 us
  transfers between devices with their start and end apart: 9, of which 2 were waited for; matrix products, arithmetic and copies ran while one was open for 1% of the time, Pallas kernels for 31%

profile of v2, /device:TPU:1, one launch (start us, length us, event | category | flops | bytes accessed | tf_op | source)
XLA Modules:
  0.0 158.8 jit_solution(17189566519875964901)
XLA Ops:
  7.2 0.0 all-gather.3.cloned.1.call-start
  7.2 0.7 all-gather.3.cloned.1.call-update
  7.9 2.5 %collective-permute-start = (bf16[1,16,2048]{2,1,0:T(8,128)(2,1)}, bf16[1,16,2048]{2,1,0:T(8,128)(2,1)S(1)}, u32[]{:S(2)}, u32[]{:S(2)}) collective-permute-start(bf16[1,16,2048]{2,1,0:T(8,128)(2,1)} %m0_ref.1), channel_id=1, source_target_pairs={{0,16},{16,32},{32,48},{48,0},{1,17},{17,33},{33,49},{49,1},{2,18}... | collective-permute-start | bytes 196616 | tf_op jit(solution)/shard_map/ppermute | solution.py:338
  10.4 3.3 %collective-permute-start.1 = (bf16[1,16,2048]{2,1,0:T(8,128)(2,1)}, bf16[1,16,2048]{2,1,0:T(8,128)(2,1)S(1)}, u32[]{:S(2)}, u32[]{:S(2)}) collective-permute-start(bf16[1,16,2048]{2,1,0:T(8,128)(2,1)} %m0_ref.1), channel_id=1, source_target_pairs={{0,32},{16,48},{32,0},{48,16},{1,33},{17,49},{33,1},{49,17},{2,34}... | collective-permute-start | bytes 196616 | tf_op jit(solution)/shard_map/ppermute | solution.py:338
  13.7 0.7 collective-permute-start.2
  14.5 1.0 fusion.12
  15.5 0.1 broadcast_in_dim.20
  15.6 0.1 broadcast_in_dim.21.hide_ref
  15.7 1.2 copy-done.1
  16.9 1.2 copy-done.2
  18.1 1.3 pack_targets.1._
  19.4 0.0 collective-permute-done.1.m2_ref
  19.4 0.0 collective-permute-done.2.m3_ref
  19.4 5.2 %project.1 = bf16[16,608,128]{2,1,0:T(8,128)(2,1)S(1)} custom-call(s32[1]{0:T(128)} %bitcast.z_ref, bf16[1,16,2048]{2,1,0:T(8,128)(2,1)S(1)} %copy-done.3, bf16[1,16,2048]{2,1,0:T(8,128)(2,1)S(1)} %collective-permute-done.m1_ref, bf16[1,16,2048]{2,1,0:T(8,128)(2,1)S(1)} %collective-permute-done.1.m2_ref, ...), custom_call_target="tpu_custom_call", output_to_operand_aliasing={{}: (7, {})} | custom-call | bytes 12582912 | tf_op jit(solution)/shard_map/project/pallas_call | solution.py:95
  24.7 42.5 %all_to_all.15.kv_ref.r_ref = bf16[16,608,128]{2,1,0:T(8,128)(2,1)S(1)} all-to-all(bf16[16,608,128]{2,1,0:T(8,128)(2,1)S(1)} %project.1), channel_id=1, replica_groups=mesh['sec'=2,'z'=4,'y'=4,'core'=2,'dp'=2] {'sec','y','core'}, dimensions={0} | all-to-all | bytes 4980736 | tf_op jit(solution)/shard_map/all_to_all | solution.py:333
  67.2 37.3 %attend.1 = (bf16[16,256,128]{2,1,0:T(8,128)(2,1)}, bf16[1024,128]{1,0:T(8,128)(2,1)S(1)}) custom-call(bf16[16,608,128]{2,1,0:T(8,128)(2,1)S(1)} %all_to_all.15.kv_ref.r_ref, bf16[16,608,128]{2,1,0:T(8,128)(2,1)S(1)} %all_to_all.15.kv_ref.r_ref), custom_call_target="tpu_custom_call" | custom-call | flops 44999999488 | bytes 4194304 | tf_op jit(solution)/shard_map/attend/pallas_call | solution.py:218
  104.5 4.6 %all-to-all-start.1 = ((bf16[16,256,128]{2,1,0:T(8,128)(2,1)}), bf16[16,256,128]{2,1,0:T(8,128)(2,1)S(1)}, u32[]{:S(2)}, u32[]{:S(2)}) async-start(bf16[16,256,128]{2,1,0:T(8,128)(2,1)} %get-tuple-element.12), calls=%async_computation.1 | async-start | bytes 2097152 | tf_op jit(solution)/shard_map/all_to_all | solution.py:333
  109.1 0.7 collective-permute-start.3
  109.8 2.0 %collective-permute-start.4 = (bf16[1024,128]{1,0:T(8,128)(2,1)S(1)}, bf16[1024,128]{1,0:T(8,128)(2,1)S(1)}, u32[]{:S(2)}, u32[]{:S(2)}) collective-permute-start(bf16[1024,128]{1,0:T(8,128)(2,1)S(1)} %get-tuple-element.11.p0_ref), channel_id=1, source_target_pairs={{0,48},{16,0},{32,16},{48,32},{1,49},{17,1},{33,17},{49,33},{2,50}... | collective-permute-start | bytes 786440 | tf_op jit(solution)/shard_map/ppermute | solution.py:338
  111.8 0.0 collective-permute-start.5
  111.8 11.8 %collective-permute-done.3.p1_ref = bf16[1024,128]{1,0:T(8,128)(2,1)S(1)} collective-permute-done((bf16[1024,128]{1,0:T(8,128)(2,1)S(1)}, bf16[1024,128]{1,0:T(8,128)(2,1)S(1)}, u32[]{:S(2)}, u32[]{:S(2)}) %collective-permute-start.3) | collective-permute-done | bytes 262176 | tf_op jit(solution)/shard_map/ppermute | solution.py:338
  123.6 0.0 collective-permute-done.4.p2_ref
  123.6 0.0 all-gather.3.cloned.1.call-done
  123.6 0.7 copy-done.5
  124.3 0.1 copy-done.6
  124.3 0.1 copy-done.7
  124.5 2.9 %weight_blocks.1 = bf16[32,32,128]{2,1,0:T(8,128)(2,1)} custom-call(s32[1]{0:T(128)} %bitcast.z_ref, bf16[1024,128]{1,0:T(8,128)(2,1)} %copy-done.4, bf16[1024,128]{1,0:T(8,128)(2,1)} %copy-done.5, bf16[1024,128]{1,0:T(8,128)(2,1)} %copy-done.6, bf16[1024,128]{1,0:T(8,128)(2,1)} %copy-done.7, bf16[1024,2048]{1,0:T(8,128)(2,1)} %bitcast.5), custom_call_target="tpu_custom_call" | custom-call | bytes 6291456 | tf_op jit(solution)/shard_map/weight_blocks/pallas_call | solution.py:268
  127.3 8.2 %all-to-all-start.2 = ((bf16[32,32,128]{2,1,0:T(8,128)(2,1)}), bf16[32,32,128]{2,1,0:T(8,128)(2,1)S(1)}, u32[]{:S(2)}, u32[]{:S(2)}) async-start(bf16[32,32,128]{2,1,0:T(8,128)(2,1)} %weight_blocks.1), calls=%async_computation.2 | async-start | bytes 524288 | tf_op jit(solution)/shard_map/all_to_all | solution.py:333
  135.5 1.9 %unpack_targets.1 = bf16[1,512,1024]{2,1,0:T(8,128)(2,1)} custom-call(bf16[16,256,128]{2,1,0:T(8,128)(2,1)S(1)} %all-to-all-done.1.in_ref), custom_call_target="tpu_custom_call" | custom-call | bytes 6291456 | tf_op jit(solution)/shard_map/unpack_targets/pallas_call | solution.py:123
  137.4 6.7 %all-to-all-done.2.in_ref = bf16[32,32,128]{2,1,0:T(8,128)(2,1)S(1)} async-done(((bf16[32,32,128]{2,1,0:T(8,128)(2,1)}), bf16[32,32,128]{2,1,0:T(8,128)(2,1)S(1)}, u32[]{:S(2)}, u32[]{:S(2)}) %all-to-all-start.2) | async-done | bytes 262176 | tf_op jit(solution)/shard_map/all_to_all | solution.py:333
  144.1 2.2 %copy-done = bf16[2048,1024]{1,0:T(8,128)(2,1)S(1)} copy-done((bf16[2048,1024]{1,0:T(8,128)(2,1)S(1)}, bf16[2048,1024]{1,0:T(8,128)(2,1)}, u32[]{:S(2)}) %copy-start) | copy-done | bytes 4194328
  146.3 5.6 %finish.1 = (bf16[1,16,2048]{2,1,0:T(8,128)(2,1)}, f32[16,1024]{1,0:T(8,128)}, f32[16,1024]{1,0:T(8,128)}) custom-call(s32[1]{0:T(128)} %bitcast.4.dp_ref, bf16[32,32,128]{2,1,0:T(8,128)(2,1)S(1)} %all-to-all-done.2.in_ref, bf16[2048,1024]{1,0:T(8,128)(2,1)S(1)} %copy-done, bf16[2048,1024]{1,0:T(8,128)(2,1)} %wv_ref.3), custom_call_target="tpu_custom_call" | custom-call | bytes 12582912 | tf_op jit(solution)/shard_map/finish/pallas_call | solution.py:316
  (14 shorter events, 0.0 us)
Async XLA Ops:
  7.2 12.3 %copy-start.3 = (bf16[1,16,2048]{2,1,0:T(8,128)(2,1)S(1)}, bf16[1,16,2048]{2,1,0:T(8,128)(2,1)}, u32[]{:S(2)}) copy-start(bf16[1,16,2048]{2,1,0:T(8,128)(2,1)} %m0_ref.1) | copy-start | bytes 196612
  7.2 116.4 %all-gather.3.cloned.1.call-start = ((), (), s32[]{:S(2)}) async-start(), calls=%async_computation.3 | async-start | bytes 4259840 | tf_op jit(solution)/shard_map/all_gather | solution.py:356
  7.9 11.5 %collective-permute-start = (bf16[1,16,2048]{2,1,0:T(8,128)(2,1)}, bf16[1,16,2048]{2,1,0:T(8,128)(2,1)S(1)}, u32[]{:S(2)}, u32[]{:S(2)}) collective-permute-start(bf16[1,16,2048]{2,1,0:T(8,128)(2,1)} %m0_ref.1), channel_id=1, source_target_pairs={{0,16},{16,32},{32,48},{48,0},{1,17},{17,33},{33,49},{49,1},{2,18}... | collective-permute-start | bytes 196616 | tf_op jit(solution)/shard_map/ppermute | solution.py:338
  10.4 9.0 %collective-permute-start.1 = (bf16[1,16,2048]{2,1,0:T(8,128)(2,1)}, bf16[1,16,2048]{2,1,0:T(8,128)(2,1)S(1)}, u32[]{:S(2)}, u32[]{:S(2)}) collective-permute-start(bf16[1,16,2048]{2,1,0:T(8,128)(2,1)} %m0_ref.1), channel_id=1, source_target_pairs={{0,32},{16,48},{32,0},{48,16},{1,33},{17,49},{33,1},{49,17},{2,34}... | collective-permute-start | bytes 196616 | tf_op jit(solution)/shard_map/ppermute | solution.py:338
  13.7 5.7 %collective-permute-start.2 = (bf16[1,16,2048]{2,1,0:T(8,128)(2,1)}, bf16[1,16,2048]{2,1,0:T(8,128)(2,1)S(1)}, u32[]{:S(2)}, u32[]{:S(2)}) collective-permute-start(bf16[1,16,2048]{2,1,0:T(8,128)(2,1)} %m0_ref.1), channel_id=1, source_target_pairs={{0,48},{16,0},{32,16},{48,32},{1,49},{17,1},{33,17},{49,33},{2,50}... | collective-permute-start | bytes 196616 | tf_op jit(solution)/shard_map/ppermute | solution.py:338
  15.7 1.2 copy-start.1
  16.9 1.2 copy-start.2
  104.5 19.1 %copy-start.4 = (bf16[1024,128]{1,0:T(8,128)(2,1)}, bf16[1024,128]{1,0:T(8,128)(2,1)S(1)}, u32[]{:S(2)}) copy-start(bf16[1024,128]{1,0:T(8,128)(2,1)S(1)} %get-tuple-element.11.p0_ref) | copy-start | bytes 786436
  104.5 22.8 %all-to-all-start.1 = ((bf16[16,256,128]{2,1,0:T(8,128)(2,1)}), bf16[16,256,128]{2,1,0:T(8,128)(2,1)S(1)}, u32[]{:S(2)}, u32[]{:S(2)}) async-start(bf16[16,256,128]{2,1,0:T(8,128)(2,1)} %get-tuple-element.12), calls=%async_computation.1 | async-start | bytes 2097152 | tf_op jit(solution)/shard_map/all_to_all | solution.py:333
  109.1 14.4 %collective-permute-start.3 = (bf16[1024,128]{1,0:T(8,128)(2,1)S(1)}, bf16[1024,128]{1,0:T(8,128)(2,1)S(1)}, u32[]{:S(2)}, u32[]{:S(2)}) collective-permute-start(bf16[1024,128]{1,0:T(8,128)(2,1)S(1)} %get-tuple-element.11.p0_ref), channel_id=1, source_target_pairs={{0,16},{16,32},{32,48},{48,0},{1,17},{17,33},{33,49},{49,1},{2,18}... | collective-permute-start | bytes 786440 | tf_op jit(solution)/shard_map/ppermute | solution.py:338
  109.8 13.7 %collective-permute-start.4 = (bf16[1024,128]{1,0:T(8,128)(2,1)S(1)}, bf16[1024,128]{1,0:T(8,128)(2,1)S(1)}, u32[]{:S(2)}, u32[]{:S(2)}) collective-permute-start(bf16[1024,128]{1,0:T(8,128)(2,1)S(1)} %get-tuple-element.11.p0_ref), channel_id=1, source_target_pairs={{0,48},{16,0},{32,16},{48,32},{1,49},{17,1},{33,17},{49,33},{2,50}... | collective-permute-start | bytes 786440 | tf_op jit(solution)/shard_map/ppermute | solution.py:338
  111.8 11.8 %collective-permute-start.5 = (bf16[1024,128]{1,0:T(8,128)(2,1)S(1)}, bf16[1024,128]{1,0:T(8,128)(2,1)S(1)}, u32[]{:S(2)}, u32[]{:S(2)}) collective-permute-start(bf16[1024,128]{1,0:T(8,128)(2,1)S(1)} %get-tuple-element.11.p0_ref), channel_id=1, source_target_pairs={{0,32},{16,48},{32,0},{48,16},{1,33},{17,49},{33,1},{49,17},{2,34}... | collective-permute-start | bytes 786440 | tf_op jit(solution)/shard_map/ppermute | solution.py:338
  123.6 0.7 copy-start.5
  123.6 0.8 copy-start.6
  123.6 0.9 copy-start.7
  127.3 16.8 %all-to-all-start.2 = ((bf16[32,32,128]{2,1,0:T(8,128)(2,1)}), bf16[32,32,128]{2,1,0:T(8,128)(2,1)S(1)}, u32[]{:S(2)}, u32[]{:S(2)}) async-start(bf16[32,32,128]{2,1,0:T(8,128)(2,1)} %weight_blocks.1), calls=%async_computation.2 | async-start | bytes 524288 | tf_op jit(solution)/shard_map/all_to_all | solution.py:333
  144.1 2.2 %copy-start = (bf16[2048,1024]{1,0:T(8,128)(2,1)S(1)}, bf16[2048,1024]{1,0:T(8,128)(2,1)}, u32[]{:S(2)}) copy-start(bf16[2048,1024]{1,0:T(8,128)(2,1)} %wk_ref.3) | copy-start | bytes 12582916
Sparse Core Ops, SparseCore 0:
  11.3 79.0 all-gather.2

commit v3 on v2

v3 whole, which is shorter than its diff:
```python
import functools

import jax
import jax.numpy as jnp
from jax import lax
from jax.experimental import pallas as pl
from jax.experimental.pallas import tpu as pltpu
from jax.sharding import Mesh, PartitionSpec as P

HD = 64
BLOCK = 128
LANES = 128
SCALE = 0.125
CHUNK = 256
STEP = 4
NT = (((1,), (1,)), ((), ()))
NN = (((1,), (0,)), ((), ()))
TN = (((0,), (0,)), ((), ()))
HEAD_AXES = ("sec", "y", "core")
SAMPLE_AXES = ("sec", "z", "y", "core")
ALL_AXES = ("sec", "z", "y", "core", "dp")
bf16 = jnp.bfloat16
f32 = jnp.float32


def dot(a, b, dims):
    return lax.dot_general(a, b, dims, preferred_element_type=f32)


def low_half():
    return lax.broadcasted_iota(jnp.int32, (1, LANES), 1) < HD


def swap_halves(a, b):
    lo = low_half()
    return jnp.where(lo, a, pltpu.roll(b, HD, 1)), jnp.where(lo, pltpu.roll(a, HD, 1), b)


def params(mib=48, **kw):
    return pltpu.CompilerParams(vmem_limit_bytes=mib << 20, **kw)


ROWS = (336, 272)
KV_ROW = 256


def pack_kernel(q_ref, g_ref, hide_ref, *out_refs):
    for t, out_ref in enumerate(out_refs):
        for i in range(2):
            cols = slice(i * LANES, (i + 1) * LANES)
            for k, ref in enumerate((q_ref, g_ref)):
                a = ref[0, t * 256 : t * 256 + 128, cols].astype(f32)
                b = ref[0, t * 256 + 128 : t * 256 + 256, cols].astype(f32)
                even, odd = swap_halves(a, b)
                out_ref[2 * i, k * 128 : k * 128 + 128, :] = even.astype(bf16)
                out_ref[2 * i + 1, k * 128 : k * 128 + 128, :] = odd.astype(bf16)
        for i in range(4):
            if t == 0:
                out_ref[i, KV_ROW : KV_ROW + 64, :] = jnp.zeros((64, LANES), bf16)
            out_ref[i, ROWS[t] - 16 : ROWS[t], :] = hide_ref[t * 16 : t * 16 + 16, :]


def pack_targets(q, g, hide):
    return pl.pallas_call(
        pack_kernel,
        grid=(4,),
        in_specs=[
            pl.BlockSpec((1, 512, 256), lambda p: (0, 0, p)),
            pl.BlockSpec((1, 512, 256), lambda p: (0, 0, p)),
            pl.BlockSpec((32, LANES), lambda p: (0, 0)),
        ],
        out_specs=[pl.BlockSpec((4, rows, LANES), lambda p: (p, 0, 0)) for rows in ROWS],
        out_shape=[jax.ShapeDtypeStruct((16, rows, LANES), bf16) for rows in ROWS],
        compiler_params=params(),
        cost_estimate=pl.CostEstimate(flops=0, bytes_accessed=9 << 20, transcendentals=0),
        name="pack_targets",
    )(q, g, hide)


def project_kernel(z_ref, m0_ref, m1_ref, m2_ref, m3_ref, wk_ref, wv_ref, _, out_ref):
    mem = jnp.concatenate([m0_ref[0], m1_ref[0], m2_ref[0], m3_ref[0]], 0)
    k = dot(mem, wk_ref[...], NN)
    v = dot(mem, wv_ref[...], NN)
    for i in range(4):
        cols = slice(i * LANES, (i + 1) * LANES)
        even, odd = swap_halves(k[:, cols], v[:, cols])
        for j in range(4):
            at = pl.multiple_of(lax.rem(z_ref[0] + 4 - j, 4) * 16, 16)
            out_ref[2 * i, pl.ds(at, 16), :] = even[j * 16 : j * 16 + 16].astype(bf16)
            out_ref[2 * i + 1, pl.ds(at, 16), :] = odd[j * 16 : j * 16 + 16].astype(bf16)


def project(z, mems, wk, wv, payload):
    d = wk.shape[0]
    mem_spec = pl.BlockSpec((1, 16, d), lambda p, z: (0, 0, 0))
    w_spec = pl.BlockSpec((d, 512), lambda p, z: (0, p))
    return pl.pallas_call(
        project_kernel,
        grid_spec=pltpu.PrefetchScalarGridSpec(
            num_scalar_prefetch=1,
            grid=(2,),
            in_specs=[mem_spec] * 4 + [w_spec] * 2 + [pl.BlockSpec(memory_space=pl.ANY)],
            out_specs=pl.BlockSpec((8, 64, LANES), lambda p, z: (p, KV_ROW // 64, 0)),
        ),
        out_shape=jax.ShapeDtypeStruct(payload.shape, bf16),
        input_output_aliases={7: 0},
        compiler_params=params(60),
        cost_estimate=pl.CostEstimate(flops=0, bytes_accessed=12 << 20, transcendentals=0),
        name="project",
    )(z, *mems, wk, wv, payload)


def unpack_kernel(first_ref, second_ref, out_ref):
    for t, ref in enumerate((first_ref, second_ref)):
        for i in range(2):
            a, b = swap_halves(ref[2 * i].astype(f32), ref[2 * i + 1].astype(f32))
            cols = slice(i * LANES, (i + 1) * LANES)
            out_ref[0, t * 256 : t * 256 + 128, cols] = a.astype(bf16)
            out_ref[0, t * 256 + 128 : t * 256 + 256, cols] = b.astype(bf16)


def unpack_targets(first, second):
    return pl.pallas_call(
        unpack_kernel,
        grid=(4,),
        in_specs=[pl.BlockSpec((4, LANES, LANES), lambda p: (p, 0, 0))] * 2,
        out_specs=pl.BlockSpec((1, 512, 256), lambda p: (0, 0, p)),
        out_shape=jax.ShapeDtypeStruct((1, 512, 1024), bf16),
        compiler_params=params(),
        cost_estimate=pl.CostEstimate(flops=0, bytes_accessed=6 << 20, transcendentals=0),
        name="unpack_targets",
    )(first, second)


def one_tile(q, g, away, k2_ref, v2_ref, kt_ref, ka_ref, va_ref):
    lo = low_half()
    n = k2_ref.shape[0]
    per = CHUNK // BLOCK
    chunks = n // CHUNK
    rows = [slice(c * CHUNK, c * CHUNK + CHUNK) for c in range(chunks)]
    q = q * jnp.asarray(SCALE, bf16)
    zero = jnp.zeros_like(q)
    q2 = jnp.concatenate([jnp.where(lo, q, zero), jnp.where(lo, zero, q)], 0)
    g2 = jnp.concatenate([jnp.where(lo, g, zero), jnp.where(lo, zero, g)], 0)
    scores = [dot(k2_ref[r, :], q2, NT) for r in rows]
    hidden = []
    top = None
    for j in range(n // BLOCK):
        part = scores[j // per][(j % per) * BLOCK : (j % per + 1) * BLOCK]
        hide = jnp.concatenate([away[j : j + 1], away[8 + j : 9 + j]], 1)
        hidden.append(hide)
        part_top = jnp.max(part, axis=0, keepdims=True) - hide
        top = part_top if top is None else jnp.maximum(top, part_top)
    expd = []
    total = None
    for c in range(chunks):
        parts = [
            jnp.exp(scores[c][i * BLOCK : (i + 1) * BLOCK] - (top + hidden[c * per + i]))
            for i in range(per)
        ]
        e = jnp.concatenate(parts, 0)
        expd.append(e)
        s = jnp.sum(e, axis=0, keepdims=True)
        total = s if total is None else total + s
    inverse = 1.0 / total
    dprobs = []
    delta = None
    for c in range(chunks):
        dp = dot(v2_ref[rows[c], :], g2, NT)
        dprobs.append(dp)
        s = jnp.sum(expd[c] * dp, axis=0, keepdims=True)
        delta = s if delta is None else delta + s
    delta = delta * inverse
    qgt = None
    for c in range(chunks):
        p = expd[c] * inverse
        ds = (p * (dprobs[c] - delta)).astype(bf16)
        va_ref[rows[c], :] += dot(p.astype(bf16), g2, NN)
        ka_ref[rows[c], :] += dot(ds, q2, NN)
        x = dot(kt_ref[:, rows[c]], ds, NN)
        qgt = x if qgt is None else qgt + x
    qgt = qgt * SCALE
    both = jnp.concatenate([qgt[:, :LANES], qgt[:, LANES:]], 0)
    return jnp.transpose(both).astype(bf16)


def attend_kernel(*refs, half):
    if half == 0:
        kv_ref, r_ref, qg_ref, ka_ref, va_ref, k2_ref, v2_ref, kt_ref = refs
    else:
        kv_ref, r_ref, k0_ref, v0_ref, qg_ref, kvg_ref, k2_ref, v2_ref, kt_ref, ka_ref, va_ref = refs
    lo = low_half()

    @pl.when(pl.program_id(0) == 0)
    def _():
        order = [(c, z) for c in (0, 8) for z in range(4)]
        kv = jnp.concatenate(
            [kv_ref[c + i, z * 16 : z * 16 + 16, :] for c, z in order for i in range(8)], 0
        ).astype(f32)
        swapped = pltpu.roll(kv, HD, 1)
        k2 = jnp.where(lo, kv, swapped)
        k2_ref[...] = k2.astype(bf16)
        v2_ref[...] = jnp.where(lo, swapped, kv).astype(bf16)
        kt_ref[...] = jnp.transpose(k2)[:HD].astype(bf16)
        ka_ref[...] = jnp.zeros_like(ka_ref) if half == 0 else k0_ref[...]
        va_ref[...] = jnp.zeros_like(va_ref) if half == 0 else v0_ref[...]

    for i in range(r_ref.shape[0]):
        away = r_ref[i, ROWS[half] - 16 : ROWS[half], :].astype(f32)
        q = r_ref[i, 0:128, :]
        g = r_ref[i, 128:256, :]
        qg_ref[i] = one_tile(q, g, away, k2_ref, v2_ref, kt_ref, ka_ref, va_ref)

    if half == 1:

        @pl.when(pl.program_id(0) == pl.num_programs(0) - 1)
        def _():
            ka = ka_ref[...]
            va = va_ref[...]
            ka = ka + pltpu.roll(ka, HD, 1)
            va = va + pltpu.roll(va, HD, 1)
            kvg_ref[...] = jnp.where(lo, ka, va).astype(bf16)


def attend(half, kv, r, *sums):
    sources = r.shape[0]
    n = 64 * sources
    whole = pl.BlockSpec((n, LANES), lambda i: (0, 0))
    wide = jax.ShapeDtypeStruct((n, LANES), f32)
    kept = [pltpu.VMEM((n, LANES), bf16), pltpu.VMEM((n, LANES), bf16), pltpu.VMEM((HD, n), bf16)]
    held = [pltpu.VMEM((n, LANES), f32), pltpu.VMEM((n, LANES), f32)]
    return pl.pallas_call(
        functools.partial(attend_kernel, half=half),
        grid=(sources // STEP,),
        in_specs=[
            pl.BlockSpec((sources, 64, LANES), lambda i: (0, KV_ROW // 64, 0)),
            pl.BlockSpec((STEP, ROWS[half], LANES), lambda i: (i, 0, 0)),
        ]
        + [whole] * len(sums),
        out_specs=[pl.BlockSpec((STEP, LANES, LANES), lambda i: (i, 0, 0))]
        + ([whole, whole] if half == 0 else [whole]),
        scratch_shapes=kept + ([] if half == 0 else held),
        out_shape=[jax.ShapeDtypeStruct((sources, LANES, LANES), bf16)]
        + ([wide, wide] if half == 0 else [jax.ShapeDtypeStruct((n, LANES), bf16)]),
        compiler_params=params(dimension_semantics=("arbitrary",)),
        cost_estimate=pl.CostEstimate(
            flops=22_000_000_000, bytes_accessed=2 << 20, transcendentals=0
        ),
        name="attend",
    )(kv, r, *sums)


def weight_kernel(z_ref, p0_ref, p1_ref, p2_ref, p3_ref, mem_ref, out_ref, total_ref):
    step = pl.program_id(0)

    @pl.when(step == 0)
    def _():
        total = p0_ref[...].astype(f32) + p1_ref[...].astype(f32)
        total = total + (p2_ref[...].astype(f32) + p3_ref[...].astype(f32))
        total_ref[...] = total.astype(bf16)

    grad = dot(mem_ref[...], total_ref[...], TN).astype(bf16)
    at = pl.multiple_of(step * 512 + z_ref[0] * 128, 128)
    tokens = total_ref[pl.ds(at, 128), :]
    for i in range(16):
        out_ref[i, 0:16, :] = grad[i * 16 : i * 16 + 16]
        out_ref[i, 16:32, :] = tokens[(i // 2) * 16 : (i // 2) * 16 + 16]


def weight_blocks(z, parts, mem):
    n = mem.shape[0]
    part_spec = pl.BlockSpec((n, LANES), lambda s, z: (0, 0))
    return pl.pallas_call(
        weight_kernel,
        grid_spec=pltpu.PrefetchScalarGridSpec(
            num_scalar_prefetch=1,
            grid=(2,),
            in_specs=[part_spec] * 4 + [pl.BlockSpec((n, 256), lambda s, z: (0, s * 4 + z[0]))],
            out_specs=pl.BlockSpec((16, 32, LANES), lambda s, z: (s, 0, 0)),
            scratch_shapes=[pltpu.VMEM((n, LANES), bf16)],
        ),
        out_shape=jax.ShapeDtypeStruct((32, 32, LANES), bf16),
        compiler_params=params(60, dimension_semantics=("arbitrary",)),
        cost_estimate=pl.CostEstimate(flops=0, bytes_accessed=6 << 20, transcendentals=0),
        name="weight_blocks",
    )(z, *parts, mem)


def finish_kernel(dp_ref, in_ref, wk_ref, wv_ref, mg_ref, wkg_ref, wvg_ref, acc_ref):
    p = pl.program_id(0)
    grads = []
    for i in range(4):
        cols = slice(i * LANES, (i + 1) * LANES)
        rows = [in_ref[4 * i + j, 0:16, :].astype(f32) for j in range(4)]
        wkg_ref[:, cols], wvg_ref[:, cols] = swap_halves(rows[0] + rows[1], rows[2] + rows[3])
        even = in_ref[pl.ds(4 * i + dp_ref[0], 1), 16:32, :][0].astype(f32)
        odd = in_ref[pl.ds(4 * i + 2 + dp_ref[0], 1), 16:32, :][0].astype(f32)
        grads.append(swap_halves(even, odd))
    kg = jnp.concatenate([x[0] for x in grads], 1).astype(bf16)
    vg = jnp.concatenate([x[1] for x in grads], 1).astype(bf16)
    part = dot(kg, wk_ref[...], NT) + dot(vg, wv_ref[...], NT)

    @pl.when(p == 0)
    def _():
        acc_ref[...] = part

    @pl.when(p > 0)
    def _():
        acc_ref[...] += part

    @pl.when(p == pl.num_programs(0) - 1)
    def _():
        mg_ref[0] = acc_ref[...].astype(bf16)


def finish(dp, x, wk, wv):
    d = wk.shape[0]
    w_spec = pl.BlockSpec((d, 512), lambda p, dp: (0, p))
    out_spec = pl.BlockSpec((16, 512), lambda p, dp: (0, p))
    shape = jax.ShapeDtypeStruct((16, wk.shape[1]), f32)
    return pl.pallas_call(
        finish_kernel,
        grid_spec=pltpu.PrefetchScalarGridSpec(
            num_scalar_prefetch=1,
            grid=(2,),
            in_specs=[pl.BlockSpec((16, 32, LANES), lambda p, dp: (p, 0, 0)), w_spec, w_spec],
            out_specs=[pl.BlockSpec((1, 16, d), lambda p, dp: (0, 0, 0)), out_spec, out_spec],
            scratch_shapes=[pltpu.VMEM((16, d), f32)],
        ),
        out_shape=[jax.ShapeDtypeStruct((1, 16, d), bf16), shape, shape],
        compiler_params=params(60, dimension_semantics=("arbitrary",)),
        cost_estimate=pl.CostEstimate(flops=0, bytes_accessed=12 << 20, transcendentals=0),
        name="finish",
    )(dp, x, wk, wv)


def exchange(x, axes):
    return lax.all_to_all(x, axes, 0, 0, tiled=True)


def shifted(x, axis, k):
    n = lax.axis_size(axis)
    return lax.ppermute(x, axis, [(i, (i + k) % n) for i in range(n)])


def body(q, g, mem, wk, wv, target_modality, memory_modality, allow_pairs):
    z = lax.axis_index("z").reshape(1)
    dp = lax.axis_index("dp").reshape(1)
    mems = [mem] + [shifted(mem, "z", k) for k in (1, 2, 3)]

    labels = jnp.arange(allow_pairs.shape[0], dtype=jnp.int32)
    q_onehot = (target_modality[0][:, None] == labels[None, :]).astype(f32)
    k_onehot = (memory_modality[0][:, None] == labels[None, :]).astype(f32)
    allowed = jnp.dot(jnp.dot(q_onehot, allow_pairs.astype(f32)), k_onehot.T) > 0.5
    allowed = allowed | (jnp.arange(allowed.shape[1], dtype=jnp.int32) == 0)[None, :]
    hide = jnp.where(allowed, 0.0, 1e30).astype(bf16).reshape(32, 1)
    hide = jnp.broadcast_to(hide, (32, LANES))

    first, second = pack_targets(q, g, hide)
    first = exchange(project(z, mems, wk, wv, first), HEAD_AXES)
    memory = lax.all_gather(mem[0], SAMPLE_AXES, axis=0, tiled=True)
    first, second = lax.optimization_barrier((first, second))
    second = exchange(second, HEAD_AXES)

    q_first, k_sum, v_sum = attend(0, first, first)
    q_first = exchange(q_first, HEAD_AXES)
    q_second, part = attend(1, first, second, k_sum, v_sum)
    q_second = exchange(q_second, HEAD_AXES)
    parts = [part] + [shifted(part, "z", k) for k in (1, 3, 2)]
    blocks = weight_blocks(z, parts, memory)
    blocks, q_second = lax.optimization_barrier((blocks, q_second))
    blocks = exchange(blocks, ("sec", "y", "core", "dp"))
    m_grad, wk_grad, wv_grad = finish(dp, blocks, wk, wv)
    return unpack_targets(q_first, q_second), m_grad, wk_grad, wv_grad


def solution(mesh):
    fine = Mesh(mesh.devices.reshape(2, 4, 4, 2, 2), ALL_AXES)
    rows = P("dp", SAMPLE_AXES, None)
    in_specs = (rows, rows, rows, P(), P(), P("dp", SAMPLE_AXES), P("dp", None), P())
    out_specs = (rows, rows, P(ALL_AXES, None), P(ALL_AXES, None))
    return jax.shard_map(body, mesh=fine, in_specs=in_specs, out_specs=out_specs, check_vma=False)
```

time: 159 us -> 175 us (1.10)
  waiting for transfers between devices: 19.2 us -> 26.2 us
  starting transfers between devices: 22.1 us -> 26.8 us
  blocking collectives: 42.5 us -> 45.5 us
  local copies, waits for them, and re-layouts: 5.65 us -> 7.81 us
    all_to_all x2 -> x3, waiting for transfers between devices: 6.75 us -> 13.7 us  [exchange(): return lax.all_to_all(x, axes, 0, 0, tiled=True)]
    all_to_all x2 -> x3, starting transfers between devices: 12.8 us -> 17.6 us  [exchange(): return lax.all_to_all(x, axes, 0, 0, tiled=True)]
    all_to_all x1 -> x2, blocking collectives: 42.5 us -> 45.5 us  [exchange(): return lax.all_to_all(x, axes, 0, 0, tiled=True)]
    pallas_call x2 -> x3, Pallas kernels: 39.2 us -> 36.7 us  [the longest x2 34.8 us: attend(): pl.pallas_call(functools.partial(attend_kernel, half=half), grid=(sources...]
    unnamed x16 -> x26, local copies, waits for them, and re-layouts: 5.49 us -> 7.65 us
  transfers between devices with their start and end apart: 9 -> 10, of which waited for: 2 -> 3; matrix products, arithmetic and copies ran while one was open for 1% -> 1% of each run, Pallas kernels for 31% -> 27%
where the time goes in v3:
time: 175 us; the launch traced here: 174 us
  Pallas kernels  52.6 us (30%)
  blocking collectives  45.5 us (26%)
  starting transfers between devices  26.8 us (15%)
  waiting for transfers between devices  26.2 us (15%)
  between operations  14.1 us (8%)
  local copies, waits for them, and re-layouts  7.81 us (4%)
    all_to_all x2, blocking collectives, exchange(): return lax.all_to_all(x, axes, 0, 0, tiled=True)  45.5 us
    pallas_call x2, Pallas kernels, attend(): pl.pallas_call(functools.partial(attend_kernel, half=half), grid=(sources...  34.8 us
    all_to_all x3, starting transfers between devices, exchange(): return lax.all_to_all(x, axes, 0, 0, tiled=True)  17.6 us
    all_to_all x3, waiting for transfers between devices, exchange(): return lax.all_to_all(x, axes, 0, 0, tiled=True)  13.7 us
    ppermute x6, waiting for transfers between devices, shifted(): return lax.ppermute(x, axis, [(i, (i + k) % n) for i in range(n)])  11.8 us
    ppermute x6, starting transfers between devices, shifted(): return lax.ppermute(x, axis, [(i, (i + k) % n) for i in range(n)])  9.25 us
    unnamed x26, local copies, waits for them, and re-layouts  7.65 us
    pallas_call x1, Pallas kernels, finish(): pl.pallas_call(finish_kernel, grid_spec=pltpu.PrefetchScalarGridSpec(num_...  5.42 us
  transfers between devices with their start and end apart: 10, of which 3 were waited for; matrix products, arithmetic and copies ran while one was open for 1% of the time, Pallas kernels for 27%

profile of v3, /device:TPU:1, one launch (start us, length us, event | category | flops | bytes accessed | tf_op | source)
XLA Modules:
  0.0 174.1 jit_solution(3162112072841635704)
XLA Ops:
  7.2 0.7 all-gather.3.cloned.1.call-update
  7.9 2.5 %collective-permute-start = (bf16[1,16,2048]{2,1,0:T(8,128)(2,1)}, bf16[1,16,2048]{2,1,0:T(8,128)(2,1)S(1)}, u32[]{:S(2)}, u32[]{:S(2)}) collective-permute-start(bf16[1,16,2048]{2,1,0:T(8,128)(2,1)} %m0_ref.1), channel_id=1, source_target_pairs={{0,16},{16,32},{32,48},{48,0},{1,17},{17,33},{33,49},{49,1},{2,18}... | collective-permute-start | bytes 196616 | tf_op jit(solution)/shard_map/ppermute | solution.py:343
  10.4 3.3 %collective-permute-start.1 = (bf16[1,16,2048]{2,1,0:T(8,128)(2,1)}, bf16[1,16,2048]{2,1,0:T(8,128)(2,1)S(1)}, u32[]{:S(2)}, u32[]{:S(2)}) collective-permute-start(bf16[1,16,2048]{2,1,0:T(8,128)(2,1)} %m0_ref.1), channel_id=1, source_target_pairs={{0,32},{16,48},{32,0},{48,16},{1,33},{17,49},{33,1},{49,17},{2,34}... | collective-permute-start | bytes 196616 | tf_op jit(solution)/shard_map/ppermute | solution.py:343
  13.7 0.7 collective-permute-start.2
  14.5 1.0 fusion.12
  15.6 1.2 copy-done.1
  16.9 1.2 copy-done.2
  18.1 2.4 %pack_targets.1 = (bf16[16,336,128]{2,1,0:T(8,128)(2,1)S(1)}, bf16[16,272,128]{2,1,0:T(8,128)(2,1)}) custom-call(bf16[1,512,1024]{2,1,0:T(8,128)(2,1)S(1)} %copy-done.1, bf16[1,512,1024]{2,1,0:T(8,128)(2,1)S(1)} %copy-done.2, bf16[32,128]{1,0:T(8,128)(2,1)S(1)} %broadcast_in_dim.21.hide_ref), custom_call_target="tpu_custom_call" | custom-call | bytes 9437184 | tf_op jit(solution)/shard_map/pack_targets/pallas_call | solution.py:64
  20.5 1.1 copy-done
  21.7 0.6 copy-done.10
  22.3 5.2 %project.1 = bf16[16,336,128]{2,1,0:T(8,128)(2,1)} custom-call(s32[1]{0:T(128)} %bitcast.z_ref, bf16[1,16,2048]{2,1,0:T(8,128)(2,1)} %m0_ref.1, bf16[1,16,2048]{2,1,0:T(8,128)(2,1)} %copy-done.10, bf16[1,16,2048]{2,1,0:T(8,128)(2,1)} %copy-done.11, bf16[1,16,2048]{2,1,0:T(8,128)(2,1)} %copy-done.12, ...), custom_call_target="tpu_custom_call", output_to_operand_aliasing={{}: (7, {})} | custom-call | bytes 12582912 | tf_op jit(solution)/shard_map/project/pallas_call | solution.py:97
  27.5 30.8 %all_to_all.25.refs_0_.refs_1_ = bf16[16,336,128]{2,1,0:T(8,128)(2,1)S(1)} all-to-all(bf16[16,336,128]{2,1,0:T(8,128)(2,1)} %project.1), channel_id=1, replica_groups=mesh['sec'=2,'z'=4,'y'=4,'core'=2,'dp'=2] {'sec','y','core'}, dimensions={0} | all-to-all | bytes 2752512 | tf_op jit(solution)/shard_map/all_to_all | solution.py:338
  58.3 4.7 %all-to-all-start.2 = ((bf16[16,272,128]{2,1,0:T(8,128)(2,1)}), bf16[16,272,128]{2,1,0:T(8,128)(2,1)S(1)}, u32[]{:S(2)}, u32[]{:S(2)}) async-start(bf16[16,272,128]{2,1,0:T(8,128)(2,1)} %get-tuple-element.22), calls=%async_computation.2 | async-start | bytes 2228224 | tf_op jit(solution)/shard_map/all_to_all | solution.py:338
  62.9 17.6 %attend.2 = (bf16[16,128,128]{2,1,0:T(8,128)(2,1)}, f32[1024,128]{1,0:T(8,128)S(1)}, f32[1024,128]{1,0:T(8,128)S(1)}) custom-call(bf16[16,336,128]{2,1,0:T(8,128)(2,1)S(1)} %all_to_all.25.refs_0_.refs_1_, bf16[16,336,128]{2,1,0:T(8,128)(2,1)S(1)} %all_to_all.25.refs_0_.refs_1_), custom_call_target="tpu_custom_call" | custom-call | flops 22000001024 | bytes 2097152 | tf_op jit(solution)/shard_map/attend/pallas_call | solution.py:232
  80.5 0.8 copy-done.4
  81.3 7.0 %all-to-all-done.2.refs_1_ = bf16[16,272,128]{2,1,0:T(8,128)(2,1)S(1)} async-done(((bf16[16,272,128]{2,1,0:T(8,128)(2,1)}), bf16[16,272,128]{2,1,0:T(8,128)(2,1)S(1)}, u32[]{:S(2)}, u32[]{:S(2)}) %all-to-all-start.2) | async-done | bytes 1114144 | tf_op jit(solution)/shard_map/all_to_all | solution.py:338
  88.3 1.0 copy-done.5
  89.3 17.3 %attend.3 = (bf16[16,128,128]{2,1,0:T(8,128)(2,1)S(1)}, bf16[1024,128]{1,0:T(8,128)(2,1)S(1)}) custom-call(bf16[16,336,128]{2,1,0:T(8,128)(2,1)S(1)} %all_to_all.25.refs_0_.refs_1_, bf16[16,272,128]{2,1,0:T(8,128)(2,1)S(1)} %all-to-all-done.2.refs_1_, f32[1024,128]{1,0:T(8,128)S(1)} %get-tuple-element.23.refs_2_, f32[1024,128]{1,0:T(8,128)S(1)} %copy-done.5), custom_call_target="tpu_custom_call" | custom-call | flops 22000001024 | bytes 2097152 | tf_op jit(solution)/shard_map/attend/pallas_call | solution.py:232
  106.6 14.7 %all_to_all.26.second_ref = bf16[16,128,128]{2,1,0:T(8,128)(2,1)S(1)} all-to-all(bf16[16,128,128]{2,1,0:T(8,128)(2,1)S(1)} %get-tuple-element.26), channel_id=1, replica_groups=mesh['sec'=2,'z'=4,'y'=4,'core'=2,'dp'=2] {'sec','y','core'}, dimensions={0} | all-to-all | bytes 1048576 | tf_op jit(solution)/shard_map/all_to_all | solution.py:338
  121.4 4.7 %all-to-all-start.1 = ((bf16[16,128,128]{2,1,0:T(8,128)(2,1)}), bf16[16,128,128]{2,1,0:T(8,128)(2,1)S(1)}, u32[]{:S(2)}, u32[]{:S(2)}) async-start(bf16[16,128,128]{2,1,0:T(8,128)(2,1)} %get-tuple-element.21), calls=%async_computation.1 | async-start | bytes 1048576 | tf_op jit(solution)/shard_map/all_to_all | solution.py:338
  126.1 0.7 collective-permute-start.3
  126.8 2.0 %collective-permute-start.4 = (bf16[1024,128]{1,0:T(8,128)(2,1)S(1)}, bf16[1024,128]{1,0:T(8,128)(2,1)S(1)}, u32[]{:S(2)}, u32[]{:S(2)}) collective-permute-start(bf16[1024,128]{1,0:T(8,128)(2,1)S(1)} %get-tuple-element.25.p0_ref), channel_id=1, source_target_pairs={{0,48},{16,0},{32,16},{48,32},{1,49},{17,1},{33,17},{49,33},{2,50}... | collective-permute-start | bytes 786440 | tf_op jit(solution)/shard_map/ppermute | solution.py:343
  128.7 11.8 %collective-permute-done.3.p1_ref = bf16[1024,128]{1,0:T(8,128)(2,1)S(1)} collective-permute-done((bf16[1024,128]{1,0:T(8,128)(2,1)S(1)}, bf16[1024,128]{1,0:T(8,128)(2,1)S(1)}, u32[]{:S(2)}, u32[]{:S(2)}) %collective-permute-start.3) | collective-permute-done | bytes 262176 | tf_op jit(solution)/shard_map/ppermute | solution.py:343
  140.6 0.6 copy-done.7
  141.2 0.1 copy-done.8
  141.3 0.1 copy-done.9
  141.4 2.9 %weight_blocks.1 = bf16[32,32,128]{2,1,0:T(8,128)(2,1)} custom-call(s32[1]{0:T(128)} %bitcast.z_ref, bf16[1024,128]{1,0:T(8,128)(2,1)} %copy-done.3, bf16[1024,128]{1,0:T(8,128)(2,1)} %copy-done.7, bf16[1024,128]{1,0:T(8,128)(2,1)} %copy-done.8, bf16[1024,128]{1,0:T(8,128)(2,1)} %copy-done.9, bf16[1024,2048]{1,0:T(8,128)(2,1)} %bitcast.5), custom_call_target="tpu_custom_call" | custom-call | bytes 6291456 | tf_op jit(solution)/shard_map/weight_blocks/pallas_call | solution.py:273
  144.3 8.2 %all-to-all-start.4 = ((bf16[32,32,128]{2,1,0:T(8,128)(2,1)}), bf16[32,32,128]{2,1,0:T(8,128)(2,1)S(1)}, u32[]{:S(2)}, u32[]{:S(2)}) async-start(bf16[32,32,128]{2,1,0:T(8,128)(2,1)} %weight_blocks.1), calls=%async_computation.4 | async-start | bytes 524288 | tf_op jit(solution)/shard_map/all_to_all | solution.py:338
  152.5 1.9 %unpack_targets.1 = bf16[1,512,1024]{2,1,0:T(8,128)(2,1)} custom-call(bf16[16,128,128]{2,1,0:T(8,128)(2,1)S(1)} %all-to-all-done.1.first_ref, bf16[16,128,128]{2,1,0:T(8,128)(2,1)S(1)} %all_to_all.26.second_ref), custom_call_target="tpu_custom_call" | custom-call | bytes 6291456 | tf_op jit(solution)/shard_map/unpack_targets/pallas_call | solution.py:123
  154.3 6.7 %all-to-all-done.4.in_ref = bf16[32,32,128]{2,1,0:T(8,128)(2,1)S(1)} async-done(((bf16[32,32,128]{2,1,0:T(8,128)(2,1)}), bf16[32,32,128]{2,1,0:T(8,128)(2,1)S(1)}, u32[]{:S(2)}, u32[]{:S(2)}) %all-to-all-start.4) | async-done | bytes 262176 | tf_op jit(solution)/shard_map/all_to_all | solution.py:338
  161.1 0.7 copy-done.6
  161.8 5.4 %finish.1 = (bf16[1,16,2048]{2,1,0:T(8,128)(2,1)}, f32[16,1024]{1,0:T(8,128)}, f32[16,1024]{1,0:T(8,128)}) custom-call(s32[1]{0:T(128)} %bitcast.4.dp_ref, bf16[32,32,128]{2,1,0:T(8,128)(2,1)} %copy-done.6, bf16[2048,1024]{1,0:T(8,128)(2,1)} %wk_ref.3, bf16[2048,1024]{1,0:T(8,128)(2,1)} %wv_ref.3), custom_call_target="tpu_custom_call" | custom-call | bytes 12582912 | tf_op jit(solution)/shard_map/finish/pallas_call | solution.py:321
  (28 shorter events, 0.3 us)
Async XLA Ops:
  7.2 133.4 %all-gather.3.cloned.1.call-start = ((), (), s32[]{:S(2)}) async-start(), calls=%async_computation.5 | async-start | bytes 4259840 | tf_op jit(solution)/shard_map/all_gather | solution.py:361
  7.9 13.7 %collective-permute-start = (bf16[1,16,2048]{2,1,0:T(8,128)(2,1)}, bf16[1,16,2048]{2,1,0:T(8,128)(2,1)S(1)}, u32[]{:S(2)}, u32[]{:S(2)}) collective-permute-start(bf16[1,16,2048]{2,1,0:T(8,128)(2,1)} %m0_ref.1), channel_id=1, source_target_pairs={{0,16},{16,32},{32,48},{48,0},{1,17},{17,33},{33,49},{49,1},{2,18}... | collective-permute-start | bytes 196616 | tf_op jit(solution)/shard_map/ppermute | solution.py:343
  10.4 11.2 %collective-permute-start.1 = (bf16[1,16,2048]{2,1,0:T(8,128)(2,1)}, bf16[1,16,2048]{2,1,0:T(8,128)(2,1)S(1)}, u32[]{:S(2)}, u32[]{:S(2)}) collective-permute-start(bf16[1,16,2048]{2,1,0:T(8,128)(2,1)} %m0_ref.1), channel_id=1, source_target_pairs={{0,32},{16,48},{32,0},{48,16},{1,33},{17,49},{33,1},{49,17},{2,34}... | collective-permute-start | bytes 196616 | tf_op jit(solution)/shard_map/ppermute | solution.py:343
  13.7 7.9 %collective-permute-start.2 = (bf16[1,16,2048]{2,1,0:T(8,128)(2,1)}, bf16[1,16,2048]{2,1,0:T(8,128)(2,1)S(1)}, u32[]{:S(2)}, u32[]{:S(2)}) collective-permute-start(bf16[1,16,2048]{2,1,0:T(8,128)(2,1)} %m0_ref.1), channel_id=1, source_target_pairs={{0,48},{16,0},{32,16},{48,32},{1,49},{17,1},{33,17},{49,33},{2,50}... | collective-permute-start | bytes 196616 | tf_op jit(solution)/shard_map/ppermute | solution.py:343
  15.6 1.2 copy-start.1
  16.9 1.2 copy-start.2
  20.5 1.1 copy-start
  21.6 0.6 copy-start.10
  21.6 0.6 copy-start.11
  21.7 0.6 copy-start.12
  58.3 30.0 %all-to-all-start.2 = ((bf16[16,272,128]{2,1,0:T(8,128)(2,1)}), bf16[16,272,128]{2,1,0:T(8,128)(2,1)S(1)}, u32[]{:S(2)}, u32[]{:S(2)}) async-start(bf16[16,272,128]{2,1,0:T(8,128)(2,1)} %get-tuple-element.22), calls=%async_computation.2 | async-start | bytes 2228224 | tf_op jit(solution)/shard_map/all_to_all | solution.py:338
  80.5 0.8 copy-start.4
  88.3 1.0 copy-start.5
  106.6 33.9 %copy-start.3 = (bf16[1024,128]{1,0:T(8,128)(2,1)}, bf16[1024,128]{1,0:T(8,128)(2,1)S(1)}, u32[]{:S(2)}) copy-start(bf16[1024,128]{1,0:T(8,128)(2,1)S(1)} %get-tuple-element.25.p0_ref) | copy-start | bytes 786436
  121.4 22.9 %all-to-all-start.1 = ((bf16[16,128,128]{2,1,0:T(8,128)(2,1)}), bf16[16,128,128]{2,1,0:T(8,128)(2,1)S(1)}, u32[]{:S(2)}, u32[]{:S(2)}) async-start(bf16[16,128,128]{2,1,0:T(8,128)(2,1)} %get-tuple-element.21), calls=%async_computation.1 | async-start | bytes 1048576 | tf_op jit(solution)/shard_map/all_to_all | solution.py:338
  126.1 14.4 %collective-permute-start.3 = (bf16[1024,128]{1,0:T(8,128)(2,1)S(1)}, bf16[1024,128]{1,0:T(8,128)(2,1)S(1)}, u32[]{:S(2)}, u32[]{:S(2)}) collective-permute-start(bf16[1024,128]{1,0:T(8,128)(2,1)S(1)} %get-tuple-element.25.p0_ref), channel_id=1, source_target_pairs={{0,16},{16,32},{32,48},{48,0},{1,17},{17,33},{33,49},{49,1},{2,18}... | collective-permute-start | bytes 786440 | tf_op jit(solution)/shard_map/ppermute | solution.py:343
  126.8 13.7 %collective-permute-start.4 = (bf16[1024,128]{1,0:T(8,128)(2,1)S(1)}, bf16[1024,128]{1,0:T(8,128)(2,1)S(1)}, u32[]{:S(2)}, u32[]{:S(2)}) collective-permute-start(bf16[1024,128]{1,0:T(8,128)(2,1)S(1)} %get-tuple-element.25.p0_ref), channel_id=1, source_target_pairs={{0,48},{16,0},{32,16},{48,32},{1,49},{17,1},{33,17},{49,33},{2,50}... | collective-permute-start | bytes 786440 | tf_op jit(solution)/shard_map/ppermute | solution.py:343
  128.7 11.8 %collective-permute-start.5 = (bf16[1024,128]{1,0:T(8,128)(2,1)S(1)}, bf16[1024,128]{1,0:T(8,128)(2,1)S(1)}, u32[]{:S(2)}, u32[]{:S(2)}) collective-permute-start(bf16[1024,128]{1,0:T(8,128)(2,1)S(1)} %get-tuple-element.25.p0_ref), channel_id=1, source_target_pairs={{0,32},{16,48},{32,0},{48,16},{1,33},{17,49},{33,1},{49,17},{2,34}... | collective-permute-start | bytes 786440 | tf_op jit(solution)/shard_map/ppermute | solution.py:343
  140.5 0.7 copy-start.7
  140.5 0.8 copy-start.8
  140.5 0.9 copy-start.9
  144.3 16.8 %all-to-all-start.4 = ((bf16[32,32,128]{2,1,0:T(8,128)(2,1)}), bf16[32,32,128]{2,1,0:T(8,128)(2,1)S(1)}, u32[]{:S(2)}, u32[]{:S(2)}) async-start(bf16[32,32,128]{2,1,0:T(8,128)(2,1)} %weight_blocks.1), calls=%async_computation.4 | async-start | bytes 524288 | tf_op jit(solution)/shard_map/all_to_all | solution.py:338
  161.1 0.7 copy-start.6
Sparse Core Ops, SparseCore 0:
  11.3 83.7 all-gather.2

commit v4 on v2

v4 whole, which is shorter than its diff:
```python
import functools

import jax
import jax.numpy as jnp
from jax import lax
from jax.experimental import pallas as pl
from jax.experimental.pallas import tpu as pltpu
from jax.sharding import Mesh, PartitionSpec as P

HD = 64
BLOCK = 128
LANES = 128
SCALE = 0.125
CHUNK = 256
NT = (((1,), (1,)), ((), ()))
NN = (((1,), (0,)), ((), ()))
TN = (((0,), (0,)), ((), ()))
HEAD_AXES = ("sec", "y", "core")
SAMPLE_AXES = ("sec", "z", "y", "core")
ALL_AXES = ("sec", "z", "y", "core", "dp")
bf16 = jnp.bfloat16
f32 = jnp.float32


def dot(a, b, dims):
    return lax.dot_general(a, b, dims, preferred_element_type=f32)


def low_half():
    return lax.broadcasted_iota(jnp.int32, (1, LANES), 1) < HD


def swap_halves(a, b):
    lo = low_half()
    return jnp.where(lo, a, pltpu.roll(b, HD, 1)), jnp.where(lo, pltpu.roll(a, HD, 1), b)


def params(mib=48, **kw):
    return pltpu.CompilerParams(vmem_limit_bytes=mib << 20, **kw)


ROWS = 592
KV_ROW = 512
MASK_ROW = 576


def prepare_kernel(z_ref, q_ref, g_ref, hide_ref, m0_ref, m1_ref, m2_ref, m3_ref, wk_ref, wv_ref, out_ref):
    mem = jnp.concatenate([m0_ref[0], m1_ref[0], m2_ref[0], m3_ref[0]], 0)
    keys = dot(mem, wk_ref[...], NN)
    values = dot(mem, wv_ref[...], NN)
    for i in range(2):
        cols = slice(i * LANES, (i + 1) * LANES)
        for k, ref in enumerate((q_ref, g_ref)):
            for t in range(2):
                a = ref[0, t * 256 : t * 256 + 128, cols].astype(f32)
                b = ref[0, t * 256 + 128 : t * 256 + 256, cols].astype(f32)
                even, odd = swap_halves(a, b)
                rows = slice(k * 256 + t * 128, k * 256 + t * 128 + 128)
                out_ref[2 * i, rows, :] = even.astype(bf16)
                out_ref[2 * i + 1, rows, :] = odd.astype(bf16)
        for n, x in enumerate(swap_halves(keys[:, cols], values[:, cols])):
            x = x.astype(bf16)
            for j in range(4):
                at = pl.multiple_of(KV_ROW + lax.rem(z_ref[0] + 4 - j, 4) * 16, 16)
                out_ref[2 * i + n, pl.ds(at, 16), :] = x[j * 16 : j * 16 + 16]
            out_ref[2 * i + n, MASK_ROW : MASK_ROW + 16, :] = hide_ref[...]


def prepare(z, q, g, hide, mems, wk, wv):
    d = wk.shape[0]
    target_spec = pl.BlockSpec((1, 512, 256), lambda p, z: (0, 0, p))
    mem_spec = pl.BlockSpec((1, 16, d), lambda p, z: (0, 0, 0))
    w_spec = pl.BlockSpec((d, 256), lambda p, z: (0, p))
    return pl.pallas_call(
        prepare_kernel,
        grid_spec=pltpu.PrefetchScalarGridSpec(
            num_scalar_prefetch=1,
            grid=(4,),
            in_specs=[target_spec] * 2
            + [pl.BlockSpec((16, LANES), lambda p, z: (0, 0))]
            + [mem_spec] * 4
            + [w_spec] * 2,
            out_specs=pl.BlockSpec((4, ROWS, LANES), lambda p, z: (p, 0, 0)),
        ),
        out_shape=jax.ShapeDtypeStruct((16, ROWS, LANES), bf16),
        compiler_params=params(60),
        cost_estimate=pl.CostEstimate(flops=0, bytes_accessed=16 << 20, transcendentals=0),
        name="prepare",
    )(z, q, g, hide, *mems, wk, wv)


def unpack_kernel(in_ref, out_ref):
    for i in range(2):
        for t in range(2):
            even = in_ref[2 * i, t * 128 : t * 128 + 128, :].astype(f32)
            odd = in_ref[2 * i + 1, t * 128 : t * 128 + 128, :].astype(f32)
            a, b = swap_halves(even, odd)
            cols = slice(i * LANES, (i + 1) * LANES)
            out_ref[0, t * 256 : t * 256 + 128, cols] = a.astype(bf16)
            out_ref[0, t * 256 + 128 : t * 256 + 256, cols] = b.astype(bf16)


def unpack_targets(x):
    return pl.pallas_call(
        unpack_kernel,
        grid=(4,),
        in_specs=[pl.BlockSpec((4, 256, LANES), lambda p: (p, 0, 0))],
        out_specs=pl.BlockSpec((1, 512, 256), lambda p: (0, 0, p)),
        out_shape=jax.ShapeDtypeStruct((1, 512, 1024), bf16),
        compiler_params=params(),
        cost_estimate=pl.CostEstimate(flops=0, bytes_accessed=6 << 20, transcendentals=0),
        name="unpack_targets",
    )(x)


def one_tile(q, g, away, k2_ref, v2_ref, kt_ref, ka_ref, va_ref):
    lo = low_half()
    n = k2_ref.shape[0]
    per = CHUNK // BLOCK
    chunks = n // CHUNK
    rows = [slice(c * CHUNK, c * CHUNK + CHUNK) for c in range(chunks)]
    q = q * jnp.asarray(SCALE, bf16)
    zero = jnp.zeros_like(q)
    q2 = jnp.concatenate([jnp.where(lo, q, zero), jnp.where(lo, zero, q)], 0)
    g2 = jnp.concatenate([jnp.where(lo, g, zero), jnp.where(lo, zero, g)], 0)
    scores = [dot(k2_ref[r, :], q2, NT) for r in rows]
    other = pltpu.roll(away, HD, 1)
    away = (jnp.where(lo, away, other), jnp.where(lo, other, away))
    hidden = []
    top = None
    for j in range(n // BLOCK):
        part = scores[j // per][(j % per) * BLOCK : (j % per + 1) * BLOCK]
        at = j // 2
        hide = jnp.concatenate([away[j % 2][at : at + 1], away[j % 2][4 + at : 5 + at]], 1)
        hidden.append(hide)
        part_top = jnp.max(part, axis=0, keepdims=True) - hide
        top = part_top if top is None else jnp.maximum(top, part_top)
    expd = []
    total = None
    for c in range(chunks):
        parts = [
            jnp.exp(scores[c][i * BLOCK : (i + 1) * BLOCK] - (top + hidden[c * per + i]))
            for i in range(per)
        ]
        e = jnp.concatenate(parts, 0)
        expd.append(e)
        s = jnp.sum(e, axis=0, keepdims=True)
        total = s if total is None else total + s
    inverse = 1.0 / total
    dprobs = []
    delta = None
    for c in range(chunks):
        dp = dot(v2_ref[rows[c], :], g2, NT)
        dprobs.append(dp)
        s = jnp.sum(expd[c] * dp, axis=0, keepdims=True)
        delta = s if delta is None else delta + s
    delta = delta * inverse
    qgt = None
    for c in range(chunks):
        p = expd[c] * inverse
        ds = (p * (dprobs[c] - delta)).astype(bf16)
        va_ref[rows[c], :] += dot(p.astype(bf16), g2, NN)
        ka_ref[rows[c], :] += dot(ds, q2, NN)
        x = dot(kt_ref[:, rows[c]], ds, NN)
        qgt = x if qgt is None else qgt + x
    qgt = qgt * SCALE
    both = jnp.concatenate([qgt[:, :LANES], qgt[:, LANES:]], 0)
    return jnp.transpose(both).astype(bf16)


def attend_kernel(kv_ref, r_ref, qg_ref, kvg_ref, k2_ref, v2_ref, kt_ref, ka_ref, va_ref):
    lo = low_half()
    step = pl.program_id(0)

    @pl.when(step == 0)
    def _():
        order = [(c, z) for c in (0, 8) for z in range(4)]
        kv = jnp.concatenate(
            [kv_ref[c + i, z * 16 : z * 16 + 16, :] for c, z in order for i in range(8)], 0
        ).astype(f32)
        swapped = pltpu.roll(kv, HD, 1)
        k2 = jnp.where(lo, kv, swapped)
        k2_ref[...] = k2.astype(bf16)
        v2_ref[...] = jnp.where(lo, swapped, kv).astype(bf16)
        kt_ref[...] = jnp.transpose(k2)[:HD].astype(bf16)
        ka_ref[...] = jnp.zeros_like(ka_ref)
        va_ref[...] = jnp.zeros_like(va_ref)

    for i in range(r_ref.shape[0]):
        for t in range(2):
            away = r_ref[i, MASK_ROW : MASK_ROW + 16, :].astype(f32)[t * 8 : t * 8 + 8]
            q = r_ref[i, t * 128 : t * 128 + 128, :]
            g = r_ref[i, 256 + t * 128 : 384 + t * 128, :]
            qg_ref[i, t * 128 : t * 128 + 128, :] = one_tile(
                q, g, away, k2_ref, v2_ref, kt_ref, ka_ref, va_ref
            )

    @pl.when(step == pl.num_programs(0) - 1)
    def _():
        ka = ka_ref[...]
        va = va_ref[...]
        ka = ka + pltpu.roll(ka, HD, 1)
        va = va + pltpu.roll(va, HD, 1)
        kvg_ref[...] = jnp.where(lo, ka, va).astype(bf16)


def attend(r):
    sources = r.shape[0]
    n = 64 * sources
    return pl.pallas_call(
        attend_kernel,
        grid=(sources // 2,),
        in_specs=[
            pl.BlockSpec((sources, 64, LANES), lambda i: (0, KV_ROW // 64, 0)),
            pl.BlockSpec((2, ROWS, LANES), lambda i: (i, 0, 0)),
        ],
        out_specs=[
            pl.BlockSpec((2, 256, LANES), lambda i: (i, 0, 0)),
            pl.BlockSpec((n, LANES), lambda i: (0, 0)),
        ],
        scratch_shapes=[
            pltpu.VMEM((n, LANES), bf16),
            pltpu.VMEM((n, LANES), bf16),
            pltpu.VMEM((HD, n), bf16),
            pltpu.VMEM((n, LANES), f32),
            pltpu.VMEM((n, LANES), f32),
        ],
        out_shape=[
            jax.ShapeDtypeStruct((sources, 256, LANES), bf16),
            jax.ShapeDtypeStruct((n, LANES), bf16),
        ],
        compiler_params=params(dimension_semantics=("arbitrary",)),
        cost_estimate=pl.CostEstimate(
            flops=40_000_000_000, bytes_accessed=4 << 20, transcendentals=0
        ),
        name="attend",
    )(r, r)


def spread_kernel(z_ref, m0_ref, m1_ref, m2_ref, m3_ref, out_ref):
    mem = jnp.concatenate([m0_ref[0], m1_ref[0], m2_ref[0], m3_ref[0]], 0)
    for i in range(16):
        out_ref[i] = mem


def spread(z, mems):
    return pl.pallas_call(
        spread_kernel,
        grid_spec=pltpu.PrefetchScalarGridSpec(
            num_scalar_prefetch=1,
            grid=(2,),
            in_specs=[pl.BlockSpec((1, 16, 256), lambda s, z: (0, 0, s * 4 + z[0]))] * 4,
            out_specs=pl.BlockSpec((16, 64, 256), lambda s, z: (0, 0, s)),
        ),
        out_shape=jax.ShapeDtypeStruct((16, 64, 512), bf16),
        compiler_params=params(),
        cost_estimate=pl.CostEstimate(flops=0, bytes_accessed=1 << 20, transcendentals=0),
        name="spread",
    )(z, *mems)


def weight_kernel(z_ref, p0_ref, p1_ref, p2_ref, p3_ref, mem_ref, out_ref, total_ref, moved_ref):
    step = pl.program_id(0)

    @pl.when(step == 0)
    def _():
        total = p0_ref[...].astype(f32) + p1_ref[...].astype(f32)
        total = total + (p2_ref[...].astype(f32) + p3_ref[...].astype(f32))
        total_ref[...] = total.astype(bf16)
        for i in range(16):
            for j in range(4):
                at = (i // 8) * 512 + lax.rem(z_ref[0] + 4 - j, 4) * 128 + (i % 8) * 16
                rows = slice(i * 64 + j * 16, i * 64 + j * 16 + 16)
                moved_ref[rows, :] = total_ref[pl.ds(pl.multiple_of(at, 16), 16), :]

    grad = dot(mem_ref[...], moved_ref[...], TN).astype(bf16)
    at = pl.multiple_of(step * 512 + z_ref[0] * 128, 128)
    tokens = total_ref[pl.ds(at, 128), :]
    for i in range(16):
        out_ref[i, 0:16, :] = grad[i * 16 : i * 16 + 16]
        out_ref[i, 16:32, :] = tokens[(i // 2) * 16 : (i // 2) * 16 + 16]


def weight_blocks(z, parts, mem):
    n = mem.shape[0]
    part_spec = pl.BlockSpec((n, LANES), lambda s, z: (0, 0))
    return pl.pallas_call(
        weight_kernel,
        grid_spec=pltpu.PrefetchScalarGridSpec(
            num_scalar_prefetch=1,
            grid=(2,),
            in_specs=[part_spec] * 4 + [pl.BlockSpec((n, 256), lambda s, z: (0, s))],
            out_specs=pl.BlockSpec((16, 32, LANES), lambda s, z: (s, 0, 0)),
            scratch_shapes=[pltpu.VMEM((n, LANES), bf16), pltpu.VMEM((n, LANES), bf16)],
        ),
        out_shape=jax.ShapeDtypeStruct((32, 32, LANES), bf16),
        compiler_params=params(dimension_semantics=("arbitrary",)),
        cost_estimate=pl.CostEstimate(flops=0, bytes_accessed=6 << 20, transcendentals=0),
        name="weight_blocks",
    )(z, *parts, mem)


def finish_kernel(dp_ref, in_ref, wk_ref, wv_ref, mg_ref, wkg_ref, wvg_ref, acc_ref):
    p = pl.program_id(0)
    grads = []
    for i in range(4):
        cols = slice(i * LANES, (i + 1) * LANES)
        rows = [in_ref[4 * i + j, 0:16, :].astype(f32) for j in range(4)]
        wkg_ref[:, cols], wvg_ref[:, cols] = swap_halves(rows[0] + rows[1], rows[2] + rows[3])
        even = in_ref[pl.ds(4 * i + dp_ref[0], 1), 16:32, :][0].astype(f32)
        odd = in_ref[pl.ds(4 * i + 2 + dp_ref[0], 1), 16:32, :][0].astype(f32)
        grads.append(swap_halves(even, odd))
    kg = jnp.concatenate([x[0] for x in grads], 1).astype(bf16)
    vg = jnp.concatenate([x[1] for x in grads], 1).astype(bf16)
    part = dot(kg, wk_ref[...], NT) + dot(vg, wv_ref[...], NT)

    @pl.when(p == 0)
    def _():
        acc_ref[...] = part

    @pl.when(p > 0)
    def _():
        acc_ref[...] += part

    @pl.when(p == pl.num_programs(0) - 1)
    def _():
        mg_ref[0] = acc_ref[...].astype(bf16)


def finish(dp, x, wk, wv):
    d = wk.shape[0]
    w_spec = pl.BlockSpec((d, 512), lambda p, dp: (0, p))
    out_spec = pl.BlockSpec((16, 512), lambda p, dp: (0, p))
    shape = jax.ShapeDtypeStruct((16, wk.shape[1]), f32)
    return pl.pallas_call(
        finish_kernel,
        grid_spec=pltpu.PrefetchScalarGridSpec(
            num_scalar_prefetch=1,
            grid=(2,),
            in_specs=[pl.BlockSpec((16, 32, LANES), lambda p, dp: (p, 0, 0)), w_spec, w_spec],
            out_specs=[pl.BlockSpec((1, 16, d), lambda p, dp: (0, 0, 0)), out_spec, out_spec],
            scratch_shapes=[pltpu.VMEM((16, d), f32)],
        ),
        out_shape=[jax.ShapeDtypeStruct((1, 16, d), bf16), shape, shape],
        compiler_params=params(60, dimension_semantics=("arbitrary",)),
        cost_estimate=pl.CostEstimate(flops=0, bytes_accessed=12 << 20, transcendentals=0),
        name="finish",
    )(dp, x, wk, wv)


def exchange(x, axes):
    return lax.all_to_all(x, axes, 0, 0, tiled=True)


def shifted(x, axis, k):
    n = lax.axis_size(axis)
    return lax.ppermute(x, axis, [(i, (i + k) % n) for i in range(n)])


def body(q, g, mem, wk, wv, target_modality, memory_modality, allow_pairs):
    z = lax.axis_index("z").reshape(1)
    dp = lax.axis_index("dp").reshape(1)
    mems = [mem] + [shifted(mem, "z", k) for k in (1, 2, 3)]

    labels = jnp.arange(allow_pairs.shape[0], dtype=jnp.int32)
    q_onehot = (target_modality[0][:, None] == labels[None, :]).astype(f32)
    k_onehot = (memory_modality[0][:, None] == labels[None, :]).astype(f32)
    allowed = jnp.dot(jnp.dot(q_onehot, allow_pairs.astype(f32)), k_onehot.T) > 0.5
    allowed = allowed | (jnp.arange(allowed.shape[1], dtype=jnp.int32) == 0)[None, :]
    hide = jnp.where(allowed, 0.0, 1e30).astype(bf16).reshape(16, 2, 1)
    hide = jnp.broadcast_to(hide, (16, 2, HD)).reshape(16, LANES)

    payload = prepare(z, q, g, hide, mems, wk, wv)
    payload, mems = lax.optimization_barrier((payload, mems))
    columns = spread(z, mems)
    targets = exchange(payload, HEAD_AXES)
    columns, targets = lax.optimization_barrier((columns, targets))
    memory = exchange(columns, HEAD_AXES).reshape(1024, 512)

    q_grad, part = attend(targets)
    part, memory = lax.optimization_barrier((part, memory))
    q_grad = exchange(q_grad, HEAD_AXES)
    parts = [part] + [shifted(part, "z", k) for k in (1, 3, 2)]
    blocks = weight_blocks(z, parts, memory)
    blocks, q_grad = lax.optimization_barrier((blocks, q_grad))
    blocks = exchange(blocks, ("sec", "y", "core", "dp"))
    m_grad, wk_grad, wv_grad = finish(dp, blocks, wk, wv)
    return unpack_targets(q_grad), m_grad, wk_grad, wv_grad


def solution(mesh):
    fine = Mesh(mesh.devices.reshape(2, 4, 4, 2, 2), ALL_AXES)
    rows = P("dp", SAMPLE_AXES, None)
    in_specs = (rows, rows, rows, P(), P(), P("dp", SAMPLE_AXES), P("dp", None), P())
    out_specs = (rows, rows, P(ALL_AXES, None), P(ALL_AXES, None))
    return jax.shard_map(body, mesh=fine, in_specs=in_specs, out_specs=out_specs, check_vma=False)
```

time: 159 us -> 152 us (0.956)
  blocking collectives: 42.5 us -> 0 us
  waiting for transfers between devices: 19.2 us -> 53.4 us
  starting transfers between devices: 22.1 us -> 40.3 us
  between operations: 14.1 us -> 0.73 us
  Pallas kernels: 54.2 us -> 51.2 us
    all_to_all x1 -> x0, blocking collectives: 42.5 us -> none  [exchange(): return lax.all_to_all(x, axes, 0, 0, tiled=True)]
    all_to_all x2 -> x4, waiting for transfers between devices: 6.75 us -> 37.9 us  [exchange(): return lax.all_to_all(x, axes, 0, 0, tiled=True)]
    all_to_all x2 -> x4, starting transfers between devices: 12.8 us -> 32.1 us  [exchange(): return lax.all_to_all(x, axes, 0, 0, tiled=True)]
    ppermute x6, waiting for transfers between devices: 11.8 us -> 15.4 us  [shifted(): return lax.ppermute(x, axis, [(i, (i + k) % n) for i in range(n)])]
    pallas_call x3, Pallas kernels: 43.9 us -> 42.1 us  [the longest x1 33.9 us: attend(): pl.pallas_call(attend_kernel, grid=(sources // 2,), in_specs=[pl.BlockSpe...]
    unnamed x16 -> x22, local copies, waits for them, and re-layouts: 5.49 us -> 3.97 us
  transfers between devices with their start and end apart: 9 -> 10, of which waited for: 2 -> 7; matrix products, arithmetic and copies ran while one was open for 1% -> 1% of each run, Pallas kernels for 31% -> 26%
where the time goes in v4:
time: 152 us; the launch traced here: 151 us
  waiting for transfers between devices  53.4 us (35%)
  Pallas kernels  51.2 us (34%)
  starting transfers between devices  40.3 us (27%)
  local copies, waits for them, and re-layouts  4.82 us (3%)
    all_to_all x4, waiting for transfers between devices, exchange(): return lax.all_to_all(x, axes, 0, 0, tiled=True)  37.9 us
    pallas_call x1, Pallas kernels, attend(): pl.pallas_call(attend_kernel, grid=(sources // 2,), in_specs=[pl.BlockSpe...  33.9 us
    all_to_all x4, starting transfers between devices, exchange(): return lax.all_to_all(x, axes, 0, 0, tiled=True)  32.1 us
    ppermute x6, waiting for transfers between devices, shifted(): return lax.ppermute(x, axis, [(i, (i + k) % n) for i in range(n)])  15.4 us
    ppermute x6, starting transfers between devices, shifted(): return lax.ppermute(x, axis, [(i, (i + k) % n) for i in range(n)])  8.15 us
    pallas_call x1, Pallas kernels, prepare(): pl.pallas_call(prepare_kernel, grid_spec=pltpu.PrefetchScalarGridSpec(num...  7.08 us
    pallas_call x1, Pallas kernels, finish(): pl.pallas_call(finish_kernel, grid_spec=pltpu.PrefetchScalarGridSpec(num_...  5.49 us
    unnamed x22, local copies, waits for them, and re-layouts  3.97 us
  transfers between devices with their start and end apart: 10, of which 7 were waited for; matrix products, arithmetic and copies ran while one was open for 1% of the time, Pallas kernels for 26%

profile of v4, /device:TPU:1, one launch (start us, length us, event | category | flops | bytes accessed | tf_op | source)
XLA Modules:
  0.0 151.4 jit_solution(7804060700804701348)
XLA Ops:
  0.6 4.7 %collective-permute-start.2 = (bf16[1,16,2048]{2,1,0:T(8,128)(2,1)}, bf16[1,16,2048]{2,1,0:T(8,128)(2,1)S(1)}, u32[]{:S(2)}, u32[]{:S(2)}) collective-permute-start(bf16[1,16,2048]{2,1,0:T(8,128)(2,1)} %m0_ref.2), channel_id=1, source_target_pairs={{0,48},{16,0},{32,16},{48,32},{1,49},{17,1},{33,17},{49,33},{2,50}... | collective-permute-start | bytes 196616 | tf_op jit(solution)/shard_map/ppermute | solution.py:357
  5.3 0.7 collective-permute-start
  6.0 1.0 fusion.12
  7.0 0.1 broadcast_in_dim.20
  7.1 0.1 broadcast_in_dim.21
  7.2 0.7 reshape.29.hide_ref
  7.9 2.4 %collective-permute-done.1.m2_ref = bf16[1,16,2048]{2,1,0:T(8,128)(2,1)S(1)} collective-permute-done((bf16[1,16,2048]{2,1,0:T(8,128)(2,1)}, bf16[1,16,2048]{2,1,0:T(8,128)(2,1)S(1)}, u32[]{:S(2)}, u32[]{:S(2)}) %collective-permute-start.1) | collective-permute-done | bytes 65568 | tf_op jit(solution)/shard_map/ppermute | solution.py:357
  10.2 0.3 collective-permute-done.m1_ref
  10.5 0.3 copy-done.4
  10.9 0.3 copy-done.6
  11.2 7.1 %prepare.1 = bf16[16,592,128]{2,1,0:T(8,128)(2,1)} custom-call(s32[1]{0:T(128)} %bitcast.z_ref, bf16[1,512,1024]{2,1,0:T(8,128)(2,1)} %q_ref.1, bf16[1,512,1024]{2,1,0:T(8,128)(2,1)} %g_ref.1, bf16[16,128]{1,0:T(8,128)(2,1)} %reshape.29.hide_ref, bf16[1,16,2048]{2,1,0:T(8,128)(2,1)} %m0_ref.2, bf16[1,16,2048]{2,1,0:T(8,128)(2,1)} %copy-done.6, ...), custom_call_target="tpu_custom_call" | custom-call | bytes 16777216 | tf_op jit(solution)/shard_map/prepare/pallas_call | solution.py:74
  18.3 9.2 %all-to-all-start = ((bf16[16,592,128]{2,1,0:T(8,128)(2,1)}), bf16[16,592,128]{2,1,0:T(8,128)(2,1)S(1)}, u32[]{:S(2)}, u32[]{:S(2)}) async-start(bf16[16,592,128]{2,1,0:T(8,128)(2,1)} %prepare.1), calls=%async_computation | async-start | bytes 4849664 | tf_op jit(solution)/shard_map/all_to_all | solution.py:352
  27.5 1.2 spread.1
  28.7 31.2 %all-to-all-done.kv_ref.r_ref = bf16[16,592,128]{2,1,0:T(8,128)(2,1)S(1)} async-done(((bf16[16,592,128]{2,1,0:T(8,128)(2,1)}), bf16[16,592,128]{2,1,0:T(8,128)(2,1)S(1)}, u32[]{:S(2)}, u32[]{:S(2)}) %all-to-all-start) | async-done | bytes 2424864 | tf_op jit(solution)/shard_map/all_to_all | solution.py:352
  59.9 8.2 %all-to-all-start.1 = ((bf16[16,64,512]{2,1,0:T(8,128)(2,1)}), bf16[16,64,512]{2,1,0:T(8,128)(2,1)S(1)}, u32[]{:S(2)}, u32[]{:S(2)}) async-start(bf16[16,64,512]{2,1,0:T(8,128)(2,1)} %spread.1), calls=%async_computation.1 | async-start | bytes 2097152 | tf_op jit(solution)/shard_map/all_to_all | solution.py:352
  68.1 33.9 %attend.1 = (bf16[16,256,128]{2,1,0:T(8,128)(2,1)S(1)}, bf16[1024,128]{1,0:T(8,128)(2,1)S(1)}) custom-call(bf16[16,592,128]{2,1,0:T(8,128)(2,1)S(1)} %all-to-all-done.kv_ref.r_ref, bf16[16,592,128]{2,1,0:T(8,128)(2,1)S(1)} %all-to-all-done.kv_ref.r_ref), custom_call_target="tpu_custom_call" | custom-call | flops 40000000000 | bytes 4194304 | tf_op jit(solution)/shard_map/attend/pallas_call | solution.py:210
  102.0 1.0 copy-done
  103.0 0.7 copy-done.8
  103.7 7.2 %all-to-all-start.2 = ((bf16[16,256,128]{2,1,0:T(8,128)(2,1)}), bf16[16,256,128]{2,1,0:T(8,128)(2,1)S(1)}, u32[]{:S(2)}, u32[]{:S(2)}) async-start(bf16[16,256,128]{2,1,0:T(8,128)(2,1)} %copy-done), calls=%async_computation.2 | async-start | bytes 2097152 | tf_op jit(solution)/shard_map/all_to_all | solution.py:352
  110.9 1.3 collective-permute-start.5
  112.2 0.1 collective-permute-start.4
  112.4 1.3 collective-permute-start.3
  113.7 6.7 %collective-permute-done.5.p3_ref = bf16[1024,128]{1,0:T(8,128)(2,1)S(1)} collective-permute-done((bf16[1024,128]{1,0:T(8,128)(2,1)}, bf16[1024,128]{1,0:T(8,128)(2,1)S(1)}, u32[]{:S(2)}, u32[]{:S(2)}) %collective-permute-start.5) | collective-permute-done | bytes 262176 | tf_op jit(solution)/shard_map/ppermute | solution.py:357
  120.4 3.8 %collective-permute-done.4.p2_ref = bf16[1024,128]{1,0:T(8,128)(2,1)S(1)} collective-permute-done((bf16[1024,128]{1,0:T(8,128)(2,1)}, bf16[1024,128]{1,0:T(8,128)(2,1)S(1)}, u32[]{:S(2)}, u32[]{:S(2)}) %collective-permute-start.4) | collective-permute-done | bytes 262176 | tf_op jit(solution)/shard_map/ppermute | solution.py:357
  124.2 2.3 %collective-permute-done.3.p1_ref = bf16[1024,128]{1,0:T(8,128)(2,1)S(1)} collective-permute-done((bf16[1024,128]{1,0:T(8,128)(2,1)}, bf16[1024,128]{1,0:T(8,128)(2,1)S(1)}, u32[]{:S(2)}, u32[]{:S(2)}) %collective-permute-start.3) | collective-permute-done | bytes 262176 | tf_op jit(solution)/shard_map/ppermute | solution.py:357
  126.4 0.9 copy-done.9
  127.4 1.7 %weight_blocks.1 = bf16[32,32,128]{2,1,0:T(8,128)(2,1)} custom-call(s32[1]{0:T(128)} %bitcast.z_ref, bf16[1024,128]{1,0:T(8,128)(2,1)S(1)} %copy-done.9, bf16[1024,128]{1,0:T(8,128)(2,1)S(1)} %collective-permute-done.3.p1_ref, bf16[1024,128]{1,0:T(8,128)(2,1)S(1)} %collective-permute-done.4.p2_ref, bf16[1024,128]{1,0:T(8,128)(2,1)S(1)} %collective-permute-done.5.p3_ref, ...), custom_call_target="tpu_custom_call" | custom-call | bytes 6291456 | tf_op jit(solution)/shard_map/weight_blocks/pallas_call | solution.py:287
  129.1 7.5 %all-to-all-start.3 = ((bf16[32,32,128]{2,1,0:T(8,128)(2,1)}), bf16[32,32,128]{2,1,0:T(8,128)(2,1)S(1)}, u32[]{:S(2)}, u32[]{:S(2)}) async-start(bf16[32,32,128]{2,1,0:T(8,128)(2,1)} %weight_blocks.1), calls=%async_computation.3 | async-start | bytes 524288 | tf_op jit(solution)/shard_map/all_to_all | solution.py:352
  136.6 1.9 %unpack_targets.1 = bf16[1,512,1024]{2,1,0:T(8,128)(2,1)} custom-call(bf16[16,256,128]{2,1,0:T(8,128)(2,1)S(1)} %all-to-all-done.2.in_ref), custom_call_target="tpu_custom_call" | custom-call | bytes 6291456 | tf_op jit(solution)/shard_map/unpack_targets/pallas_call | solution.py:104
  138.5 6.7 %all-to-all-done.3.in_ref = bf16[32,32,128]{2,1,0:T(8,128)(2,1)S(1)} async-done(((bf16[32,32,128]{2,1,0:T(8,128)(2,1)}), bf16[32,32,128]{2,1,0:T(8,128)(2,1)S(1)}, u32[]{:S(2)}, u32[]{:S(2)}) %all-to-all-start.3) | async-done | bytes 262176 | tf_op jit(solution)/shard_map/all_to_all | solution.py:352
  145.3 0.7 copy-done.10
  146.0 5.5 %finish.1 = (bf16[1,16,2048]{2,1,0:T(8,128)(2,1)}, f32[16,1024]{1,0:T(8,128)}, f32[16,1024]{1,0:T(8,128)}) custom-call(s32[1]{0:T(128)} %bitcast.4.dp_ref, bf16[32,32,128]{2,1,0:T(8,128)(2,1)} %copy-done.10, bf16[2048,1024]{1,0:T(8,128)(2,1)} %wk_ref.3, bf16[2048,1024]{1,0:T(8,128)(2,1)} %wv_ref.3), custom_call_target="tpu_custom_call" | custom-call | bytes 12582912 | tf_op jit(solution)/shard_map/finish/pallas_call | solution.py:335
  (21 shorter events, 0.1 us)
Async XLA Ops:
  0.6 7.2 %collective-permute-start.2 = (bf16[1,16,2048]{2,1,0:T(8,128)(2,1)}, bf16[1,16,2048]{2,1,0:T(8,128)(2,1)S(1)}, u32[]{:S(2)}, u32[]{:S(2)}) collective-permute-start(bf16[1,16,2048]{2,1,0:T(8,128)(2,1)} %m0_ref.2), channel_id=1, source_target_pairs={{0,48},{16,0},{32,16},{48,32},{1,49},{17,1},{33,17},{49,33},{2,50}... | collective-permute-start | bytes 196616 | tf_op jit(solution)/shard_map/ppermute | solution.py:357
  5.3 4.9 %collective-permute-start.1 = (bf16[1,16,2048]{2,1,0:T(8,128)(2,1)}, bf16[1,16,2048]{2,1,0:T(8,128)(2,1)S(1)}, u32[]{:S(2)}, u32[]{:S(2)}) collective-permute-start(bf16[1,16,2048]{2,1,0:T(8,128)(2,1)} %m0_ref.2), channel_id=1, source_target_pairs={{0,32},{16,48},{32,0},{48,16},{1,33},{17,49},{33,1},{49,17},{2,34}... | collective-permute-start | bytes 196616 | tf_op jit(solution)/shard_map/ppermute | solution.py:357
  5.3 5.2 %collective-permute-start = (bf16[1,16,2048]{2,1,0:T(8,128)(2,1)}, bf16[1,16,2048]{2,1,0:T(8,128)(2,1)S(1)}, u32[]{:S(2)}, u32[]{:S(2)}) collective-permute-start(bf16[1,16,2048]{2,1,0:T(8,128)(2,1)} %m0_ref.2), channel_id=1, source_target_pairs={{0,16},{16,32},{32,48},{48,0},{1,17},{17,33},{33,49},{49,1},{2,18}... | collective-permute-start | bytes 196616 | tf_op jit(solution)/shard_map/ppermute | solution.py:357
  7.9 2.7 %copy-start.2 = (bf16[1,16,2048]{2,1,0:T(8,128)(2,1)}, bf16[1,16,2048]{2,1,0:T(8,128)(2,1)S(1)}, u32[]{:S(2)}) copy-start(bf16[1,16,2048]{2,1,0:T(8,128)(2,1)S(1)} %collective-permute-done.2.m3_ref) | copy-start | bytes 196612
  10.2 0.6 copy-start.4
  10.5 0.6 copy-start.6
  18.2 9.2 %copy-start.1 = (bf16[1,16,2048]{2,1,0:T(8,128)(2,1)S(1)}, bf16[1,16,2048]{2,1,0:T(8,128)(2,1)}, u32[]{:S(2)}) copy-start(bf16[1,16,2048]{2,1,0:T(8,128)(2,1)} %m0_ref.2) | copy-start | bytes 196612
  18.2 9.2 %copy-start.3 = (bf16[1,16,2048]{2,1,0:T(8,128)(2,1)S(1)}, bf16[1,16,2048]{2,1,0:T(8,128)(2,1)}, u32[]{:S(2)}) copy-start(bf16[1,16,2048]{2,1,0:T(8,128)(2,1)} %copy-done.2) | copy-start | bytes 196612
  18.2 9.2 %copy-start.5 = (bf16[1,16,2048]{2,1,0:T(8,128)(2,1)S(1)}, bf16[1,16,2048]{2,1,0:T(8,128)(2,1)}, u32[]{:S(2)}) copy-start(bf16[1,16,2048]{2,1,0:T(8,128)(2,1)} %copy-done.4) | copy-start | bytes 196612
  18.3 9.2 %copy-start.7 = (bf16[1,16,2048]{2,1,0:T(8,128)(2,1)S(1)}, bf16[1,16,2048]{2,1,0:T(8,128)(2,1)}, u32[]{:S(2)}) copy-start(bf16[1,16,2048]{2,1,0:T(8,128)(2,1)} %copy-done.6) | copy-start | bytes 196612
  18.3 41.6 %all-to-all-start = ((bf16[16,592,128]{2,1,0:T(8,128)(2,1)}), bf16[16,592,128]{2,1,0:T(8,128)(2,1)S(1)}, u32[]{:S(2)}, u32[]{:S(2)}) async-start(bf16[16,592,128]{2,1,0:T(8,128)(2,1)} %prepare.1), calls=%async_computation | async-start | bytes 4849664 | tf_op jit(solution)/shard_map/all_to_all | solution.py:352
  59.9 43.8 %all-to-all-start.1 = ((bf16[16,64,512]{2,1,0:T(8,128)(2,1)}), bf16[16,64,512]{2,1,0:T(8,128)(2,1)S(1)}, u32[]{:S(2)}, u32[]{:S(2)}) async-start(bf16[16,64,512]{2,1,0:T(8,128)(2,1)} %spread.1), calls=%async_computation.1 | async-start | bytes 2097152 | tf_op jit(solution)/shard_map/all_to_all | solution.py:352
  102.0 1.0 copy-start
  103.0 0.7 copy-start.8
  103.7 25.5 %all-to-all-start.2 = ((bf16[16,256,128]{2,1,0:T(8,128)(2,1)}), bf16[16,256,128]{2,1,0:T(8,128)(2,1)S(1)}, u32[]{:S(2)}, u32[]{:S(2)}) async-start(bf16[16,256,128]{2,1,0:T(8,128)(2,1)} %copy-done), calls=%async_computation.2 | async-start | bytes 2097152 | tf_op jit(solution)/shard_map/all_to_all | solution.py:352
  110.9 9.5 %collective-permute-start.5 = (bf16[1024,128]{1,0:T(8,128)(2,1)}, bf16[1024,128]{1,0:T(8,128)(2,1)S(1)}, u32[]{:S(2)}, u32[]{:S(2)}) collective-permute-start(bf16[1024,128]{1,0:T(8,128)(2,1)} %copy-done.8), channel_id=1, source_target_pairs={{0,32},{16,48},{32,0},{48,16},{1,33},{17,49},{33,1},{49,17},{2,34}... | collective-permute-start | bytes 786440 | tf_op jit(solution)/shard_map/ppermute | solution.py:357
  112.2 12.0 %collective-permute-start.4 = (bf16[1024,128]{1,0:T(8,128)(2,1)}, bf16[1024,128]{1,0:T(8,128)(2,1)S(1)}, u32[]{:S(2)}, u32[]{:S(2)}) collective-permute-start(bf16[1024,128]{1,0:T(8,128)(2,1)} %copy-done.8), channel_id=1, source_target_pairs={{0,48},{16,0},{32,16},{48,32},{1,49},{17,1},{33,17},{49,33},{2,50}... | collective-permute-start | bytes 786440 | tf_op jit(solution)/shard_map/ppermute | solution.py:357
  112.4 14.1 %collective-permute-start.3 = (bf16[1024,128]{1,0:T(8,128)(2,1)}, bf16[1024,128]{1,0:T(8,128)(2,1)S(1)}, u32[]{:S(2)}, u32[]{:S(2)}) collective-permute-start(bf16[1024,128]{1,0:T(8,128)(2,1)} %copy-done.8), channel_id=1, source_target_pairs={{0,16},{16,32},{32,48},{48,0},{1,17},{17,33},{33,49},{49,1},{2,18}... | collective-permute-start | bytes 786440 | tf_op jit(solution)/shard_map/ppermute | solution.py:357
  126.4 1.0 copy-start.9
  129.1 16.1 %all-to-all-start.3 = ((bf16[32,32,128]{2,1,0:T(8,128)(2,1)}), bf16[32,32,128]{2,1,0:T(8,128)(2,1)S(1)}, u32[]{:S(2)}, u32[]{:S(2)}) async-start(bf16[32,32,128]{2,1,0:T(8,128)(2,1)} %weight_blocks.1), calls=%async_computation.3 | async-start | bytes 524288 | tf_op jit(solution)/shard_map/all_to_all | solution.py:352
  145.3 0.7 copy-start.10

commit v5 on v4

--- a/solution.py
+++ b/solution.py
@@ -15,7 +15,8 @@
 NT = (((1,), (1,)), ((), ()))
 NN = (((1,), (0,)), ((), ()))
 TN = (((0,), (0,)), ((), ()))
-HEAD_AXES = ("sec", "y", "core")
+HEAD_AXES = ("z", "y")
+SUM_AXES = ("sec", "core")
 SAMPLE_AXES = ("sec", "z", "y", "core")
 ALL_AXES = ("sec", "z", "y", "core", "dp")
 bf16 = jnp.bfloat16
@@ -39,54 +40,54 @@
     return pltpu.CompilerParams(vmem_limit_bytes=mib << 20, **kw)
 
 
-ROWS = 592
-KV_ROW = 512
-MASK_ROW = 576
-
-
-def prepare_kernel(z_ref, q_ref, g_ref, hide_ref, m0_ref, m1_ref, m2_ref, m3_ref, wk_ref, wv_ref, out_ref):
+ROWS = (336, 272)
+KV_ROW = 256
+STEP = 4
+
+
+def prepare_kernel(me_ref, q_ref, g_ref, hide_ref, m0_ref, m1_ref, m2_ref, m3_ref, wk_ref, wv_ref, *out_refs):
     mem = jnp.concatenate([m0_ref[0], m1_ref[0], m2_ref[0], m3_ref[0]], 0)
     keys = dot(mem, wk_ref[...], NN)
     values = dot(mem, wv_ref[...], NN)
     for i in range(2):
         cols = slice(i * LANES, (i + 1) * LANES)
-        for k, ref in enumerate((q_ref, g_ref)):
-            for t in range(2):
+        for t, out_ref in enumerate(out_refs):
+            for k, ref in enumerate((q_ref, g_ref)):
                 a = ref[0, t * 256 : t * 256 + 128, cols].astype(f32)
                 b = ref[0, t * 256 + 128 : t * 256 + 256, cols].astype(f32)
                 even, odd = swap_halves(a, b)
-                rows = slice(k * 256 + t * 128, k * 256 + t * 128 + 128)
-                out_ref[2 * i, rows, :] = even.astype(bf16)
-                out_ref[2 * i + 1, rows, :] = odd.astype(bf16)
+                out_ref[2 * i, k * 128 : k * 128 + 128, :] = even.astype(bf16)
+                out_ref[2 * i + 1, k * 128 : k * 128 + 128, :] = odd.astype(bf16)
+            for n in range(2):
+                out_ref[2 * i + n, ROWS[t] - 16 : ROWS[t], :] = hide_ref[...]
         for n, x in enumerate(swap_halves(keys[:, cols], values[:, cols])):
             x = x.astype(bf16)
             for j in range(4):
-                at = pl.multiple_of(KV_ROW + lax.rem(z_ref[0] + 4 - j, 4) * 16, 16)
-                out_ref[2 * i + n, pl.ds(at, 16), :] = x[j * 16 : j * 16 + 16]
-            out_ref[2 * i + n, MASK_ROW : MASK_ROW + 16, :] = hide_ref[...]
-
-
-def prepare(z, q, g, hide, mems, wk, wv):
+                at = pl.multiple_of(KV_ROW + (me_ref[0] ^ j) * 16, 16)
+                out_refs[0][2 * i + n, pl.ds(at, 16), :] = x[j * 16 : j * 16 + 16]
+
+
+def prepare(me, q, g, hide, mems, wk, wv):
     d = wk.shape[0]
-    target_spec = pl.BlockSpec((1, 512, 256), lambda p, z: (0, 0, p))
-    mem_spec = pl.BlockSpec((1, 16, d), lambda p, z: (0, 0, 0))
-    w_spec = pl.BlockSpec((d, 256), lambda p, z: (0, p))
+    target_spec = pl.BlockSpec((1, 512, 256), lambda p, me: (0, 0, p))
+    mem_spec = pl.BlockSpec((1, 16, d), lambda p, me: (0, 0, 0))
+    w_spec = pl.BlockSpec((d, 256), lambda p, me: (0, p))
     return pl.pallas_call(
         prepare_kernel,
         grid_spec=pltpu.PrefetchScalarGridSpec(
             num_scalar_prefetch=1,
             grid=(4,),
             in_specs=[target_spec] * 2
-            + [pl.BlockSpec((16, LANES), lambda p, z: (0, 0))]
+            + [pl.BlockSpec((16, LANES), lambda p, me: (0, 0))]
             + [mem_spec] * 4
             + [w_spec] * 2,
-            out_specs=pl.BlockSpec((4, ROWS, LANES), lambda p, z: (p, 0, 0)),
+            out_specs=[pl.BlockSpec((4, rows, LANES), lambda p, me: (p, 0, 0)) for rows in ROWS],
         ),
-        out_shape=jax.ShapeDtypeStruct((16, ROWS, LANES), bf16),
+        out_shape=[jax.ShapeDtypeStruct((16, rows, LANES), bf16) for rows in ROWS],
         compiler_params=params(60),
         cost_estimate=pl.CostEstimate(flops=0, bytes_accessed=16 << 20, transcendentals=0),
         name="prepare",
-    )(z, q, g, hide, *mems, wk, wv)
+    )(me, q, g, hide, *mems, wk, wv)
 
 
 def unpack_kernel(in_ref, out_ref):
@@ -168,16 +169,17 @@
     return jnp.transpose(both).astype(bf16)
 
 
-def attend_kernel(kv_ref, r_ref, qg_ref, kvg_ref, k2_ref, v2_ref, kt_ref, ka_ref, va_ref):
+def attend_kernel(*refs, half):
+    if half == 0:
+        kv_ref, r_ref, qg_ref, kvg_ref, k2_ref, v2_ref, kt_ref, ka_ref, va_ref = refs
+    else:
+        kv_ref, r_ref, before_ref, _, qg_ref, kvg_ref, k2_ref, v2_ref, kt_ref, ka_ref, va_ref = refs
     lo = low_half()
-    step = pl.program_id(0)
-
-    @pl.when(step == 0)
-    def _():
-        order = [(c, z) for c in (0, 8) for z in range(4)]
-        kv = jnp.concatenate(
-            [kv_ref[c + i, z * 16 : z * 16 + 16, :] for c, z in order for i in range(8)], 0
-        ).astype(f32)
+
+    @pl.when(pl.program_id(0) == 0)
+    def _():
+        order = [(i, j * 32) for j in range(2) for i in range(16)]
+        kv = jnp.concatenate([kv_ref[i, at : at + 32, :] for i, at in order], 0).astype(f32)
         swapped = pltpu.roll(kv, HD, 1)
         k2 = jnp.where(lo, kv, swapped)
         k2_ref[...] = k2.astype(bf16)
@@ -186,38 +188,37 @@
         ka_ref[...] = jnp.zeros_like(ka_ref)
         va_ref[...] = jnp.zeros_like(va_ref)
 
-    for i in range(r_ref.shape[0]):
-        for t in range(2):
-            away = r_ref[i, MASK_ROW : MASK_ROW + 16, :].astype(f32)[t * 8 : t * 8 + 8]
-            q = r_ref[i, t * 128 : t * 128 + 128, :]
-            g = r_ref[i, 256 + t * 128 : 384 + t * 128, :]
-            qg_ref[i, t * 128 : t * 128 + 128, :] = one_tile(
-                q, g, away, k2_ref, v2_ref, kt_ref, ka_ref, va_ref
-            )
-
-    @pl.when(step == pl.num_programs(0) - 1)
+    for i in range(STEP):
+        away = r_ref[i, ROWS[half] - 16 : ROWS[half], :].astype(f32)[half * 8 : half * 8 + 8]
+        q = r_ref[i, 0:128, :]
+        g = r_ref[i, 128:256, :]
+        qg_ref[i] = one_tile(q, g, away, k2_ref, v2_ref, kt_ref, ka_ref, va_ref)
+
+    @pl.when(pl.program_id(0) == pl.num_programs(0) - 1)
     def _():
         ka = ka_ref[...]
         va = va_ref[...]
         ka = ka + pltpu.roll(ka, HD, 1)
         va = va + pltpu.roll(va, HD, 1)
-        kvg_ref[...] = jnp.where(lo, ka, va).astype(bf16)
-
-
-def attend(r):
+        kvg = jnp.where(lo, ka, va)
+        if half == 1:
+            kvg = kvg + before_ref[...].astype(f32)
+        kvg_ref[...] = kvg.astype(bf16)
+
+
+def attend(half, kv, r, *before):
     sources = r.shape[0]
     n = 64 * sources
-    return pl.pallas_call(
-        attend_kernel,
-        grid=(sources // 2,),
+    whole = pl.BlockSpec((n, LANES), lambda i: (0, 0))
+    return pl.pallas_call(
+        functools.partial(attend_kernel, half=half),
+        grid=(sources // STEP,),
         in_specs=[
             pl.BlockSpec((sources, 64, LANES), lambda i: (0, KV_ROW // 64, 0)),
-            pl.BlockSpec((2, ROWS, LANES), lambda i: (i, 0, 0)),
-        ],
-        out_specs=[
-            pl.BlockSpec((2, 256, LANES), lambda i: (i, 0, 0)),
-            pl.BlockSpec((n, LANES), lambda i: (0, 0)),
-        ],
+            pl.BlockSpec((STEP, ROWS[half], LANES), lambda i: (i, 0, 0)),
+        ]
+        + ([] if half == 0 else [whole, pl.BlockSpec(memory_space=pl.ANY)]),
+        out_specs=[pl.BlockSpec((STEP, LANES, LANES), lambda i: (i, half, 0)), whole],
         scratch_shapes=[
             pltpu.VMEM((n, LANES), bf16),
             pltpu.VMEM((n, LANES), bf16),
@@ -226,41 +227,37 @@
             pltpu.VMEM((n, LANES), f32),
         ],
         out_shape=[
-            jax.ShapeDtypeStruct((sources, 256, LANES), bf16),
+            jax.ShapeDtypeStruct((sources, 2 * LANES, LANES), bf16),
             jax.ShapeDtypeStruct((n, LANES), bf16),
         ],
-        compiler_params=params(dimension_semantics=("arbitrary",)),
+        input_output_aliases={} if half == 0 else {3: 0},
+        compiler_params=params(60, dimension_semantics=("arbitrary",)),
         cost_estimate=pl.CostEstimate(
-            flops=40_000_000_000, bytes_accessed=4 << 20, transcendentals=0
+            flops=20_000_000_000, bytes_accessed=2 << 20, transcendentals=0
         ),
         name="attend",
-    )(r, r)
-
-
-def spread_kernel(z_ref, m0_ref, m1_ref, m2_ref, m3_ref, out_ref):
-    mem = jnp.concatenate([m0_ref[0], m1_ref[0], m2_ref[0], m3_ref[0]], 0)
+    )(kv, r, *before)
+
+
+def spread_kernel(in_ref, out_ref):
     for i in range(16):
-        out_ref[i] = mem
-
-
-def spread(z, mems):
+        out_ref[i] = in_ref[...]
+
+
+def spread(x):
     return pl.pallas_call(
         spread_kernel,
-        grid_spec=pltpu.PrefetchScalarGridSpec(
-            num_scalar_prefetch=1,
-            grid=(2,),
-            in_specs=[pl.BlockSpec((1, 16, 256), lambda s, z: (0, 0, s * 4 + z[0]))] * 4,
-            out_specs=pl.BlockSpec((16, 64, 256), lambda s, z: (0, 0, s)),
-        ),
-        out_shape=jax.ShapeDtypeStruct((16, 64, 512), bf16),
+        out_shape=jax.ShapeDtypeStruct((16,) + x.shape, bf16),
         compiler_params=params(),
         cost_estimate=pl.CostEstimate(flops=0, bytes_accessed=1 << 20, transcendentals=0),
         name="spread",
-    )(z, *mems)
-
-
-def weight_kernel(z_ref, p0_ref, p1_ref, p2_ref, p3_ref, mem_ref, out_ref, total_ref, moved_ref):
+    )(x)
+
+
+def weight_kernel(me_ref, p0_ref, p1_ref, p2_ref, p3_ref, mem_ref, out_ref, total_ref, moved_ref):
     step = pl.program_id(0)
+    sec = me_ref[0] // 2
+    core = lax.rem(me_ref[0], 2)
 
     @pl.when(step == 0)
     def _():
@@ -269,35 +266,34 @@
         total_ref[...] = total.astype(bf16)
         for i in range(16):
             for j in range(4):
-                at = (i // 8) * 512 + lax.rem(z_ref[0] + 4 - j, 4) * 128 + (i % 8) * 16
+                at = (sec ^ (j // 2)) * 512 + i * 32 + (core ^ (j % 2)) * 16
                 rows = slice(i * 64 + j * 16, i * 64 + j * 16 + 16)
                 moved_ref[rows, :] = total_ref[pl.ds(pl.multiple_of(at, 16), 16), :]
 
     grad = dot(mem_ref[...], moved_ref[...], TN).astype(bf16)
-    at = pl.multiple_of(step * 512 + z_ref[0] * 128, 128)
-    tokens = total_ref[pl.ds(at, 128), :]
     for i in range(16):
+        at = sec * 512 + step * 256 + (i // 2) * 32 + core * 16
         out_ref[i, 0:16, :] = grad[i * 16 : i * 16 + 16]
-        out_ref[i, 16:32, :] = tokens[(i // 2) * 16 : (i // 2) * 16 + 16]
-
-
-def weight_blocks(z, parts, mem):
+        out_ref[i, 16:32, :] = total_ref[pl.ds(pl.multiple_of(at, 16), 16), :]
+
+
+def weight_blocks(me, parts, mem):
     n = mem.shape[0]
-    part_spec = pl.BlockSpec((n, LANES), lambda s, z: (0, 0))
+    part_spec = pl.BlockSpec((n, LANES), lambda s, me: (0, 0))
     return pl.pallas_call(
         weight_kernel,
         grid_spec=pltpu.PrefetchScalarGridSpec(
             num_scalar_prefetch=1,
             grid=(2,),
-            in_specs=[part_spec] * 4 + [pl.BlockSpec((n, 256), lambda s, z: (0, s))],
-            out_specs=pl.BlockSpec((16, 32, LANES), lambda s, z: (s, 0, 0)),
+            in_specs=[part_spec] * 4 + [pl.BlockSpec((n, 256), lambda s, me: (0, s))],
+            out_specs=pl.BlockSpec((16, 32, LANES), lambda s, me: (s, 0, 0)),
             scratch_shapes=[pltpu.VMEM((n, LANES), bf16), pltpu.VMEM((n, LANES), bf16)],
         ),
         out_shape=jax.ShapeDtypeStruct((32, 32, LANES), bf16),
         compiler_params=params(dimension_semantics=("arbitrary",)),
         cost_estimate=pl.CostEstimate(flops=0, bytes_accessed=6 << 20, transcendentals=0),
         name="weight_blocks",
-    )(z, *parts, mem)
+    )(me, *parts, mem)
 
 
 def finish_kernel(dp_ref, in_ref, wk_ref, wv_ref, mg_ref, wkg_ref, wvg_ref, acc_ref):
@@ -352,15 +348,14 @@
     return lax.all_to_all(x, axes, 0, 0, tiled=True)
 
 
-def shifted(x, axis, k):
-    n = lax.axis_size(axis)
-    return lax.ppermute(x, axis, [(i, (i + k) % n) for i in range(n)])
+def crossed(x, k):
+    return lax.ppermute(x, SUM_AXES, [(i, i ^ k) for i in range(4)])
 
 
 def body(q, g, mem, wk, wv, target_modality, memory_modality, allow_pairs):
-    z = lax.axis_index("z").reshape(1)
+    me = lax.axis_index(SUM_AXES).reshape(1)
     dp = lax.axis_index("dp").reshape(1)
-    mems = [mem] + [shifted(mem, "z", k) for k in (1, 2, 3)]
+    mems = [mem] + [crossed(mem, k) for k in (1, 2, 3)]
 
     labels = jnp.arange(allow_pairs.shape[0], dtype=jnp.int32)
     q_onehot = (target_modality[0][:, None] == labels[None, :]).astype(f32)
@@ -370,20 +365,26 @@
     hide = jnp.where(allowed, 0.0, 1e30).astype(bf16).reshape(16, 2, 1)
     hide = jnp.broadcast_to(hide, (16, 2, HD)).reshape(16, LANES)
 
-    payload = prepare(z, q, g, hide, mems, wk, wv)
-    payload, mems = lax.optimization_barrier((payload, mems))
-    columns = spread(z, mems)
-    targets = exchange(payload, HEAD_AXES)
-    columns, targets = lax.optimization_barrier((columns, targets))
+    first, second = prepare(me, q, g, hide, mems, wk, wv)
+    first, mems = lax.optimization_barrier((first, mems))
+    columns = jnp.concatenate(mems, 0).reshape(64, 2, 16, 2, 32)
+    columns = lax.dynamic_index_in_dim(columns, me[0] // 2, 1, keepdims=False)
+    columns = lax.dynamic_index_in_dim(columns, me[0] % 2, 2, keepdims=False)
+    columns = spread(columns.reshape(64, 512))
+    first = exchange(first, HEAD_AXES)
+    first, second = lax.optimization_barrier((first, second))
+    second = exchange(second, HEAD_AXES)
+    columns, second = lax.optimization_barrier((columns, second))
     memory = exchange(columns, HEAD_AXES).reshape(1024, 512)
 
-    q_grad, part = attend(targets)
+    q_grad, part = attend(0, first, first)
+    q_grad, part = attend(1, first, second, part, q_grad)
     part, memory = lax.optimization_barrier((part, memory))
     q_grad = exchange(q_grad, HEAD_AXES)
-    parts = [part] + [shifted(part, "z", k) for k in (1, 3, 2)]
-    blocks = weight_blocks(z, parts, memory)
+    parts = [part] + [crossed(part, k) for k in (3, 2, 1)]
+    blocks = weight_blocks(me, parts, memory)
     blocks, q_grad = lax.optimization_barrier((blocks, q_grad))
-    blocks = exchange(blocks, ("sec", "y", "core", "dp"))
+    blocks = exchange(blocks, HEAD_AXES + ("dp",))
     m_grad, wk_grad, wv_grad = finish(dp, blocks, wk, wv)
     return unpack_targets(q_grad), m_grad, wk_grad, wv_grad
 

time: 152 us -> 146 us (0.961)
  waiting for transfers between devices: 53.4 us -> 39.1 us
  Pallas kernels: 51.2 us -> 55.5 us
  starting transfers between devices: 40.3 us -> 44.2 us
    all_to_all x4 -> x5, waiting for transfers between devices: 37.9 us -> 23.7 us  [exchange(): return lax.all_to_all(x, axes, 0, 0, tiled=True)]
    pallas_call x2 -> x3, Pallas kernels: 35.1 us -> 39.3 us  [the longest x2 38.3 us: attend(): pl.pallas_call(functools.partial(attend_kernel, half=half), grid=(sources...]
    unnamed x22, local copies, waits for them, and re-layouts: 3.97 us -> 1.38 us
    ppermute x6, starting transfers between devices: 8.15 us -> 10.3 us  [crossed(): return lax.ppermute(x, SUM_AXES, [(i, i ^ k) for i in range(4)])]
    all_to_all x4 -> x5, starting transfers between devices: 32.1 us -> 33.8 us  [exchange(): return lax.all_to_all(x, axes, 0, 0, tiled=True)]
  transfers between devices with their start and end apart: 10 -> 11, of which waited for: 7 -> 6; matrix products, arithmetic and copies ran while one was open for 1% -> 3% of each run, Pallas kernels for 26% -> 30%
where the time goes in v5:
time: 146 us; the launch traced here: 145 us
  Pallas kernels  55.5 us (38%)
  starting transfers between devices  44.2 us (30%)
  waiting for transfers between devices  39.1 us (27%)
  local copies, waits for them, and re-layouts  4.13 us (3%)
    pallas_call x2, Pallas kernels, attend(): pl.pallas_call(functools.partial(attend_kernel, half=half), grid=(sources...  38.3 us
    all_to_all x5, starting transfers between devices, exchange(): return lax.all_to_all(x, axes, 0, 0, tiled=True)  33.8 us
    all_to_all x5, waiting for transfers between devices, exchange(): return lax.all_to_all(x, axes, 0, 0, tiled=True)  23.7 us
    ppermute x6, waiting for transfers between devices, crossed(): return lax.ppermute(x, SUM_AXES, [(i, i ^ k) for i in range(4)])  15.4 us
    ppermute x6, starting transfers between devices, crossed(): return lax.ppermute(x, SUM_AXES, [(i, i ^ k) for i in range(4)])  10.3 us
    pallas_call x1, Pallas kernels, prepare(): pl.pallas_call(prepare_kernel, grid_spec=pltpu.PrefetchScalarGridSpec(num...  7.1 us
    pallas_call x1, Pallas kernels, finish(): pl.pallas_call(finish_kernel, grid_spec=pltpu.PrefetchScalarGridSpec(num_...  5.51 us
  transfers between devices with their start and end apart: 11, of which 6 were waited for; matrix products, arithmetic and copies ran while one was open for 3% of the time, Pallas kernels for 30%

profile of v5, /device:TPU:1, one launch (start us, length us, event | category | flops | bytes accessed | tf_op | source)
XLA Modules:
  0.0 145.0 jit_solution(7721403331404647173)
XLA Ops:
  0.6 4.2 %collective-permute-start.2 = (bf16[1,16,2048]{2,1,0:T(8,128)(2,1)}, bf16[1,16,2048]{2,1,0:T(8,128)(2,1)S(1)}, u32[]{:S(2)}, u32[]{:S(2)}) collective-permute-start(bf16[1,16,2048]{2,1,0:T(8,128)(2,1)} %m0_ref.1), channel_id=1, source_target_pairs={{0,66},{2,64},{64,2},{66,0},{1,67},{3,65},{65,3},{67,1},{4,70},{6,... | collective-permute-start | bytes 196616 | tf_op jit(solution)/shard_map/ppermute | solution.py:352
  4.8 0.1 collective-permute-start.1
  5.0 0.3 collective-permute-start
  5.3 1.0 fusion.12
  6.5 0.7 reshape.38.hide_ref
  7.2 0.5 collective-permute-done.2.m3_ref
  7.7 2.7 %collective-permute-done.1.m2_ref = bf16[1,16,2048]{2,1,0:T(8,128)(2,1)S(1)} collective-permute-done((bf16[1,16,2048]{2,1,0:T(8,128)(2,1)}, bf16[1,16,2048]{2,1,0:T(8,128)(2,1)S(1)}, u32[]{:S(2)}, u32[]{:S(2)}) %collective-permute-start.1) | collective-permute-done | bytes 65568 | tf_op jit(solution)/shard_map/ppermute | solution.py:352
  10.4 0.6 copy-done.7
  11.0 7.1 %prepare.1 = (bf16[16,336,128]{2,1,0:T(8,128)(2,1)}, bf16[16,272,128]{2,1,0:T(8,128)(2,1)}) custom-call(s32[1]{0:T(128)} %bitcast.me_ref, bf16[1,512,1024]{2,1,0:T(8,128)(2,1)} %q_ref.1, bf16[1,512,1024]{2,1,0:T(8,128)(2,1)} %g_ref.1, bf16[16,128]{1,0:T(8,128)(2,1)} %reshape.38.hide_ref, bf16[1,16,2048]{2,1,0:T(8,128)(2,1)} %m0_ref.1, ...), custom_call_target="tpu_custom_call" | custom-call | bytes 16777216 | tf_op jit(solution)/shard_map/prepare/pallas_call | solution.py:75
  18.2 7.9 %all-to-all-start = ((bf16[16,336,128]{2,1,0:T(8,128)(2,1)}), bf16[16,336,128]{2,1,0:T(8,128)(2,1)S(1)}, u32[]{:S(2)}, u32[]{:S(2)}) async-start(bf16[16,336,128]{2,1,0:T(8,128)(2,1)} %get-tuple-element.27), calls=%async_computation | async-start | bytes 2752512 | tf_op jit(solution)/shard_map/all_to_all | solution.py:348
  26.2 0.8 reshape.39
  27.0 0.6 constant_dynamic-slice_fusion
  27.6 0.4 copy.14
  28.0 0.1 copy.15.in_ref
  28.1 1.0 spread.1
  29.2 16.5 %all-to-all-done.refs_0_.refs_1_ = bf16[16,336,128]{2,1,0:T(8,128)(2,1)S(1)} async-done(((bf16[16,336,128]{2,1,0:T(8,128)(2,1)}), bf16[16,336,128]{2,1,0:T(8,128)(2,1)S(1)}, u32[]{:S(2)}, u32[]{:S(2)}) %all-to-all-start) | async-done | bytes 1376288 | tf_op jit(solution)/shard_map/all_to_all | solution.py:348
  45.7 5.5 %all-to-all-start.1 = ((bf16[16,272,128]{2,1,0:T(8,128)(2,1)}), bf16[16,272,128]{2,1,0:T(8,128)(2,1)S(1)}, u32[]{:S(2)}, u32[]{:S(2)}) async-start(bf16[16,272,128]{2,1,0:T(8,128)(2,1)} %get-tuple-element.34), calls=%async_computation.1 | async-start | bytes 2228224 | tf_op jit(solution)/shard_map/all_to_all | solution.py:348
  51.2 19.1 %attend.2 = (bf16[16,256,128]{2,1,0:T(8,128)(2,1)}, bf16[1024,128]{1,0:T(8,128)(2,1)}) custom-call(bf16[16,336,128]{2,1,0:T(8,128)(2,1)} %copy-done.1, bf16[16,336,128]{2,1,0:T(8,128)(2,1)} %copy-done.1), custom_call_target="tpu_custom_call" | custom-call | flops 20000000000 | bytes 2097152 | tf_op jit(solution)/shard_map/attend/pallas_call | solution.py:213
  70.3 6.7 %all-to-all-start.2 = ((bf16[16,64,512]{2,1,0:T(8,128)(2,1)}), bf16[16,64,512]{2,1,0:T(8,128)(2,1)S(1)}, u32[]{:S(2)}, u32[]{:S(2)}) async-start(bf16[16,64,512]{2,1,0:T(8,128)(2,1)} %spread.1), calls=%async_computation.2 | async-start | bytes 2097152 | tf_op jit(solution)/shard_map/all_to_all | solution.py:348
  77.0 19.2 %attend.3 = (bf16[16,256,128]{2,1,0:T(8,128)(2,1)}, bf16[1024,128]{1,0:T(8,128)(2,1)}) custom-call(bf16[16,336,128]{2,1,0:T(8,128)(2,1)} %copy-done.1, bf16[16,272,128]{2,1,0:T(8,128)(2,1)} %copy-done.2, bf16[1024,128]{1,0:T(8,128)(2,1)} %get-tuple-element.36.refs_2_, bf16[16,256,128]{2,1,0:T(8,128)(2,1)} %get-tuple-element.37.refs_3_), custom_call_target="tpu_custom_call", output_to_operand_aliasing={{0}: (3, {})} | custom-call | flops 20000000000 | bytes 2097152 | tf_op jit(solution)/shard_map/attend/pallas_call | solution.py:213
  96.2 6.8 %all-to-all-start.3 = ((bf16[16,256,128]{2,1,0:T(8,128)(2,1)}), bf16[16,256,128]{2,1,0:T(8,128)(2,1)S(1)}, u32[]{:S(2)}, u32[]{:S(2)}) async-start(bf16[16,256,128]{2,1,0:T(8,128)(2,1)} %get-tuple-element.42), calls=%async_computation.3 | async-start | bytes 2097152 | tf_op jit(solution)/shard_map/all_to_all | solution.py:348
  103.0 2.4 %collective-permute-start.5 = (bf16[1024,128]{1,0:T(8,128)(2,1)S(1)}, bf16[1024,128]{1,0:T(8,128)(2,1)S(1)}, u32[]{:S(2)}, u32[]{:S(2)}) collective-permute-start(bf16[1024,128]{1,0:T(8,128)(2,1)S(1)} %copy-done), channel_id=1, source_target_pairs={{0,2},{2,0},{64,66},{66,64},{1,3},{3,1},{65,67},{67,65},{4,6},{6,4... | collective-permute-start | bytes 786440 | tf_op jit(solution)/shard_map/ppermute | solution.py:352
  105.4 2.1 %collective-permute-start.4 = (bf16[1024,128]{1,0:T(8,128)(2,1)S(1)}, bf16[1024,128]{1,0:T(8,128)(2,1)S(1)}, u32[]{:S(2)}, u32[]{:S(2)}) collective-permute-start(bf16[1024,128]{1,0:T(8,128)(2,1)S(1)} %copy-done), channel_id=1, source_target_pairs={{0,64},{2,66},{64,0},{66,2},{1,65},{3,67},{65,1},{67,3},{4,68},{6,... | collective-permute-start | bytes 786440 | tf_op jit(solution)/shard_map/ppermute | solution.py:352
  107.5 1.1 collective-permute-start.3
  108.6 6.1 %collective-permute-done.4.p2_ref = bf16[1024,128]{1,0:T(8,128)(2,1)S(1)} collective-permute-done((bf16[1024,128]{1,0:T(8,128)(2,1)S(1)}, bf16[1024,128]{1,0:T(8,128)(2,1)S(1)}, u32[]{:S(2)}, u32[]{:S(2)}) %collective-permute-start.4) | collective-permute-done | bytes 262176 | tf_op jit(solution)/shard_map/ppermute | solution.py:352
  114.8 6.1 %collective-permute-done.3.p1_ref = bf16[1024,128]{1,0:T(8,128)(2,1)S(1)} collective-permute-done((bf16[1024,128]{1,0:T(8,128)(2,1)S(1)}, bf16[1024,128]{1,0:T(8,128)(2,1)S(1)}, u32[]{:S(2)}, u32[]{:S(2)}) %collective-permute-start.3) | collective-permute-done | bytes 262176 | tf_op jit(solution)/shard_map/ppermute | solution.py:352
  120.9 1.7 %weight_blocks.1 = bf16[32,32,128]{2,1,0:T(8,128)(2,1)} custom-call(s32[1]{0:T(128)} %bitcast.me_ref, bf16[1024,128]{1,0:T(8,128)(2,1)S(1)} %copy-done, bf16[1024,128]{1,0:T(8,128)(2,1)S(1)} %collective-permute-done.3.p1_ref, bf16[1024,128]{1,0:T(8,128)(2,1)S(1)} %collective-permute-done.4.p2_ref, bf16[1024,128]{1,0:T(8,128)(2,1)S(1)} %collective-permute-done.5.p3_ref, ...), custom_call_target="tpu_custom_call" | custom-call | bytes 6291456 | tf_op jit(solution)/shard_map/weight_blocks/pallas_call | solution.py:283
  122.6 7.0 %all-to-all-start.4 = ((bf16[32,32,128]{2,1,0:T(8,128)(2,1)}), bf16[32,32,128]{2,1,0:T(8,128)(2,1)S(1)}, u32[]{:S(2)}, u32[]{:S(2)}) async-start(bf16[32,32,128]{2,1,0:T(8,128)(2,1)} %weight_blocks.1), calls=%async_computation.4 | async-start | bytes 524288 | tf_op jit(solution)/shard_map/all_to_all | solution.py:348
  129.6 1.9 %unpack_targets.1 = bf16[1,512,1024]{2,1,0:T(8,128)(2,1)} custom-call(bf16[16,256,128]{2,1,0:T(8,128)(2,1)S(1)} %all-to-all-done.3.in_ref), custom_call_target="tpu_custom_call" | custom-call | bytes 6291456 | tf_op jit(solution)/shard_map/unpack_targets/pallas_call | solution.py:105
  131.4 7.2 %all-to-all-done.4.in_ref = bf16[32,32,128]{2,1,0:T(8,128)(2,1)S(1)} async-done(((bf16[32,32,128]{2,1,0:T(8,128)(2,1)}), bf16[32,32,128]{2,1,0:T(8,128)(2,1)S(1)}, u32[]{:S(2)}, u32[]{:S(2)}) %all-to-all-start.4) | async-done | bytes 262176 | tf_op jit(solution)/shard_map/all_to_all | solution.py:348
  138.6 0.7 copy-done.3
  139.3 5.5 %finish.1 = (bf16[1,16,2048]{2,1,0:T(8,128)(2,1)}, f32[16,1024]{1,0:T(8,128)}, f32[16,1024]{1,0:T(8,128)}) custom-call(s32[1]{0:T(128)} %bitcast.5.dp_ref, bf16[32,32,128]{2,1,0:T(8,128)(2,1)} %copy-done.3, bf16[2048,1024]{1,0:T(8,128)(2,1)} %wk_ref.3, bf16[2048,1024]{1,0:T(8,128)(2,1)} %wv_ref.3), custom_call_target="tpu_custom_call" | custom-call | bytes 12582912 | tf_op jit(solution)/shard_map/finish/pallas_call | solution.py:331
  (29 shorter events, 0.3 us)
Async XLA Ops:
  0.6 7.0 %collective-permute-start.2 = (bf16[1,16,2048]{2,1,0:T(8,128)(2,1)}, bf16[1,16,2048]{2,1,0:T(8,128)(2,1)S(1)}, u32[]{:S(2)}, u32[]{:S(2)}) collective-permute-start(bf16[1,16,2048]{2,1,0:T(8,128)(2,1)} %m0_ref.1), channel_id=1, source_target_pairs={{0,66},{2,64},{64,2},{66,0},{1,67},{3,65},{65,3},{67,1},{4,70},{6,... | collective-permute-start | bytes 196616 | tf_op jit(solution)/shard_map/ppermute | solution.py:352
  4.8 5.5 %collective-permute-start.1 = (bf16[1,16,2048]{2,1,0:T(8,128)(2,1)}, bf16[1,16,2048]{2,1,0:T(8,128)(2,1)S(1)}, u32[]{:S(2)}, u32[]{:S(2)}) collective-permute-start(bf16[1,16,2048]{2,1,0:T(8,128)(2,1)} %m0_ref.1), channel_id=1, source_target_pairs={{0,64},{2,66},{64,0},{66,2},{1,65},{3,67},{65,1},{67,3},{4,68},{6,... | collective-permute-start | bytes 196616 | tf_op jit(solution)/shard_map/ppermute | solution.py:352
  5.0 5.4 %collective-permute-start = (bf16[1,16,2048]{2,1,0:T(8,128)(2,1)}, bf16[1,16,2048]{2,1,0:T(8,128)(2,1)S(1)}, u32[]{:S(2)}, u32[]{:S(2)}) collective-permute-start(bf16[1,16,2048]{2,1,0:T(8,128)(2,1)} %m0_ref.1), channel_id=1, source_target_pairs={{0,2},{2,0},{64,66},{66,64},{1,3},{3,1},{65,67},{67,65},{4,6},{6,4... | collective-permute-start | bytes 196616 | tf_op jit(solution)/shard_map/ppermute | solution.py:352
  7.7 2.7 %copy-start.5 = (bf16[1,16,2048]{2,1,0:T(8,128)(2,1)}, bf16[1,16,2048]{2,1,0:T(8,128)(2,1)S(1)}, u32[]{:S(2)}) copy-start(bf16[1,16,2048]{2,1,0:T(8,128)(2,1)S(1)} %collective-permute-done.2.m3_ref) | copy-start | bytes 196612
  10.4 0.6 copy-start.7
  10.4 0.6 copy-start.9
  18.1 8.0 %copy-start.4 = (bf16[1,16,2048]{2,1,0:T(8,128)(2,1)S(1)}, bf16[1,16,2048]{2,1,0:T(8,128)(2,1)}, u32[]{:S(2)}) copy-start(bf16[1,16,2048]{2,1,0:T(8,128)(2,1)} %m0_ref.1) | copy-start | bytes 196612
  18.1 8.0 %copy-start.6 = (bf16[1,16,2048]{2,1,0:T(8,128)(2,1)S(1)}, bf16[1,16,2048]{2,1,0:T(8,128)(2,1)}, u32[]{:S(2)}) copy-start(bf16[1,16,2048]{2,1,0:T(8,128)(2,1)} %copy-done.5) | copy-start | bytes 196612
  18.2 8.0 %copy-start.8 = (bf16[1,16,2048]{2,1,0:T(8,128)(2,1)S(1)}, bf16[1,16,2048]{2,1,0:T(8,128)(2,1)}, u32[]{:S(2)}) copy-start(bf16[1,16,2048]{2,1,0:T(8,128)(2,1)} %copy-done.7) | copy-start | bytes 196612
  18.2 8.0 %copy-start.10 = (bf16[1,16,2048]{2,1,0:T(8,128)(2,1)S(1)}, bf16[1,16,2048]{2,1,0:T(8,128)(2,1)}, u32[]{:S(2)}) copy-start(bf16[1,16,2048]{2,1,0:T(8,128)(2,1)} %copy-done.9) | copy-start | bytes 196612
  18.2 27.5 %all-to-all-start = ((bf16[16,336,128]{2,1,0:T(8,128)(2,1)}), bf16[16,336,128]{2,1,0:T(8,128)(2,1)S(1)}, u32[]{:S(2)}, u32[]{:S(2)}) async-start(bf16[16,336,128]{2,1,0:T(8,128)(2,1)} %get-tuple-element.27), calls=%async_computation | async-start | bytes 2752512 | tf_op jit(solution)/shard_map/all_to_all | solution.py:348
  45.7 5.5 %copy-start.1 = (bf16[16,336,128]{2,1,0:T(8,128)(2,1)}, bf16[16,336,128]{2,1,0:T(8,128)(2,1)S(1)}, u32[]{:S(2)}) copy-start(bf16[16,336,128]{2,1,0:T(8,128)(2,1)S(1)} %all-to-all-done.refs_0_.refs_1_) | copy-start | bytes 4128772
  45.7 24.6 %all-to-all-start.1 = ((bf16[16,272,128]{2,1,0:T(8,128)(2,1)}), bf16[16,272,128]{2,1,0:T(8,128)(2,1)S(1)}, u32[]{:S(2)}, u32[]{:S(2)}) async-start(bf16[16,272,128]{2,1,0:T(8,128)(2,1)} %get-tuple-element.34), calls=%async_computation.1 | async-start | bytes 2228224 | tf_op jit(solution)/shard_map/all_to_all | solution.py:348
  70.3 6.7 %copy-start.2 = (bf16[16,272,128]{2,1,0:T(8,128)(2,1)}, bf16[16,272,128]{2,1,0:T(8,128)(2,1)S(1)}, u32[]{:S(2)}) copy-start(bf16[16,272,128]{2,1,0:T(8,128)(2,1)S(1)} %all-to-all-done.1.refs_1_) | copy-start | bytes 3342340
  70.3 25.9 %all-to-all-start.2 = ((bf16[16,64,512]{2,1,0:T(8,128)(2,1)}), bf16[16,64,512]{2,1,0:T(8,128)(2,1)S(1)}, u32[]{:S(2)}, u32[]{:S(2)}) async-start(bf16[16,64,512]{2,1,0:T(8,128)(2,1)} %spread.1), calls=%async_computation.2 | async-start | bytes 2097152 | tf_op jit(solution)/shard_map/all_to_all | solution.py:348
  96.2 6.8 %copy-start = (bf16[1024,128]{1,0:T(8,128)(2,1)S(1)}, bf16[1024,128]{1,0:T(8,128)(2,1)}, u32[]{:S(2)}) copy-start(bf16[1024,128]{1,0:T(8,128)(2,1)} %get-tuple-element.40.p0_ref) | copy-start | bytes 786436
  96.2 26.4 %all-to-all-start.3 = ((bf16[16,256,128]{2,1,0:T(8,128)(2,1)}), bf16[16,256,128]{2,1,0:T(8,128)(2,1)S(1)}, u32[]{:S(2)}, u32[]{:S(2)}) async-start(bf16[16,256,128]{2,1,0:T(8,128)(2,1)} %get-tuple-element.42), calls=%async_computation.3 | async-start | bytes 2097152 | tf_op jit(solution)/shard_map/all_to_all | solution.py:348
  103.0 5.6 %collective-permute-start.5 = (bf16[1024,128]{1,0:T(8,128)(2,1)S(1)}, bf16[1024,128]{1,0:T(8,128)(2,1)S(1)}, u32[]{:S(2)}, u32[]{:S(2)}) collective-permute-start(bf16[1024,128]{1,0:T(8,128)(2,1)S(1)} %copy-done), channel_id=1, source_target_pairs={{0,2},{2,0},{64,66},{66,64},{1,3},{3,1},{65,67},{67,65},{4,6},{6,4... | collective-permute-start | bytes 786440 | tf_op jit(solution)/shard_map/ppermute | solution.py:352
  105.4 9.4 %collective-permute-start.4 = (bf16[1024,128]{1,0:T(8,128)(2,1)S(1)}, bf16[1024,128]{1,0:T(8,128)(2,1)S(1)}, u32[]{:S(2)}, u32[]{:S(2)}) collective-permute-start(bf16[1024,128]{1,0:T(8,128)(2,1)S(1)} %copy-done), channel_id=1, source_target_pairs={{0,64},{2,66},{64,0},{66,2},{1,65},{3,67},{65,1},{67,3},{4,68},{6,... | collective-permute-start | bytes 786440 | tf_op jit(solution)/shard_map/ppermute | solution.py:352
  107.5 13.3 %collective-permute-start.3 = (bf16[1024,128]{1,0:T(8,128)(2,1)S(1)}, bf16[1024,128]{1,0:T(8,128)(2,1)S(1)}, u32[]{:S(2)}, u32[]{:S(2)}) collective-permute-start(bf16[1024,128]{1,0:T(8,128)(2,1)S(1)} %copy-done), channel_id=1, source_target_pairs={{0,66},{2,64},{64,2},{66,0},{1,67},{3,65},{65,3},{67,1},{4,70},{6,... | collective-permute-start | bytes 786440 | tf_op jit(solution)/shard_map/ppermute | solution.py:352
  122.6 16.0 %all-to-all-start.4 = ((bf16[32,32,128]{2,1,0:T(8,128)(2,1)}), bf16[32,32,128]{2,1,0:T(8,128)(2,1)S(1)}, u32[]{:S(2)}, u32[]{:S(2)}) async-start(bf16[32,32,128]{2,1,0:T(8,128)(2,1)} %weight_blocks.1), calls=%async_computation.4 | async-start | bytes 524288 | tf_op jit(solution)/shard_map/all_to_all | solution.py:348
  138.6 0.7 copy-start.3

commit v6 on v5

--- a/solution.py
+++ b/solution.py
@@ -254,7 +254,7 @@
     )(x)
 
 
-def weight_kernel(me_ref, p0_ref, p1_ref, p2_ref, p3_ref, mem_ref, out_ref, total_ref, moved_ref):
+def weight_kernel(me_ref, p0_ref, p1_ref, mem_ref, out_ref, total_ref, moved_ref):
     step = pl.program_id(0)
     sec = me_ref[0] // 2
     core = lax.rem(me_ref[0], 2)
@@ -262,7 +262,6 @@
     @pl.when(step == 0)
     def _():
         total = p0_ref[...].astype(f32) + p1_ref[...].astype(f32)
-        total = total + (p2_ref[...].astype(f32) + p3_ref[...].astype(f32))
         total_ref[...] = total.astype(bf16)
         for i in range(16):
             for j in range(4):
@@ -285,7 +284,7 @@
         grid_spec=pltpu.PrefetchScalarGridSpec(
             num_scalar_prefetch=1,
             grid=(2,),
-            in_specs=[part_spec] * 4 + [pl.BlockSpec((n, 256), lambda s, me: (0, s))],
+            in_specs=[part_spec] * 2 + [pl.BlockSpec((n, 256), lambda s, me: (0, s))],
             out_specs=pl.BlockSpec((16, 32, LANES), lambda s, me: (s, 0, 0)),
             scratch_shapes=[pltpu.VMEM((n, LANES), bf16), pltpu.VMEM((n, LANES), bf16)],
         ),
@@ -381,8 +380,8 @@
     q_grad, part = attend(1, first, second, part, q_grad)
     part, memory = lax.optimization_barrier((part, memory))
     q_grad = exchange(q_grad, HEAD_AXES)
-    parts = [part] + [crossed(part, k) for k in (3, 2, 1)]
-    blocks = weight_blocks(me, parts, memory)
+    pair = (part.astype(f32) + crossed(part, 1).astype(f32)).astype(bf16)
+    blocks = weight_blocks(me, [pair, crossed(pair, 2)], memory)
     blocks, q_grad = lax.optimization_barrier((blocks, q_grad))
     blocks = exchange(blocks, HEAD_AXES + ("dp",))
     m_grad, wk_grad, wv_grad = finish(dp, blocks, wk, wv)

time: 146 us -> 141 us (0.966)
  waiting for transfers between devices: 39.1 us -> 35.1 us
    ppermute x6 -> x5, waiting for transfers between devices: 15.4 us -> 11.2 us  [crossed(): return lax.ppermute(x, SUM_AXES, [(i, i ^ k) for i in range(4)])]
    ppermute x6 -> x5, starting transfers between devices: 10.3 us -> 9.27 us  [crossed(): return lax.ppermute(x, SUM_AXES, [(i, i ^ k) for i in range(4)])]
  transfers between devices with their start and end apart: 11 -> 10, of which waited for: 6 -> 7; matrix products, arithmetic and copies ran while one was open for 3% -> 3% of each run, Pallas kernels for 30% -> 31%
where the time goes in v6:
time: 141 us; the launch traced here: 140 us
  Pallas kernels  55.4 us (39%)
  starting transfers between devices  42.8 us (30%)
  waiting for transfers between devices  35.1 us (25%)
  local copies, waits for them, and re-layouts  4.12 us (3%)
    pallas_call x2, Pallas kernels, attend(): pl.pallas_call(functools.partial(attend_kernel, half=half), grid=(sources...  38.3 us
    all_to_all x5, starting transfers between devices, exchange(): return lax.all_to_all(x, axes, 0, 0, tiled=True)  33.5 us
    all_to_all x5, waiting for transfers between devices, exchange(): return lax.all_to_all(x, axes, 0, 0, tiled=True)  23.9 us
    ppermute x5, waiting for transfers between devices, crossed(): return lax.ppermute(x, SUM_AXES, [(i, i ^ k) for i in range(4)])  11.2 us
    ppermute x5, starting transfers between devices, crossed(): return lax.ppermute(x, SUM_AXES, [(i, i ^ k) for i in range(4)])  9.27 us
    pallas_call x1, Pallas kernels, prepare(): pl.pallas_call(prepare_kernel, grid_spec=pltpu.PrefetchScalarGridSpec(num...  7.1 us
    pallas_call x1, Pallas kernels, finish(): pl.pallas_call(finish_kernel, grid_spec=pltpu.PrefetchScalarGridSpec(num_...  5.51 us
  transfers between devices with their start and end apart: 10, of which 7 were waited for; matrix products, arithmetic and copies ran while one was open for 3% of the time, Pallas kernels for 31%

profile of v6, /device:TPU:1, one launch (start us, length us, event | category | flops | bytes accessed | tf_op | source)
XLA Modules:
  0.0 139.5 jit_solution(3686437546163835396)
XLA Ops:
  0.6 4.2 %collective-permute-start.2 = (bf16[1,16,2048]{2,1,0:T(8,128)(2,1)}, bf16[1,16,2048]{2,1,0:T(8,128)(2,1)S(1)}, u32[]{:S(2)}, u32[]{:S(2)}) collective-permute-start(bf16[1,16,2048]{2,1,0:T(8,128)(2,1)} %m0_ref.1), channel_id=1, source_target_pairs={{0,66},{2,64},{64,2},{66,0},{1,67},{3,65},{65,3},{67,1},{4,70},{6,... | collective-permute-start | bytes 196616 | tf_op jit(solution)/shard_map/ppermute | solution.py:351
  4.8 0.1 collective-permute-start.1
  5.0 0.3 collective-permute-start
  5.3 1.0 fusion.12
  6.5 0.7 reshape.38.hide_ref
  7.2 0.5 collective-permute-done.2.m3_ref
  7.7 2.7 %collective-permute-done.1.m2_ref = bf16[1,16,2048]{2,1,0:T(8,128)(2,1)S(1)} collective-permute-done((bf16[1,16,2048]{2,1,0:T(8,128)(2,1)}, bf16[1,16,2048]{2,1,0:T(8,128)(2,1)S(1)}, u32[]{:S(2)}, u32[]{:S(2)}) %collective-permute-start.1) | collective-permute-done | bytes 65568 | tf_op jit(solution)/shard_map/ppermute | solution.py:351
  10.4 0.6 copy-done.6
  11.0 7.1 %prepare.1 = (bf16[16,336,128]{2,1,0:T(8,128)(2,1)}, bf16[16,272,128]{2,1,0:T(8,128)(2,1)}) custom-call(s32[1]{0:T(128)} %bitcast.me_ref, bf16[1,512,1024]{2,1,0:T(8,128)(2,1)} %q_ref.1, bf16[1,512,1024]{2,1,0:T(8,128)(2,1)} %g_ref.1, bf16[16,128]{1,0:T(8,128)(2,1)} %reshape.38.hide_ref, bf16[1,16,2048]{2,1,0:T(8,128)(2,1)} %m0_ref.1, ...), custom_call_target="tpu_custom_call" | custom-call | bytes 16777216 | tf_op jit(solution)/shard_map/prepare/pallas_call | solution.py:75
  18.2 7.9 %all-to-all-start = ((bf16[16,336,128]{2,1,0:T(8,128)(2,1)}), bf16[16,336,128]{2,1,0:T(8,128)(2,1)S(1)}, u32[]{:S(2)}, u32[]{:S(2)}) async-start(bf16[16,336,128]{2,1,0:T(8,128)(2,1)} %get-tuple-element.27), calls=%async_computation | async-start | bytes 2752512 | tf_op jit(solution)/shard_map/all_to_all | solution.py:347
  26.2 0.8 reshape.39
  27.0 0.6 constant_dynamic-slice_fusion
  27.6 0.4 copy.14
  28.0 0.1 copy.15.in_ref
  28.1 1.0 spread.1
  29.2 16.5 %all-to-all-done.refs_0_.refs_1_ = bf16[16,336,128]{2,1,0:T(8,128)(2,1)S(1)} async-done(((bf16[16,336,128]{2,1,0:T(8,128)(2,1)}), bf16[16,336,128]{2,1,0:T(8,128)(2,1)S(1)}, u32[]{:S(2)}, u32[]{:S(2)}) %all-to-all-start) | async-done | bytes 1376288 | tf_op jit(solution)/shard_map/all_to_all | solution.py:347
  45.7 5.5 %all-to-all-start.1 = ((bf16[16,272,128]{2,1,0:T(8,128)(2,1)}), bf16[16,272,128]{2,1,0:T(8,128)(2,1)S(1)}, u32[]{:S(2)}, u32[]{:S(2)}) async-start(bf16[16,272,128]{2,1,0:T(8,128)(2,1)} %get-tuple-element.34), calls=%async_computation.1 | async-start | bytes 2228224 | tf_op jit(solution)/shard_map/all_to_all | solution.py:347
  51.2 19.1 %attend.2 = (bf16[16,256,128]{2,1,0:T(8,128)(2,1)}, bf16[1024,128]{1,0:T(8,128)(2,1)}) custom-call(bf16[16,336,128]{2,1,0:T(8,128)(2,1)} %copy-done, bf16[16,336,128]{2,1,0:T(8,128)(2,1)} %copy-done), custom_call_target="tpu_custom_call" | custom-call | flops 20000000000 | bytes 2097152 | tf_op jit(solution)/shard_map/attend/pallas_call | solution.py:213
  70.3 6.7 %all-to-all-start.2 = ((bf16[16,64,512]{2,1,0:T(8,128)(2,1)}), bf16[16,64,512]{2,1,0:T(8,128)(2,1)S(1)}, u32[]{:S(2)}, u32[]{:S(2)}) async-start(bf16[16,64,512]{2,1,0:T(8,128)(2,1)} %spread.1), calls=%async_computation.2 | async-start | bytes 2097152 | tf_op jit(solution)/shard_map/all_to_all | solution.py:347
  77.0 19.2 %attend.3 = (bf16[16,256,128]{2,1,0:T(8,128)(2,1)}, bf16[1024,128]{1,0:T(8,128)(2,1)}) custom-call(bf16[16,336,128]{2,1,0:T(8,128)(2,1)} %copy-done, bf16[16,272,128]{2,1,0:T(8,128)(2,1)} %copy-done.1, bf16[1024,128]{1,0:T(8,128)(2,1)} %get-tuple-element.36.refs_2_, bf16[16,256,128]{2,1,0:T(8,128)(2,1)} %get-tuple-element.37.refs_3_), custom_call_target="tpu_custom_call", output_to_operand_aliasing={{0}: (3, {})} | custom-call | flops 20000000000 | bytes 2097152 | tf_op jit(solution)/shard_map/attend/pallas_call | solution.py:213
  96.2 6.8 %all-to-all-start.3 = ((bf16[16,256,128]{2,1,0:T(8,128)(2,1)}), bf16[16,256,128]{2,1,0:T(8,128)(2,1)S(1)}, u32[]{:S(2)}, u32[]{:S(2)}) async-start(bf16[16,256,128]{2,1,0:T(8,128)(2,1)} %get-tuple-element.42), calls=%async_computation.3 | async-start | bytes 2097152 | tf_op jit(solution)/shard_map/all_to_all | solution.py:347
  103.0 2.4 %collective-permute-start.3 = (bf16[1024,128]{1,0:T(8,128)(2,1)S(1)}, bf16[1024,128]{1,0:T(8,128)(2,1)S(1)}, u32[]{:S(2)}, u32[]{:S(2)}) collective-permute-start(bf16[1024,128]{1,0:T(8,128)(2,1)S(1)} %copy-done.10), channel_id=1, source_target_pairs={{0,2},{2,0},{64,66},{66,64},{1,3},{3,1},{65,67},{67,65},{4,6},{6,4... | collective-permute-start | bytes 786440 | tf_op jit(solution)/shard_map/ppermute | solution.py:351
  105.4 1.2 collective-permute-done.3
  106.6 2.2 %collective-permute-start.4 = (bf16[1024,128]{1,0:T(8,128)(2,1)S(1)}, bf16[1024,128]{1,0:T(8,128)(2,1)S(1)}, u32[]{:S(2)}, u32[]{:S(2)}) collective-permute-start(bf16[1024,128]{1,0:T(8,128)(2,1)S(1)} %add_convert_fusion.p0_ref), channel_id=1, source_target_pairs={{0,64},{2,66},{64,0},{66,2},{1,65},{3,67},{65,1},{67,3},{4,68},{6,... | collective-permute-start | bytes 786440 | tf_op jit(solution)/shard_map/ppermute | solution.py:351
  108.8 6.9 %collective-permute-done.4.p1_ref = bf16[1024,128]{1,0:T(8,128)(2,1)S(1)} collective-permute-done((bf16[1024,128]{1,0:T(8,128)(2,1)S(1)}, bf16[1024,128]{1,0:T(8,128)(2,1)S(1)}, u32[]{:S(2)}, u32[]{:S(2)}) %collective-permute-start.4) | collective-permute-done | bytes 262176 | tf_op jit(solution)/shard_map/ppermute | solution.py:351
  115.7 1.6 %weight_blocks.1 = bf16[32,32,128]{2,1,0:T(8,128)(2,1)} custom-call(s32[1]{0:T(128)} %bitcast.me_ref, bf16[1024,128]{1,0:T(8,128)(2,1)S(1)} %add_convert_fusion.p0_ref, bf16[1024,128]{1,0:T(8,128)(2,1)S(1)} %collective-permute-done.4.p1_ref, bf16[1024,512]{1,0:T(8,128)(2,1)S(1)} %bitcast.6), custom_call_target="tpu_custom_call" | custom-call | bytes 6291456 | tf_op jit(solution)/shard_map/weight_blocks/pallas_call | solution.py:282
  117.4 0.6 all-to-all-done.3.in_ref
  118.0 6.7 %all-to-all-start.4 = ((bf16[32,32,128]{2,1,0:T(8,128)(2,1)}), bf16[32,32,128]{2,1,0:T(8,128)(2,1)S(1)}, u32[]{:S(2)}, u32[]{:S(2)}) async-start(bf16[32,32,128]{2,1,0:T(8,128)(2,1)} %weight_blocks.1), calls=%async_computation.4 | async-start | bytes 524288 | tf_op jit(solution)/shard_map/all_to_all | solution.py:347
  124.6 1.9 %unpack_targets.1 = bf16[1,512,1024]{2,1,0:T(8,128)(2,1)} custom-call(bf16[16,256,128]{2,1,0:T(8,128)(2,1)S(1)} %all-to-all-done.3.in_ref), custom_call_target="tpu_custom_call" | custom-call | bytes 6291456 | tf_op jit(solution)/shard_map/unpack_targets/pallas_call | solution.py:105
  126.5 6.7 %all-to-all-done.4.in_ref = bf16[32,32,128]{2,1,0:T(8,128)(2,1)S(1)} async-done(((bf16[32,32,128]{2,1,0:T(8,128)(2,1)}), bf16[32,32,128]{2,1,0:T(8,128)(2,1)S(1)}, u32[]{:S(2)}, u32[]{:S(2)}) %all-to-all-start.4) | async-done | bytes 262176 | tf_op jit(solution)/shard_map/all_to_all | solution.py:347
  133.2 0.7 copy-done.2
  133.9 5.5 %finish.1 = (bf16[1,16,2048]{2,1,0:T(8,128)(2,1)}, f32[16,1024]{1,0:T(8,128)}, f32[16,1024]{1,0:T(8,128)}) custom-call(s32[1]{0:T(128)} %bitcast.5.dp_ref, bf16[32,32,128]{2,1,0:T(8,128)(2,1)} %copy-done.2, bf16[2048,1024]{1,0:T(8,128)(2,1)} %wk_ref.3, bf16[2048,1024]{1,0:T(8,128)(2,1)} %wv_ref.3), custom_call_target="tpu_custom_call" | custom-call | bytes 12582912 | tf_op jit(solution)/shard_map/finish/pallas_call | solution.py:330
  (28 shorter events, 0.4 us)
Async XLA Ops:
  0.6 7.0 %collective-permute-start.2 = (bf16[1,16,2048]{2,1,0:T(8,128)(2,1)}, bf16[1,16,2048]{2,1,0:T(8,128)(2,1)S(1)}, u32[]{:S(2)}, u32[]{:S(2)}) collective-permute-start(bf16[1,16,2048]{2,1,0:T(8,128)(2,1)} %m0_ref.1), channel_id=1, source_target_pairs={{0,66},{2,64},{64,2},{66,0},{1,67},{3,65},{65,3},{67,1},{4,70},{6,... | collective-permute-start | bytes 196616 | tf_op jit(solution)/shard_map/ppermute | solution.py:351
  4.8 5.5 %collective-permute-start.1 = (bf16[1,16,2048]{2,1,0:T(8,128)(2,1)}, bf16[1,16,2048]{2,1,0:T(8,128)(2,1)S(1)}, u32[]{:S(2)}, u32[]{:S(2)}) collective-permute-start(bf16[1,16,2048]{2,1,0:T(8,128)(2,1)} %m0_ref.1), channel_id=1, source_target_pairs={{0,64},{2,66},{64,0},{66,2},{1,65},{3,67},{65,1},{67,3},{4,68},{6,... | collective-permute-start | bytes 196616 | tf_op jit(solution)/shard_map/ppermute | solution.py:351
  5.0 5.4 %collective-permute-start = (bf16[1,16,2048]{2,1,0:T(8,128)(2,1)}, bf16[1,16,2048]{2,1,0:T(8,128)(2,1)S(1)}, u32[]{:S(2)}, u32[]{:S(2)}) collective-permute-start(bf16[1,16,2048]{2,1,0:T(8,128)(2,1)} %m0_ref.1), channel_id=1, source_target_pairs={{0,2},{2,0},{64,66},{66,64},{1,3},{3,1},{65,67},{67,65},{4,6},{6,4... | collective-permute-start | bytes 196616 | tf_op jit(solution)/shard_map/ppermute | solution.py:351
  7.7 2.7 %copy-start.4 = (bf16[1,16,2048]{2,1,0:T(8,128)(2,1)}, bf16[1,16,2048]{2,1,0:T(8,128)(2,1)S(1)}, u32[]{:S(2)}) copy-start(bf16[1,16,2048]{2,1,0:T(8,128)(2,1)S(1)} %collective-permute-done.2.m3_ref) | copy-start | bytes 196612
  10.4 0.6 copy-start.6
  10.4 0.6 copy-start.8
  18.1 8.0 %copy-start.3 = (bf16[1,16,2048]{2,1,0:T(8,128)(2,1)S(1)}, bf16[1,16,2048]{2,1,0:T(8,128)(2,1)}, u32[]{:S(2)}) copy-start(bf16[1,16,2048]{2,1,0:T(8,128)(2,1)} %m0_ref.1) | copy-start | bytes 196612
  18.1 8.0 %copy-start.5 = (bf16[1,16,2048]{2,1,0:T(8,128)(2,1)S(1)}, bf16[1,16,2048]{2,1,0:T(8,128)(2,1)}, u32[]{:S(2)}) copy-start(bf16[1,16,2048]{2,1,0:T(8,128)(2,1)} %copy-done.4) | copy-start | bytes 196612
  18.1 8.0 %copy-start.7 = (bf16[1,16,2048]{2,1,0:T(8,128)(2,1)S(1)}, bf16[1,16,2048]{2,1,0:T(8,128)(2,1)}, u32[]{:S(2)}) copy-start(bf16[1,16,2048]{2,1,0:T(8,128)(2,1)} %copy-done.6) | copy-start | bytes 196612
  18.2 8.0 %copy-start.9 = (bf16[1,16,2048]{2,1,0:T(8,128)(2,1)S(1)}, bf16[1,16,2048]{2,1,0:T(8,128)(2,1)}, u32[]{:S(2)}) copy-start(bf16[1,16,2048]{2,1,0:T(8,128)(2,1)} %copy-done.8) | copy-start | bytes 196612
  18.2 27.5 %all-to-all-start = ((bf16[16,336,128]{2,1,0:T(8,128)(2,1)}), bf16[16,336,128]{2,1,0:T(8,128)(2,1)S(1)}, u32[]{:S(2)}, u32[]{:S(2)}) async-start(bf16[16,336,128]{2,1,0:T(8,128)(2,1)} %get-tuple-element.27), calls=%async_computation | async-start | bytes 2752512 | tf_op jit(solution)/shard_map/all_to_all | solution.py:347
  45.7 5.5 %copy-start = (bf16[16,336,128]{2,1,0:T(8,128)(2,1)}, bf16[16,336,128]{2,1,0:T(8,128)(2,1)S(1)}, u32[]{:S(2)}) copy-start(bf16[16,336,128]{2,1,0:T(8,128)(2,1)S(1)} %all-to-all-done.refs_0_.refs_1_) | copy-start | bytes 4128772
  45.7 24.6 %all-to-all-start.1 = ((bf16[16,272,128]{2,1,0:T(8,128)(2,1)}), bf16[16,272,128]{2,1,0:T(8,128)(2,1)S(1)}, u32[]{:S(2)}, u32[]{:S(2)}) async-start(bf16[16,272,128]{2,1,0:T(8,128)(2,1)} %get-tuple-element.34), calls=%async_computation.1 | async-start | bytes 2228224 | tf_op jit(solution)/shard_map/all_to_all | solution.py:347
  70.3 6.7 %copy-start.1 = (bf16[16,272,128]{2,1,0:T(8,128)(2,1)}, bf16[16,272,128]{2,1,0:T(8,128)(2,1)S(1)}, u32[]{:S(2)}) copy-start(bf16[16,272,128]{2,1,0:T(8,128)(2,1)S(1)} %all-to-all-done.1.refs_1_) | copy-start | bytes 3342340
  70.3 25.9 %all-to-all-start.2 = ((bf16[16,64,512]{2,1,0:T(8,128)(2,1)}), bf16[16,64,512]{2,1,0:T(8,128)(2,1)S(1)}, u32[]{:S(2)}, u32[]{:S(2)}) async-start(bf16[16,64,512]{2,1,0:T(8,128)(2,1)} %spread.1), calls=%async_computation.2 | async-start | bytes 2097152 | tf_op jit(solution)/shard_map/all_to_all | solution.py:347
  96.2 6.8 %copy-start.10 = (bf16[1024,128]{1,0:T(8,128)(2,1)S(1)}, bf16[1024,128]{1,0:T(8,128)(2,1)}, u32[]{:S(2)}) copy-start(bf16[1024,128]{1,0:T(8,128)(2,1)} %get-tuple-element.40) | copy-start | bytes 786436
  96.2 21.8 %all-to-all-start.3 = ((bf16[16,256,128]{2,1,0:T(8,128)(2,1)}), bf16[16,256,128]{2,1,0:T(8,128)(2,1)S(1)}, u32[]{:S(2)}, u32[]{:S(2)}) async-start(bf16[16,256,128]{2,1,0:T(8,128)(2,1)} %get-tuple-element.42), calls=%async_computation.3 | async-start | bytes 2097152 | tf_op jit(solution)/shard_map/all_to_all | solution.py:347
  103.0 3.5 %collective-permute-start.3 = (bf16[1024,128]{1,0:T(8,128)(2,1)S(1)}, bf16[1024,128]{1,0:T(8,128)(2,1)S(1)}, u32[]{:S(2)}, u32[]{:S(2)}) collective-permute-start(bf16[1024,128]{1,0:T(8,128)(2,1)S(1)} %copy-done.10), channel_id=1, source_target_pairs={{0,2},{2,0},{64,66},{66,64},{1,3},{3,1},{65,67},{67,65},{4,6},{6,4... | collective-permute-start | bytes 786440 | tf_op jit(solution)/shard_map/ppermute | solution.py:351
  106.6 9.1 %collective-permute-start.4 = (bf16[1024,128]{1,0:T(8,128)(2,1)S(1)}, bf16[1024,128]{1,0:T(8,128)(2,1)S(1)}, u32[]{:S(2)}, u32[]{:S(2)}) collective-permute-start(bf16[1024,128]{1,0:T(8,128)(2,1)S(1)} %add_convert_fusion.p0_ref), channel_id=1, source_target_pairs={{0,64},{2,66},{64,0},{66,2},{1,65},{3,67},{65,1},{67,3},{4,68},{6,... | collective-permute-start | bytes 786440 | tf_op jit(solution)/shard_map/ppermute | solution.py:351
  118.0 15.2 %all-to-all-start.4 = ((bf16[32,32,128]{2,1,0:T(8,128)(2,1)}), bf16[32,32,128]{2,1,0:T(8,128)(2,1)S(1)}, u32[]{:S(2)}, u32[]{:S(2)}) async-start(bf16[32,32,128]{2,1,0:T(8,128)(2,1)} %weight_blocks.1), calls=%async_computation.4 | async-start | bytes 524288 | tf_op jit(solution)/shard_map/all_to_all | solution.py:347
  133.2 0.7 copy-start.2

commit v7 on v6

--- a/solution.py
+++ b/solution.py
@@ -49,7 +49,7 @@
     mem = jnp.concatenate([m0_ref[0], m1_ref[0], m2_ref[0], m3_ref[0]], 0)
     keys = dot(mem, wk_ref[...], NN)
     values = dot(mem, wv_ref[...], NN)
-    for i in range(2):
+    for i in range(4):
         cols = slice(i * LANES, (i + 1) * LANES)
         for t, out_ref in enumerate(out_refs):
             for k, ref in enumerate((q_ref, g_ref)):
@@ -69,19 +69,19 @@
 
 def prepare(me, q, g, hide, mems, wk, wv):
     d = wk.shape[0]
-    target_spec = pl.BlockSpec((1, 512, 256), lambda p, me: (0, 0, p))
+    target_spec = pl.BlockSpec((1, 512, 512), lambda p, me: (0, 0, p))
     mem_spec = pl.BlockSpec((1, 16, d), lambda p, me: (0, 0, 0))
-    w_spec = pl.BlockSpec((d, 256), lambda p, me: (0, p))
+    w_spec = pl.BlockSpec((d, 512), lambda p, me: (0, p))
     return pl.pallas_call(
         prepare_kernel,
         grid_spec=pltpu.PrefetchScalarGridSpec(
             num_scalar_prefetch=1,
-            grid=(4,),
+            grid=(2,),
             in_specs=[target_spec] * 2
             + [pl.BlockSpec((16, LANES), lambda p, me: (0, 0))]
             + [mem_spec] * 4
             + [w_spec] * 2,
-            out_specs=[pl.BlockSpec((4, rows, LANES), lambda p, me: (p, 0, 0)) for rows in ROWS],
+            out_specs=[pl.BlockSpec((8, rows, LANES), lambda p, me: (p, 0, 0)) for rows in ROWS],
         ),
         out_shape=[jax.ShapeDtypeStruct((16, rows, LANES), bf16) for rows in ROWS],
         compiler_params=params(60),

time: 141 us -> 140 us (level)
  no operation moved by 1% of the time
where the time goes in v7:
time: 140 us; the launch traced here: 139 us
  Pallas kernels  54.6 us (39%)
  starting transfers between devices  42.8 us (31%)
  waiting for transfers between devices  35.1 us (25%)
  local copies, waits for them, and re-layouts  4.12 us (3%)
    pallas_call x2, Pallas kernels, attend(): pl.pallas_call(functools.partial(attend_kernel, half=half), grid=(sources...  38.3 us
    all_to_all x5, starting transfers between devices, exchange(): return lax.all_to_all(x, axes, 0, 0, tiled=True)  33.5 us
    all_to_all x5, waiting for transfers between devices, exchange(): return lax.all_to_all(x, axes, 0, 0, tiled=True)  23.9 us
    ppermute x5, waiting for transfers between devices, crossed(): return lax.ppermute(x, SUM_AXES, [(i, i ^ k) for i in range(4)])  11.3 us
    ppermute x5, starting transfers between devices, crossed(): return lax.ppermute(x, SUM_AXES, [(i, i ^ k) for i in range(4)])  9.28 us
    pallas_call x1, Pallas kernels, prepare(): pl.pallas_call(prepare_kernel, grid_spec=pltpu.PrefetchScalarGridSpec(num...  6.27 us
    pallas_call x1, Pallas kernels, finish(): pl.pallas_call(finish_kernel, grid_spec=pltpu.PrefetchScalarGridSpec(num_...  5.51 us
  transfers between devices with their start and end apart: 10, of which 7 were waited for; matrix products, arithmetic and copies ran while one was open for 3% of the time, Pallas kernels for 31%

profile of v7, /device:TPU:1, one launch (start us, length us, event | category | flops | bytes accessed | tf_op | source)
XLA Modules:
  0.0 138.7 jit_solution(9624256525069752113)
XLA Ops:
  0.6 4.2 %collective-permute-start.2 = (bf16[1,16,2048]{2,1,0:T(8,128)(2,1)}, bf16[1,16,2048]{2,1,0:T(8,128)(2,1)S(1)}, u32[]{:S(2)}, u32[]{:S(2)}) collective-permute-start(bf16[1,16,2048]{2,1,0:T(8,128)(2,1)} %m0_ref.1), channel_id=1, source_target_pairs={{0,66},{2,64},{64,2},{66,0},{1,67},{3,65},{65,3},{67,1},{4,70},{6,... | collective-permute-start | bytes 196616 | tf_op jit(solution)/shard_map/ppermute | solution.py:351
  4.8 0.1 collective-permute-start.1
  5.0 0.3 collective-permute-start
  5.3 1.0 fusion.12
  6.5 0.7 reshape.38.hide_ref
  7.2 0.5 collective-permute-done.2.m3_ref
  7.7 2.7 %collective-permute-done.1.m2_ref = bf16[1,16,2048]{2,1,0:T(8,128)(2,1)S(1)} collective-permute-done((bf16[1,16,2048]{2,1,0:T(8,128)(2,1)}, bf16[1,16,2048]{2,1,0:T(8,128)(2,1)S(1)}, u32[]{:S(2)}, u32[]{:S(2)}) %collective-permute-start.1) | collective-permute-done | bytes 65568 | tf_op jit(solution)/shard_map/ppermute | solution.py:351
  10.4 0.6 copy-done.6
  11.0 6.3 %prepare.1 = (bf16[16,336,128]{2,1,0:T(8,128)(2,1)}, bf16[16,272,128]{2,1,0:T(8,128)(2,1)}) custom-call(s32[1]{0:T(128)} %bitcast.me_ref, bf16[1,512,1024]{2,1,0:T(8,128)(2,1)} %q_ref.1, bf16[1,512,1024]{2,1,0:T(8,128)(2,1)} %g_ref.1, bf16[16,128]{1,0:T(8,128)(2,1)} %reshape.38.hide_ref, bf16[1,16,2048]{2,1,0:T(8,128)(2,1)} %m0_ref.1, ...), custom_call_target="tpu_custom_call" | custom-call | bytes 16777216 | tf_op jit(solution)/shard_map/prepare/pallas_call | solution.py:75
  17.3 7.9 %all-to-all-start = ((bf16[16,336,128]{2,1,0:T(8,128)(2,1)}), bf16[16,336,128]{2,1,0:T(8,128)(2,1)S(1)}, u32[]{:S(2)}, u32[]{:S(2)}) async-start(bf16[16,336,128]{2,1,0:T(8,128)(2,1)} %get-tuple-element.27), calls=%async_computation | async-start | bytes 2752512 | tf_op jit(solution)/shard_map/all_to_all | solution.py:347
  25.4 0.8 reshape.39
  26.2 0.6 constant_dynamic-slice_fusion
  26.8 0.4 copy.14
  27.2 0.1 copy.15.in_ref
  27.3 1.0 spread.1
  28.3 16.6 %all-to-all-done.refs_0_.refs_1_ = bf16[16,336,128]{2,1,0:T(8,128)(2,1)S(1)} async-done(((bf16[16,336,128]{2,1,0:T(8,128)(2,1)}), bf16[16,336,128]{2,1,0:T(8,128)(2,1)S(1)}, u32[]{:S(2)}, u32[]{:S(2)}) %all-to-all-start) | async-done | bytes 1376288 | tf_op jit(solution)/shard_map/all_to_all | solution.py:347
  44.9 5.5 %all-to-all-start.1 = ((bf16[16,272,128]{2,1,0:T(8,128)(2,1)}), bf16[16,272,128]{2,1,0:T(8,128)(2,1)S(1)}, u32[]{:S(2)}, u32[]{:S(2)}) async-start(bf16[16,272,128]{2,1,0:T(8,128)(2,1)} %get-tuple-element.34), calls=%async_computation.1 | async-start | bytes 2228224 | tf_op jit(solution)/shard_map/all_to_all | solution.py:347
  50.4 19.1 %attend.2 = (bf16[16,256,128]{2,1,0:T(8,128)(2,1)}, bf16[1024,128]{1,0:T(8,128)(2,1)}) custom-call(bf16[16,336,128]{2,1,0:T(8,128)(2,1)} %copy-done, bf16[16,336,128]{2,1,0:T(8,128)(2,1)} %copy-done), custom_call_target="tpu_custom_call" | custom-call | flops 20000000000 | bytes 2097152 | tf_op jit(solution)/shard_map/attend/pallas_call | solution.py:213
  69.5 6.7 %all-to-all-start.2 = ((bf16[16,64,512]{2,1,0:T(8,128)(2,1)}), bf16[16,64,512]{2,1,0:T(8,128)(2,1)S(1)}, u32[]{:S(2)}, u32[]{:S(2)}) async-start(bf16[16,64,512]{2,1,0:T(8,128)(2,1)} %spread.1), calls=%async_computation.2 | async-start | bytes 2097152 | tf_op jit(solution)/shard_map/all_to_all | solution.py:347
  76.2 19.2 %attend.3 = (bf16[16,256,128]{2,1,0:T(8,128)(2,1)}, bf16[1024,128]{1,0:T(8,128)(2,1)}) custom-call(bf16[16,336,128]{2,1,0:T(8,128)(2,1)} %copy-done, bf16[16,272,128]{2,1,0:T(8,128)(2,1)} %copy-done.1, bf16[1024,128]{1,0:T(8,128)(2,1)} %get-tuple-element.36.refs_2_, bf16[16,256,128]{2,1,0:T(8,128)(2,1)} %get-tuple-element.37.refs_3_), custom_call_target="tpu_custom_call", output_to_operand_aliasing={{0}: (3, {})} | custom-call | flops 20000000000 | bytes 2097152 | tf_op jit(solution)/shard_map/attend/pallas_call | solution.py:213
  95.4 6.8 %all-to-all-start.3 = ((bf16[16,256,128]{2,1,0:T(8,128)(2,1)}), bf16[16,256,128]{2,1,0:T(8,128)(2,1)S(1)}, u32[]{:S(2)}, u32[]{:S(2)}) async-start(bf16[16,256,128]{2,1,0:T(8,128)(2,1)} %get-tuple-element.42), calls=%async_computation.3 | async-start | bytes 2097152 | tf_op jit(solution)/shard_map/all_to_all | solution.py:347
  102.2 2.4 %collective-permute-start.3 = (bf16[1024,128]{1,0:T(8,128)(2,1)S(1)}, bf16[1024,128]{1,0:T(8,128)(2,1)S(1)}, u32[]{:S(2)}, u32[]{:S(2)}) collective-permute-start(bf16[1024,128]{1,0:T(8,128)(2,1)S(1)} %copy-done.10), channel_id=1, source_target_pairs={{0,2},{2,0},{64,66},{66,64},{1,3},{3,1},{65,67},{67,65},{4,6},{6,4... | collective-permute-start | bytes 786440 | tf_op jit(solution)/shard_map/ppermute | solution.py:351
  104.6 1.2 collective-permute-done.3
  105.8 2.2 %collective-permute-start.4 = (bf16[1024,128]{1,0:T(8,128)(2,1)S(1)}, bf16[1024,128]{1,0:T(8,128)(2,1)S(1)}, u32[]{:S(2)}, u32[]{:S(2)}) collective-permute-start(bf16[1024,128]{1,0:T(8,128)(2,1)S(1)} %add_convert_fusion.p0_ref), channel_id=1, source_target_pairs={{0,64},{2,66},{64,0},{66,2},{1,65},{3,67},{65,1},{67,3},{4,68},{6,... | collective-permute-start | bytes 786440 | tf_op jit(solution)/shard_map/ppermute | solution.py:351
  108.0 6.9 %collective-permute-done.4.p1_ref = bf16[1024,128]{1,0:T(8,128)(2,1)S(1)} collective-permute-done((bf16[1024,128]{1,0:T(8,128)(2,1)S(1)}, bf16[1024,128]{1,0:T(8,128)(2,1)S(1)}, u32[]{:S(2)}, u32[]{:S(2)}) %collective-permute-start.4) | collective-permute-done | bytes 262176 | tf_op jit(solution)/shard_map/ppermute | solution.py:351
  114.9 1.6 %weight_blocks.1 = bf16[32,32,128]{2,1,0:T(8,128)(2,1)} custom-call(s32[1]{0:T(128)} %bitcast.me_ref, bf16[1024,128]{1,0:T(8,128)(2,1)S(1)} %add_convert_fusion.p0_ref, bf16[1024,128]{1,0:T(8,128)(2,1)S(1)} %collective-permute-done.4.p1_ref, bf16[1024,512]{1,0:T(8,128)(2,1)S(1)} %bitcast.6), custom_call_target="tpu_custom_call" | custom-call | bytes 6291456 | tf_op jit(solution)/shard_map/weight_blocks/pallas_call | solution.py:282
  116.5 0.6 all-to-all-done.3.in_ref
  117.2 6.6 %all-to-all-start.4 = ((bf16[32,32,128]{2,1,0:T(8,128)(2,1)}), bf16[32,32,128]{2,1,0:T(8,128)(2,1)S(1)}, u32[]{:S(2)}, u32[]{:S(2)}) async-start(bf16[32,32,128]{2,1,0:T(8,128)(2,1)} %weight_blocks.1), calls=%async_computation.4 | async-start | bytes 524288 | tf_op jit(solution)/shard_map/all_to_all | solution.py:347
  123.8 1.9 %unpack_targets.1 = bf16[1,512,1024]{2,1,0:T(8,128)(2,1)} custom-call(bf16[16,256,128]{2,1,0:T(8,128)(2,1)S(1)} %all-to-all-done.3.in_ref), custom_call_target="tpu_custom_call" | custom-call | bytes 6291456 | tf_op jit(solution)/shard_map/unpack_targets/pallas_call | solution.py:105
  125.7 6.7 %all-to-all-done.4.in_ref = bf16[32,32,128]{2,1,0:T(8,128)(2,1)S(1)} async-done(((bf16[32,32,128]{2,1,0:T(8,128)(2,1)}), bf16[32,32,128]{2,1,0:T(8,128)(2,1)S(1)}, u32[]{:S(2)}, u32[]{:S(2)}) %all-to-all-start.4) | async-done | bytes 262176 | tf_op jit(solution)/shard_map/all_to_all | solution.py:347
  132.4 0.7 copy-done.2
  133.1 5.5 %finish.1 = (bf16[1,16,2048]{2,1,0:T(8,128)(2,1)}, f32[16,1024]{1,0:T(8,128)}, f32[16,1024]{1,0:T(8,128)}) custom-call(s32[1]{0:T(128)} %bitcast.5.dp_ref, bf16[32,32,128]{2,1,0:T(8,128)(2,1)} %copy-done.2, bf16[2048,1024]{1,0:T(8,128)(2,1)} %wk_ref.3, bf16[2048,1024]{1,0:T(8,128)(2,1)} %wv_ref.3), custom_call_target="tpu_custom_call" | custom-call | bytes 12582912 | tf_op jit(solution)/shard_map/finish/pallas_call | solution.py:330
  (28 shorter events, 0.4 us)
Async XLA Ops:
  0.6 7.0 %collective-permute-start.2 = (bf16[1,16,2048]{2,1,0:T(8,128)(2,1)}, bf16[1,16,2048]{2,1,0:T(8,128)(2,1)S(1)}, u32[]{:S(2)}, u32[]{:S(2)}) collective-permute-start(bf16[1,16,2048]{2,1,0:T(8,128)(2,1)} %m0_ref.1), channel_id=1, source_target_pairs={{0,66},{2,64},{64,2},{66,0},{1,67},{3,65},{65,3},{67,1},{4,70},{6,... | collective-permute-start | bytes 196616 | tf_op jit(solution)/shard_map/ppermute | solution.py:351
  4.8 5.5 %collective-permute-start.1 = (bf16[1,16,2048]{2,1,0:T(8,128)(2,1)}, bf16[1,16,2048]{2,1,0:T(8,128)(2,1)S(1)}, u32[]{:S(2)}, u32[]{:S(2)}) collective-permute-start(bf16[1,16,2048]{2,1,0:T(8,128)(2,1)} %m0_ref.1), channel_id=1, source_target_pairs={{0,64},{2,66},{64,0},{66,2},{1,65},{3,67},{65,1},{67,3},{4,68},{6,... | collective-permute-start | bytes 196616 | tf_op jit(solution)/shard_map/ppermute | solution.py:351
  5.0 5.4 %collective-permute-start = (bf16[1,16,2048]{2,1,0:T(8,128)(2,1)}, bf16[1,16,2048]{2,1,0:T(8,128)(2,1)S(1)}, u32[]{:S(2)}, u32[]{:S(2)}) collective-permute-start(bf16[1,16,2048]{2,1,0:T(8,128)(2,1)} %m0_ref.1), channel_id=1, source_target_pairs={{0,2},{2,0},{64,66},{66,64},{1,3},{3,1},{65,67},{67,65},{4,6},{6,4... | collective-permute-start | bytes 196616 | tf_op jit(solution)/shard_map/ppermute | solution.py:351
  7.7 2.7 %copy-start.4 = (bf16[1,16,2048]{2,1,0:T(8,128)(2,1)}, bf16[1,16,2048]{2,1,0:T(8,128)(2,1)S(1)}, u32[]{:S(2)}) copy-start(bf16[1,16,2048]{2,1,0:T(8,128)(2,1)S(1)} %collective-permute-done.2.m3_ref) | copy-start | bytes 196612
  10.4 0.6 copy-start.6
  10.4 0.6 copy-start.8
  17.3 8.0 %copy-start.3 = (bf16[1,16,2048]{2,1,0:T(8,128)(2,1)S(1)}, bf16[1,16,2048]{2,1,0:T(8,128)(2,1)}, u32[]{:S(2)}) copy-start(bf16[1,16,2048]{2,1,0:T(8,128)(2,1)} %m0_ref.1) | copy-start | bytes 196612
  17.3 8.0 %copy-start.5 = (bf16[1,16,2048]{2,1,0:T(8,128)(2,1)S(1)}, bf16[1,16,2048]{2,1,0:T(8,128)(2,1)}, u32[]{:S(2)}) copy-start(bf16[1,16,2048]{2,1,0:T(8,128)(2,1)} %copy-done.4) | copy-start | bytes 196612
  17.3 8.0 %copy-start.7 = (bf16[1,16,2048]{2,1,0:T(8,128)(2,1)S(1)}, bf16[1,16,2048]{2,1,0:T(8,128)(2,1)}, u32[]{:S(2)}) copy-start(bf16[1,16,2048]{2,1,0:T(8,128)(2,1)} %copy-done.6) | copy-start | bytes 196612
  17.3 8.0 %copy-start.9 = (bf16[1,16,2048]{2,1,0:T(8,128)(2,1)S(1)}, bf16[1,16,2048]{2,1,0:T(8,128)(2,1)}, u32[]{:S(2)}) copy-start(bf16[1,16,2048]{2,1,0:T(8,128)(2,1)} %copy-done.8) | copy-start | bytes 196612
  17.3 27.6 %all-to-all-start = ((bf16[16,336,128]{2,1,0:T(8,128)(2,1)}), bf16[16,336,128]{2,1,0:T(8,128)(2,1)S(1)}, u32[]{:S(2)}, u32[]{:S(2)}) async-start(bf16[16,336,128]{2,1,0:T(8,128)(2,1)} %get-tuple-element.27), calls=%async_computation | async-start | bytes 2752512 | tf_op jit(solution)/shard_map/all_to_all | solution.py:347
  44.9 5.5 %copy-start = (bf16[16,336,128]{2,1,0:T(8,128)(2,1)}, bf16[16,336,128]{2,1,0:T(8,128)(2,1)S(1)}, u32[]{:S(2)}) copy-start(bf16[16,336,128]{2,1,0:T(8,128)(2,1)S(1)} %all-to-all-done.refs_0_.refs_1_) | copy-start | bytes 4128772
  44.9 24.6 %all-to-all-start.1 = ((bf16[16,272,128]{2,1,0:T(8,128)(2,1)}), bf16[16,272,128]{2,1,0:T(8,128)(2,1)S(1)}, u32[]{:S(2)}, u32[]{:S(2)}) async-start(bf16[16,272,128]{2,1,0:T(8,128)(2,1)} %get-tuple-element.34), calls=%async_computation.1 | async-start | bytes 2228224 | tf_op jit(solution)/shard_map/all_to_all | solution.py:347
  69.5 6.7 %copy-start.1 = (bf16[16,272,128]{2,1,0:T(8,128)(2,1)}, bf16[16,272,128]{2,1,0:T(8,128)(2,1)S(1)}, u32[]{:S(2)}) copy-start(bf16[16,272,128]{2,1,0:T(8,128)(2,1)S(1)} %all-to-all-done.1.refs_1_) | copy-start | bytes 3342340
  69.5 25.9 %all-to-all-start.2 = ((bf16[16,64,512]{2,1,0:T(8,128)(2,1)}), bf16[16,64,512]{2,1,0:T(8,128)(2,1)S(1)}, u32[]{:S(2)}, u32[]{:S(2)}) async-start(bf16[16,64,512]{2,1,0:T(8,128)(2,1)} %spread.1), calls=%async_computation.2 | async-start | bytes 2097152 | tf_op jit(solution)/shard_map/all_to_all | solution.py:347
  95.4 6.8 %copy-start.10 = (bf16[1024,128]{1,0:T(8,128)(2,1)S(1)}, bf16[1024,128]{1,0:T(8,128)(2,1)}, u32[]{:S(2)}) copy-start(bf16[1024,128]{1,0:T(8,128)(2,1)} %get-tuple-element.40) | copy-start | bytes 786436
  95.4 21.8 %all-to-all-start.3 = ((bf16[16,256,128]{2,1,0:T(8,128)(2,1)}), bf16[16,256,128]{2,1,0:T(8,128)(2,1)S(1)}, u32[]{:S(2)}, u32[]{:S(2)}) async-start(bf16[16,256,128]{2,1,0:T(8,128)(2,1)} %get-tuple-element.42), calls=%async_computation.3 | async-start | bytes 2097152 | tf_op jit(solution)/shard_map/all_to_all | solution.py:347
  102.2 3.6 %collective-permute-start.3 = (bf16[1024,128]{1,0:T(8,128)(2,1)S(1)}, bf16[1024,128]{1,0:T(8,128)(2,1)S(1)}, u32[]{:S(2)}, u32[]{:S(2)}) collective-permute-start(bf16[1024,128]{1,0:T(8,128)(2,1)S(1)} %copy-done.10), channel_id=1, source_target_pairs={{0,2},{2,0},{64,66},{66,64},{1,3},{3,1},{65,67},{67,65},{4,6},{6,4... | collective-permute-start | bytes 786440 | tf_op jit(solution)/shard_map/ppermute | solution.py:351
  105.8 9.1 %collective-permute-start.4 = (bf16[1024,128]{1,0:T(8,128)(2,1)S(1)}, bf16[1024,128]{1,0:T(8,128)(2,1)S(1)}, u32[]{:S(2)}, u32[]{:S(2)}) collective-permute-start(bf16[1024,128]{1,0:T(8,128)(2,1)S(1)} %add_convert_fusion.p0_ref), channel_id=1, source_target_pairs={{0,64},{2,66},{64,0},{66,2},{1,65},{3,67},{65,1},{67,3},{4,68},{6,... | collective-permute-start | bytes 786440 | tf_op jit(solution)/shard_map/ppermute | solution.py:351
  117.2 15.2 %all-to-all-start.4 = ((bf16[32,32,128]{2,1,0:T(8,128)(2,1)}), bf16[32,32,128]{2,1,0:T(8,128)(2,1)S(1)}, u32[]{:S(2)}, u32[]{:S(2)}) async-start(bf16[32,32,128]{2,1,0:T(8,128)(2,1)} %weight_blocks.1), calls=%async_computation.4 | async-start | bytes 524288 | tf_op jit(solution)/shard_map/all_to_all | solution.py:347
  132.4 0.7 copy-start.2
